TPU v7x, 768 devices: a whole 4x8x12 slice. The times are simulated.
768 devices in a mesh: section: 4 (over z_hi), row: 64 (over x, y, core), col: 3 (over z_lo).
Axes of the slice: x: 4, y: 8, z: 12 (z_hi: 4, z_lo: 3; z = z_hi * 3 + z_lo), core: 2. Of those that a mesh axis runs over, the one named last changes fastest.
Arguments:
- act_in: bfloat16 [4, 128, 12288], P('section', 'row', 'col'), may hold values from -6 to 6
- hid_in: bfloat16 [4, 128, 24576], P('section', None, 'row'), may hold values from -6 to 6
- grad_in: bfloat16 [4, 128, 12288], P('section', 'row', 'col'), may hold values from -6 to 6
- saved_in: bfloat16 [4, 128, 12288], P('section', 'row', 'col'), may hold values from -6 to 6
- saved_pre: bfloat16 [4, 128, 24576], P('section', None, 'row'), may hold values from -6 to 6
- weights: bfloat16 [4, 12288, 24576], P('section', 'col', 'row'), may hold values from -0.0546875 to 0.0546875
- norm_gain: float32 [2, 12288], P(None, 'col'), may hold values from 0.25 to 1.75
- norm_bias: float32 [2, 12288], P(None, 'col'), may hold values from -0.5 to 0.5
Outputs:
- act_out: bfloat16 [4, 128, 12288], P('section', 'row', 'col')
- hid_out: bfloat16 [4, 128, 24576], P('section', None, 'row')
- grad_out: bfloat16 [4, 128, 12288], P('section', 'row', 'col')
All inputs are finite; a program needn't handle non-finite values.
Results may differ from a plain program's by a relative error of at most 0.0035.
Values may be sent and summed in bfloat16 or wider, within the bound.
No kernel may reach another device: no remote copies, remote signals or barrier semaphores. Data moves between devices by JAX's collectives and lax.ppermute only.
A program may use at most 32 MiB of HBM per device.

v0:
```python
import jax
import jax.numpy as jnp
from jax import lax
from jax.sharding import PartitionSpec as P

D = 12288


epsilon = 1e-05


def passed_along(block, axis, distance):
    devices = range(lax.axis_size(axis))
    route = [((i - distance) % len(devices), i) for i in devices]
    return lax.ppermute(block, axis, route)


def partner(shard, axis, stride):
    return lax.ppermute(shard, axis, [(i, i ^ 1 << stride) for i in range(lax.axis_size(axis))])


def col_total(values):
    return lax.psum(values, "col")


def boundary(values, offset):
    return passed_along(values, "section", offset)


def statistics(total, squares):
    average = total / D
    inverse_scale = lax.rsqrt(squares / D - average * average + epsilon)
    return (average[:, None], inverse_scale[:, None])


def gelu_slope(preact, upstream):
    return jax.vjp(lambda value: jax.nn.gelu(value, approximate=True), preact)[1](upstream)[0]


def per_device(act_in, hid_in, grad_in, saved_in, saved_pre, weights, norm_gain, norm_bias):
    section_index = lax.axis_index("section")
    is_even = section_index % 2 == 0
    layer = section_index // 2
    gain = lax.dynamic_index_in_dim(norm_gain, layer, 0, keepdims=False)
    offset_bias = lax.dynamic_index_in_dim(norm_bias, layer, 0, keepdims=False)
    weight = weights[0]
    stream = act_in[0]
    gradient = grad_in[0]
    stream_float = stream.astype(jnp.float32)
    saved_float = saved_in[0].astype(jnp.float32)
    sums = col_total(
        (
            jnp.sum(stream_float, axis=-1),
            jnp.sum(stream_float * stream_float, axis=-1),
            jnp.sum(saved_float, axis=-1),
            jnp.sum(saved_float * saved_float, axis=-1),
        )
    )
    stream_mean, stream_scale = statistics(sums[0], sums[1])
    saved_mean, saved_scale = statistics(sums[2], sums[3])
    normed = ((stream_float - stream_mean) * stream_scale * gain + offset_bias).astype(jnp.bfloat16)
    leading = jnp.where(is_even, normed, gradient)
    partial_sums = jnp.dot(
        lax.all_gather(leading, "row", axis=0, tiled=True),
        weight,
        preferred_element_type=jnp.float32,
    )
    summed = col_total(partial_sums)
    hidden_value = jnp.where(is_even, jax.nn.gelu(summed, approximate=True), summed).astype(
        jnp.bfloat16
    )
    hidden_next = partner(hidden_value, "section", 0)
    slope = gelu_slope(saved_pre[0].astype(jnp.float32), hid_in[0].astype(jnp.float32)).astype(
        jnp.bfloat16
    )
    right_side = jnp.where(is_even, slope, hid_in[0])
    term = lax.psum_scatter(
        lax.dot_general(
            right_side, weight, (((1,), (1,)), ((), ())), preferred_element_type=jnp.float32
        ),
        "row",
        scatter_dimension=0,
        tiled=True,
    )
    forward_odd = (stream_float + term).astype(jnp.bfloat16)
    saved_hat = (saved_float - saved_mean) * saved_scale
    scaled = term * gain
    moments = col_total((jnp.sum(scaled, axis=-1), jnp.sum(scaled * saved_hat, axis=-1)))
    first_mean = (moments[0] / D)[:, None]
    second_mean = (moments[1] / D)[:, None]
    backward_even = (
        gradient.astype(jnp.float32) + saved_scale * (scaled - first_mean - saved_hat * second_mean)
    ).astype(jnp.bfloat16)
    forward_value = jnp.where(is_even, stream, forward_odd)
    backward_value = jnp.where(is_even, backward_even, gradient)
    act_next = boundary(forward_value, 1)
    grad_next = boundary(backward_value, -1)
    return (act_next[None], hidden_next[None], grad_next[None])


def solution(mesh):
    in_specs = (
        P("section", "row", "col"),
        P("section", None, "row"),
        P("section", "row", "col"),
        P("section", "row", "col"),
        P("section", None, "row"),
        P("section", "col", "row"),
        P(None, "col"),
        P(None, "col"),
    )
    out_specs = (P("section", "row", "col"), P("section", None, "row"), P("section", "row", "col"))
    return jax.shard_map(
        per_device, mesh=mesh, in_specs=in_specs, out_specs=out_specs, check_vma=False
    )
```

profile of v0, /device:TPU:64, one launch (start us, length us, event | category | flops | bytes accessed | tf_op | source)
XLA Modules:
  0.0 410.8 jit_solution(13608215522814052373)
XLA Ops:
  7.2 0.0 copy-start
  7.2 0.0 all-reduce.8.cloned.1.call-start
  7.2 1.0 convert_reduce_fusion.1
  8.3 0.9 fusion.32
  9.1 0.0 copy-done
  9.1 0.0 copy-start.2
  9.1 0.0 copy-start.4
  9.2 0.0 copy-start.5
  9.2 0.0 copy-start.1
  9.2 0.0 copy-start.3
  9.2 3.5 fusion.2
  12.7 0.0 all-reduce.8.cloned.1.call-update
  12.7 0.0 all-gather.3.cloned.1.call-start
  12.8 13.1 %all-reduce.2 = (f32[2]{0:T(128)S(1)}, f32[2]{0:T(128)S(1)}) all-reduce(f32[2]{0:T(128)S(1)} %fusion.32, f32[2]{0:T(128)S(1)} %convert_reduce_fusion.1), channel_id=1, replica_groups=mesh['section'=4,'row'=64,'col'=3] {'col'}, use_global_device_ids=true, to_apply=%region_7.8 | all-reduce | flops 4 | bytes 32 | tf_op jit(solution)/shard_map/psum | solution.py:23
  25.9 1.3 dynamic-slice
  27.8 0.0 copy-done.2
  27.8 0.2 convert_reduce_fusion
  28.0 0.0 copy-done.4
  28.0 0.0 copy-done.5
  28.1 202.5 %all-reduce.8.cloned.1.call-done = f32[128,4096]{1,0:T(8,128)} async-done(((f32[128,4096]{1,0:T(8,128)}), f32[128,4096]{1,0:T(8,128)}) %all-reduce.8.cloned.1.call-update) | async-done | bytes 2097168
  230.6 0.0 copy-done.1
  230.6 1.1 fusion.47
  231.7 6.0 %all-reduce.1 = (f32[2]{0:T(128)S(1)}, f32[2]{0:T(128)S(1)}, f32[2]{0:T(128)S(1)}, f32[2]{0:T(128)S(1)}) all-reduce(f32[2]{0:T(128)S(1)} %get-tuple-element.6, f32[2]{0:T(128)S(1)} %get-tuple-element.5, f32[2]{0:T(128)S(1)} %get-tuple-element.4, f32[2]{0:T(128)S(1)} %get-tuple-element.3), channel_id=1, replica_groups=mesh['section'=4,'row'=64,'col'=3] {'col'}, use_global_device_ids=true, to_apply=%region_4.5 | all-reduce | flops 8 | bytes 64 | tf_op jit(solution)/shard_map/psum | solution.py:23
  237.8 0.0 copy-done.3
  237.8 1.7 broadcast_select_fusion
  239.4 0.0 all-gather.3.cloned.1.call-update
  239.4 0.0 all-reduce.6.cloned.1.call-start
  239.5 87.4 %all-gather.3.cloned.1.call-done = bf16[64,2,4096]{2,1,0:T(2,128)(2,1)} async-done(((bf16[1,2,4096]{2,1,0:T(2,128)(2,1)}), bf16[64,2,4096]{2,1,0:T(2,128)(2,1)}) %all-gather.3.cloned.1.call-update) | async-done | bytes 1048592 | tf_op jit(solution)/shard_map/all_gather | solution.py:64
  326.9 2.3 reshape.15
  329.1 2.6 fusion
  331.8 0.0 all-reduce.6.cloned.1.call-update
  331.8 51.7 %all-reduce.6.cloned.1.call-done = f32[128,384]{1,0:T(8,128)} async-done(((f32[128,384]{1,0:T(8,128)}), f32[128,384]{1,0:T(8,128)}) %all-reduce.6.cloned.1.call-update) | async-done | bytes 196624 | tf_op jit(solution)/shard_map/psum | solution.py:23
  383.5 1.0 fusion.15
  384.5 7.4 %collective-permute-start.1 = (bf16[128,384]{1,0:T(8,128)(2,1)S(1)}, bf16[128,384]{1,0:T(8,128)(2,1)S(1)}, u32[]{:S(2)}, u32[]{:S(2)}) collective-permute-start(bf16[128,384]{1,0:T(8,128)(2,1)S(1)} %fusion.15), channel_id=1, source_target_pairs={{0,192},{192,0},{384,576},{576,384},{1,193},{193,1},{385,577},{577... | collective-permute-start | bytes 294920 | tf_op jit(solution)/shard_map/ppermute | solution.py:19
  391.9 1.9 collective-permute-start
  393.8 6.9 %collective-permute-start.2 = (bf16[2,4096]{1,0:T(2,128)(2,1)S(1)}, bf16[2,4096]{1,0:T(2,128)(2,1)S(1)}, u32[]{:S(2)}, u32[]{:S(2)}) collective-permute-start(bf16[2,4096]{1,0:T(2,128)(2,1)S(1)} %get-tuple-element.13), channel_id=1, source_target_pairs={{192,0},{384,192},{576,384},{0,576},{193,1},{385,193},{577,385},{1... | collective-permute-start | bytes 49160 | tf_op jit(solution)/shard_map/ppermute | solution.py:15
  400.8 0.0 collective-permute-done
  400.8 1.7 collective-permute-done.2
  402.5 0.0 collective-permute-done.1
  402.5 0.6 copy.16
  403.1 0.6 copy.17
  403.7 0.6 copy.18
  (5 shorter events, 0.1 us)
Async XLA Ops:
  7.2 2.0 copy-start
  7.2 223.4 %all-reduce.8.cloned.1.call-start = ((), (), s32[]{:S(2)}) async-start(), calls=%async_computation.2 | async-start | bytes 4194304
  9.1 18.7 %copy-start.2 = (bf16[1,2,4096]{2,1,0:T(2,128)(2,1)S(1)}, bf16[1,2,4096]{2,1,0:T(2,128)(2,1)}, u32[]{:S(2)}) copy-start(bf16[1,2,4096]{2,1,0:T(2,128)(2,1)} %param.8) | copy-start | bytes 49156
  9.1 18.8 %copy-start.4 = (f32[2,4096]{1,0:T(2,128)S(1)}, f32[2,4096]{1,0:T(2,128)}, u32[]{:S(2)}) copy-start(f32[2,4096]{1,0:T(2,128)} %param.14) | copy-start | bytes 98308
  9.2 18.9 %copy-start.5 = (f32[2,4096]{1,0:T(2,128)S(1)}, f32[2,4096]{1,0:T(2,128)}, u32[]{:S(2)}) copy-start(f32[2,4096]{1,0:T(2,128)} %param.15) | copy-start | bytes 98308
  9.2 221.4 %copy-start.1 = (bf16[1,2,4096]{2,1,0:T(2,128)(2,1)S(1)}, bf16[1,2,4096]{2,1,0:T(2,128)(2,1)}, u32[]{:S(2)}) copy-start(bf16[1,2,4096]{2,1,0:T(2,128)(2,1)} %param.11) | copy-start | bytes 49156
  9.2 228.6 %copy-start.3 = (bf16[1,2,4096]{2,1,0:T(2,128)(2,1)S(1)}, bf16[1,2,4096]{2,1,0:T(2,128)(2,1)}, u32[]{:S(2)}) copy-start(bf16[1,2,4096]{2,1,0:T(2,128)(2,1)} %param.10) | copy-start | bytes 49156
  12.7 314.2 %all-gather.3.cloned.1.call-start = ((), (), s32[]{:S(2)}) async-start(), calls=%async_computation.1 | async-start | bytes 1064960 | tf_op jit(solution)/shard_map/all_gather | solution.py:64
  239.4 144.0 %all-reduce.6.cloned.1.call-start = ((), (), s32[]{:S(2)}) async-start(), calls=%async_computation | async-start | bytes 393216 | tf_op jit(solution)/shard_map/psum | solution.py:23
  384.5 18.0 %collective-permute-start.1 = (bf16[128,384]{1,0:T(8,128)(2,1)S(1)}, bf16[128,384]{1,0:T(8,128)(2,1)S(1)}, u32[]{:S(2)}, u32[]{:S(2)}) collective-permute-start(bf16[128,384]{1,0:T(8,128)(2,1)S(1)} %fusion.15), channel_id=1, source_target_pairs={{0,192},{192,0},{384,576},{576,384},{1,193},{193,1},{385,577},{577... | collective-permute-start | bytes 294920 | tf_op jit(solution)/shard_map/ppermute | solution.py:19
  391.9 8.9 %collective-permute-start = (bf16[2,4096]{1,0:T(2,128)(2,1)S(1)}, bf16[2,4096]{1,0:T(2,128)(2,1)S(1)}, u32[]{:S(2)}, u32[]{:S(2)}) collective-permute-start(bf16[2,4096]{1,0:T(2,128)(2,1)S(1)} %get-tuple-element.14), channel_id=1, source_target_pairs={{576,0},{0,192},{192,384},{384,576},{577,1},{1,193},{193,385},{385... | collective-permute-start | bytes 49160 | tf_op jit(solution)/shard_map/ppermute | solution.py:15
  393.8 8.6 %collective-permute-start.2 = (bf16[2,4096]{1,0:T(2,128)(2,1)S(1)}, bf16[2,4096]{1,0:T(2,128)(2,1)S(1)}, u32[]{:S(2)}, u32[]{:S(2)}) collective-permute-start(bf16[2,4096]{1,0:T(2,128)(2,1)S(1)} %get-tuple-element.13), channel_id=1, source_target_pairs={{192,0},{384,192},{576,384},{0,576},{193,1},{385,193},{577,385},{1... | collective-permute-start | bytes 49160 | tf_op jit(solution)/shard_map/ppermute | solution.py:15
Sparse Core Ops, SparseCore 0:
  12.8 217.6 all-reduce.7
  239.6 87.2 all-gather.2
  331.9 51.4 all-reduce.5
where the time goes:
time: 411 us
  waiting for transfers between devices  343 us (83%)
  blocking collectives  19.1 us (5%)
  starting transfers between devices  16.4 us (4%)
  between operations  14.6 us (4%)
  matrix products  6.12 us (1%)
  other arithmetic  5.89 us (1%)
  local copies, waits for them, and re-layouts  5.47 us (1%)
    unnamed x4, waiting for transfers between devices  203 us
    all_gather x1, waiting for transfers between devices, per_device(): lax.all_gather(leading, 'row', axis=0, tiled=True)  87.4 us
    psum x1, waiting for transfers between devices, col_total(): return lax.psum(values, 'col')  51.7 us
    psum x2, blocking collectives, col_total(): return lax.psum(values, 'col')  19.1 us
    ppermute x2, starting transfers between devices, passed_along(): return lax.ppermute(block, axis, route)  8.85 us
  transfers between devices with their start and end apart: 6, of which 4 were waited for; matrix products, arithmetic and copies ran while one was open for 0% of the time, Pallas kernels for 0%

commit v1 on v0

v1 whole, which is shorter than its diff:
```python
import jax
import jax.numpy as jnp
from jax import lax
from jax.sharding import Mesh, PartitionSpec as P

D = 12288
epsilon = 1e-05

LAYER_AXIS, HALF, COLS = "layer", "half", "cols"
PLANE = ("px", "py")
CORE = "core"
ROWS = PLANE + (CORE,)
SECTION = (LAYER_AXIS, HALF)


def boundary(values, offset):
    return lax.ppermute(values, SECTION, [(i, (i + offset) % 4) for i in range(4)])


def statistics(total, squares):
    average = total / D
    inverse_scale = lax.rsqrt(squares / D - average * average + epsilon)
    return (average[:, None], inverse_scale[:, None])


def gelu_slope(preact, upstream):
    return jax.vjp(lambda value: jax.nn.gelu(value, approximate=True), preact)[1](upstream)[0]


def per_device(act_in, hid_in, grad_in, saved_in, saved_pre, weights, norm_gain, norm_bias):
    f32, bf16 = jnp.float32, jnp.bfloat16
    half = lax.axis_index(HALF)
    core = lax.axis_index(CORE)
    layer = lax.axis_index(LAYER_AXIS)
    is_even = half == 0
    gain = lax.dynamic_index_in_dim(norm_gain, layer, 0, keepdims=False)
    offset_bias = lax.dynamic_index_in_dim(norm_bias, layer, 0, keepdims=False)
    weight = weights[0]
    stream, gradient = act_in[0], grad_in[0]
    features = weight.shape[0]
    hidden = weight.shape[1]
    tokens = hid_in.shape[1]
    cols = lax.axis_size(COLS)
    planes = lax.axis_size(PLANE)
    own = stream.shape[0]
    half_tokens = tokens // 2

    stream_float = stream.astype(f32)
    saved_float = saved_in[0].astype(f32)
    sums = lax.psum(
        jnp.stack(
            (
                jnp.sum(stream_float, axis=-1),
                jnp.sum(stream_float * stream_float, axis=-1),
                jnp.sum(saved_float, axis=-1),
                jnp.sum(saved_float * saved_float, axis=-1),
            )
        ),
        COLS,
    )
    stream_mean, stream_scale = statistics(sums[0], sums[1])
    saved_mean, saved_scale = statistics(sums[2], sums[3])
    normed = ((stream_float - stream_mean) * stream_scale * gain + offset_bias).astype(bf16)
    leading = jnp.where(is_even, normed, gradient)

    slope = gelu_slope(saved_pre[0].astype(f32), hid_in[0].astype(f32)).astype(bf16)
    right_side = jnp.where(is_even, slope, hid_in[0])
    right_side = right_side.reshape(planes, 2, own, hidden).transpose(1, 0, 2, 3)
    right_side = right_side.reshape(2, half_tokens, hidden)

    def product(which):
        rows = lax.dynamic_index_in_dim(right_side, which, 0, keepdims=False)
        return lax.dot_general(rows, weight, (((1,), (1,)), ((), ())), preferred_element_type=f32)

    swap = [(0, 1), (1, 0)]
    arriving = lax.ppermute(product(1 - core).astype(bf16), CORE, swap)
    chip_sum = (product(core) + arriving.astype(f32)).astype(bf16)

    outgoing = jnp.concatenate(
        (
            chip_sum.reshape(planes, own, features),
            jnp.broadcast_to(leading[None], (planes, own, features)),
        ),
        axis=1,
    )
    incoming = lax.all_to_all(outgoing, PLANE, 0, 0, tiled=True)
    term = jnp.sum(incoming[:, :own].astype(f32), axis=0)
    near = incoming[:, own:].reshape(half_tokens, features)
    far = lax.ppermute(near, CORE, swap)

    forward_odd = (stream_float + term).astype(bf16)
    act_next = boundary(jnp.where(is_even, stream, forward_odd), 1)
    saved_hat = (saved_float - saved_mean) * saved_scale
    scaled = term * gain
    moments = jnp.stack((jnp.sum(scaled, axis=-1), jnp.sum(scaled * saved_hat, axis=-1)))

    near_product = jnp.dot(near, weight, preferred_element_type=f32)
    far_product = jnp.dot(far, weight, preferred_element_type=f32)
    first = core == 0
    partial = jnp.stack(
        (jnp.where(first, near_product, far_product), jnp.where(first, far_product, near_product))
    )
    part = hidden // cols
    partial = partial.reshape(tokens, cols, part).transpose(1, 0, 2)
    extra = jnp.pad(moments.reshape(1, -1), ((0, 7), (0, part - moments.size)))
    partial = jnp.concatenate((partial, jnp.broadcast_to(extra[None], (cols, 8, part))), axis=1)
    summed = jnp.sum(lax.all_to_all(partial, COLS, 0, 0, tiled=True), axis=0)
    moments = summed[tokens, : moments.size].reshape(moments.shape)
    summed = summed[:tokens]
    hidden_value = jnp.where(is_even, jax.nn.gelu(summed, approximate=True), summed).astype(bf16)

    outgoing = jnp.broadcast_to(hidden_value[None], (2 * cols, tokens, part))
    incoming = lax.all_to_all(outgoing, (HALF, COLS), 0, 0, tiled=True)
    incoming = lax.dynamic_index_in_dim(
        incoming.reshape(2, cols, 2, planes, own, part), 1 - half, 0, keepdims=False
    )
    hidden_next = incoming.transpose(2, 1, 3, 0, 4).reshape(tokens, hidden)

    first_mean = (moments[0] / D)[:, None]
    second_mean = (moments[1] / D)[:, None]
    backward_even = (
        gradient.astype(f32) + saved_scale * (scaled - first_mean - saved_hat * second_mean)
    ).astype(bf16)
    grad_next = boundary(jnp.where(is_even, backward_even, gradient), -1)
    return (act_next[None], hidden_next[None], grad_next[None])


def solution(mesh):
    names = SECTION + ROWS + (COLS,)
    parts = Mesh(mesh.devices.reshape(2, 2, 4, 8, 2, 3), names)
    in_specs = (
        P(SECTION, ROWS, COLS),
        P(SECTION, None, ROWS),
        P(SECTION, ROWS, COLS),
        P(SECTION, ROWS, COLS),
        P(SECTION, None, ROWS),
        P(SECTION, COLS, ROWS),
        P(None, COLS),
        P(None, COLS),
    )
    out_specs = (P(SECTION, ROWS, COLS), P(SECTION, None, ROWS), P(SECTION, ROWS, COLS))
    return jax.shard_map(
        per_device, mesh=parts, in_specs=in_specs, out_specs=out_specs, check_vma=False
    )
```

time: 411 us -> 121 us (0.29)
  the two profiles are of different devices: /device:TPU:64 before, /device:TPU:8 now
where the time goes in v1:
time: 121 us; the launch traced here: 120 us
  starting transfers between devices  36.7 us (30%)
  waiting for transfers between devices  35.4 us (29%)
  blocking collectives  17.2 us (14%)
  local copies, waits for them, and re-layouts  13.7 us (11%)
  matrix products  8.11 us (7%)
  other arithmetic  7.54 us (6%)
    all_to_all x1, waiting for transfers between devices, per_device(): incoming = lax.all_to_all(outgoing, PLANE, 0, 0, tiled=True)  28.5 us
    all_to_all x1, starting transfers between devices, per_device(): incoming = lax.all_to_all(outgoing, PLANE, 0, 0, tiled=True)  11.9 us
    ppermute x2, starting transfers between devices, boundary(): lax.ppermute(values, SECTION, [(i, (i + offset) % 4) for i in range(4)])  11.3 us
    all_to_all x1, starting transfers between devices, per_device(): incoming = lax.all_to_all(outgoing, (HALF, COLS), 0, 0, tiled=True)  9.72 us
    all_to_all x1, blocking collectives, per_device(): summed = jnp.sum(lax.all_to_all(partial, COLS, 0, 0, tiled=True), axis=0)  9.5 us
    psum x1, blocking collectives, per_device(): lax.psum(jnp.stack((jnp.sum(stream_float, axis=-1), jnp.sum(stream_float...  7.66 us
    ppermute x2, waiting for transfers between devices, boundary(): lax.ppermute(values, SECTION, [(i, (i + offset) % 4) for i in range(4)])  6.91 us
    dot_general x2, matrix products, product(): lax.dot_general(rows, weight, (((1,), (1,)), ((), ())), preferred_element...  4.88 us
  transfers between devices with their start and end apart: 6, of which 2 were waited for; matrix products, arithmetic and copies ran while one was open for 4% of the time, Pallas kernels for 0%

profile of v1, /device:TPU:8, one launch (start us, length us, event | category | flops | bytes accessed | tf_op | source)
XLA Modules:
  0.0 119.6 jit_solution(4940817674508521956)
XLA Ops:
  0.6 0.0 copy-start
  0.7 0.0 copy-start.2
  0.7 0.0 copy-start.3
  0.7 1.1 squeeze.36
  1.8 1.0 reshape.124
  2.8 0.2 fusion.18
  2.9 0.1 copy.48
  3.0 0.2 constant_dynamic-slice_fusion.4
  3.3 0.0 copy-start.4
  3.3 0.0 copy-start.5
  3.3 1.9 %convolution_convert_fusion = bf16[64,4096]{1,0:T(8,128)(2,1)} fusion(bf16[1,4096,384]{2,1,0:T(8,128)(2,1)S(1)} %copy-done, bf16[1,64,384]{2,0,1:T(2,128)(2,1)S(1)} %get-tuple-element.10), kind=kOutput, calls=%fused_computation | convolution fusion | flops 201588736 | bytes 3719168 | tf_op jit(solution)/shard_map/dot_general | solution.py:73
  5.2 1.9 %collective-permute-start = (bf16[64,4096]{1,0:T(8,128)(2,1)}, bf16[64,4096]{1,0:T(8,128)(2,1)}, u32[]{:S(2)}, u32[]{:S(2)}) collective-permute-start(bf16[64,4096]{1,0:T(8,128)(2,1)} %convolution_convert_fusion), channel_id=1, source_target_pairs={{0,3},{3,0},{1,4},{4,1},{2,5},{5,2},{6,9},{9,6},{7,10},{10,7},{8,1... | collective-permute-start | bytes 1572872 | tf_op jit(solution)/shard_map/ppermute | solution.py:76
  7.1 0.1 fusion.36
  7.3 0.1 convert_reduce_fusion.2
  7.4 0.2 convert_reduce_fusion.1
  7.6 7.7 %psum.7 = f32[4,2]{1,0:T(4,128)S(1)} all-reduce(f32[4,2]{1,0:T(4,128)S(1)} %pad_maximum_fusion.3), channel_id=1, replica_groups=mesh['layer'=2,'half'=2,'px'=4,'py'=8,'core'=2,'cols'=3] {'cols'}, use_global_device_ids=true, to_apply=%region_4.5 | all-reduce | flops 8 | bytes 64 | tf_op jit(solution)/shard_map/psum | solution.py:50
  15.4 0.1 fusion.40
  15.5 0.0 collective-permute-done
  15.5 3.0 %add_convert_fusion = bf16[64,4096]{1,0:T(8,128)(2,1)} fusion(bf16[64,4096]{1,0:T(8,128)(2,1)} %collective-permute-done, bf16[1,4096,384]{2,1,0:T(8,128)(2,1)S(1)} %copy-done, bf16[1,64,384]{2,0,1:T(2,128)(2,1)S(1)} %get-tuple-element.9), kind=kOutput, calls=%fused_computation.10 | convolution fusion | flops 202113024 | bytes 4243456 | tf_op jit(solution)/shard_map/dot_general | solution.py:73
  18.5 2.2 %reshape.119 = bf16[32,2,4096]{2,1,0:T(2,128)(2,1)} reshape(bf16[64,4096]{1,0:T(8,128)(2,1)} %add_convert_fusion) | data formatting | bytes 1048576 | tf_op jit(solution)/shard_map/reshape | solution.py:81
  20.6 0.5 broadcast_in_dim.13
  21.1 3.2 %pad_maximum_fusion = bf16[32,4,4096]{2,1,0:T(4,128)(2,1)} fusion(bf16[32,2,4096]{2,1,0:T(2,128)(2,1)S(1)} %broadcast_in_dim.13, bf16[32,2,4096]{2,1,0:T(2,128)(2,1)} %reshape.119), kind=kLoop, calls=%fused_computation.8 | loop fusion | flops 2097152 | bytes 2097152 | tf_op jit(solution)/shard_map/concatenate | solution.py:79
  24.3 11.9 %all-to-all-start = ((bf16[32,4,4096]{2,1,0:T(4,128)(2,1)}), bf16[32,4,4096]{2,1,0:T(4,128)(2,1)}, u32[]{:S(2)}, u32[]{:S(2)}) async-start(bf16[32,4,4096]{2,1,0:T(4,128)(2,1)} %pad_maximum_fusion), calls=%async_computation | async-start | bytes 2097152 | tf_op jit(solution)/shard_map/all_to_all | solution.py:86
  36.2 28.5 %all-to-all-done = bf16[32,4,4096]{2,1,0:T(4,128)(2,1)} async-done(((bf16[32,4,4096]{2,1,0:T(4,128)(2,1)}), bf16[32,4,4096]{2,1,0:T(4,128)(2,1)}, u32[]{:S(2)}, u32[]{:S(2)}) %all-to-all-start) | async-done | bytes 1048608 | tf_op jit(solution)/shard_map/all_to_all | solution.py:86
  64.6 2.7 %slice.42 = bf16[32,2,4096]{2,1,0:T(2,128)(2,1)} slice(bf16[32,4,4096]{2,1,0:T(4,128)(2,1)} %all-to-all-done), slice={[0:32], [2:4], [0:4096]} | slice | bytes 1048576 | tf_op jit(solution)/shard_map/slice | solution.py:88
  67.3 2.1 %reshape.120 = bf16[64,4096]{1,0:T(8,128)(2,1)} reshape(bf16[32,2,4096]{2,1,0:T(2,128)(2,1)} %slice.42) | data formatting | bytes 1048576 | tf_op jit(solution)/shard_map/reshape | solution.py:88
  69.4 1.9 %collective-permute-start.2 = (bf16[64,4096]{1,0:T(8,128)(2,1)}, bf16[64,4096]{1,0:T(8,128)(2,1)}, u32[]{:S(2)}, u32[]{:S(2)}) collective-permute-start(bf16[64,4096]{1,0:T(8,128)(2,1)} %reshape.120), channel_id=1, source_target_pairs={{0,3},{3,0},{1,4},{4,1},{2,5},{5,2},{6,9},{9,6},{7,10},{10,7},{8,1... | collective-permute-start | bytes 1572872 | tf_op jit(solution)/shard_map/ppermute | solution.py:89
  71.3 1.7 %convert_reduce_fusion = f32[2,4096]{1,0:T(2,128)S(1)} fusion(bf16[32,4,4096]{2,1,0:T(4,128)(2,1)} %all-to-all-done), kind=kLoop, calls=%fused_computation.9 | loop fusion | flops 516096 | bytes 557056 | tf_op jit(solution)/shard_map/reduce_sum | solution.py:87
  73.0 0.2 multiply_reduce_fusion.1
  73.2 0.1 reshape.122
  73.3 1.6 %fusion.2 = f32[64,384]{1,0:T(8,128)S(1)} fusion(bf16[64,4096]{1,0:T(8,128)(2,1)} %reshape.120, bf16[1,4096,384]{2,1,0:T(8,128)(2,1)S(1)} %copy-done), kind=kOutput, calls=%fused_computation.3 | convolution fusion | flops 201326592 | bytes 3768320 | tf_op jit(solution)/shard_map/dot_general | solution.py:97
  74.9 1.6 %select_bitcast_fusion.1 = (f32[1,64,384]{2,1,0:T(8,128)S(1)}, f32[1,64,384]{2,1,0:T(8,128)S(1)}) fusion(f32[64,384]{1,0:T(8,128)S(1)} %fusion.2, pred[]{:T(512)S(6)} %eq.7, bf16[64,4096]{1,0:T(8,128)(2,1)} %collective-permute-done.2, bf16[1,4096,384]{2,1,0:T(8,128)(2,1)S(1)} %copy-done), kind=kOutput, calls=%fused_computation.32 | convolution fusion | flops 201375744 | bytes 3964929 | tf_op jit(solution)/shard_map/dot_general | solution.py:98
  76.5 0.7 pad_maximum_fusion.2
  77.2 1.0 reshape.121
  78.2 0.1 pad_maximum_fusion.1
  78.3 9.5 %all_to_all.15 = f32[3,136,128]{2,1,0:T(8,128)S(1)} all-to-all(f32[3,136,128]{2,1,0:T(8,128)S(1)} %copy.49), channel_id=1, replica_groups=mesh['layer'=2,'half'=2,'px'=4,'py'=8,'core'=2,'cols'=3] {'cols'}, dimensions={0} | all-to-all | bytes 417792 | tf_op jit(solution)/shard_map/all_to_all | solution.py:107
  87.9 0.1 fusion.42
  88.0 0.7 broadcast_in_dim.16
  88.7 9.7 %all-to-all-start.2 = ((bf16[6,128,128]{2,1,0:T(8,128)(2,1)}), bf16[6,128,128]{2,1,0:T(8,128)(2,1)S(1)}, u32[]{:S(2)}, u32[]{:S(2)}) async-start(bf16[6,128,128]{2,1,0:T(8,128)(2,1)} %broadcast_in_dim.16), calls=%async_computation.2 | async-start | bytes 393216 | tf_op jit(solution)/shard_map/all_to_all | solution.py:113
  98.4 0.9 broadcast_select_fusion.1
  99.2 9.3 %collective-permute-start.3 = (bf16[2,4096]{1,0:T(2,128)(2,1)S(1)}, bf16[2,4096]{1,0:T(2,128)(2,1)S(1)}, u32[]{:S(2)}, u32[]{:S(2)}) collective-permute-start(bf16[2,4096]{1,0:T(2,128)(2,1)S(1)} %get-tuple-element.13), channel_id=1, source_target_pairs={{0,576},{192,0},{384,192},{576,384},{1,577},{193,1},{385,193},{577... | collective-permute-start | bytes 49160 | tf_op jit(solution)/shard_map/ppermute | solution.py:17
  108.6 1.9 %collective-permute-start.1 = (bf16[2,4096]{1,0:T(2,128)(2,1)S(1)}, bf16[2,4096]{1,0:T(2,128)(2,1)S(1)}, u32[]{:S(2)}, u32[]{:S(2)}) collective-permute-start(bf16[2,4096]{1,0:T(2,128)(2,1)S(1)} %get-tuple-element.14), channel_id=1, source_target_pairs={{0,192},{192,384},{384,576},{576,0},{1,193},{193,385},{385,577},{5... | collective-permute-start | bytes 49160 | tf_op jit(solution)/shard_map/ppermute | solution.py:17
  110.5 6.9 %collective-permute-done.1 = bf16[2,4096]{1,0:T(2,128)(2,1)S(1)} collective-permute-done((bf16[2,4096]{1,0:T(2,128)(2,1)S(1)}, bf16[2,4096]{1,0:T(2,128)(2,1)S(1)}, u32[]{:S(2)}, u32[]{:S(2)}) %collective-permute-start.1) | collective-permute-done | bytes 16416 | tf_op jit(solution)/shard_map/ppermute | solution.py:17
  117.4 0.1 constant_dynamic-slice_fusion
  117.5 0.1 copy.51
  117.6 0.7 broadcast_in_dim_reshape.3
  118.4 0.6 copy.74
  119.0 0.6 copy.75
  (21 shorter events, 0.2 us)
Async XLA Ops:
  0.6 2.7 %copy-start = (bf16[1,4096,384]{2,1,0:T(8,128)(2,1)S(1)}, bf16[1,4096,384]{2,1,0:T(8,128)(2,1)}, u32[]{:S(2)}) copy-start(bf16[1,4096,384]{2,1,0:T(8,128)(2,1)} %param.13) | copy-start | bytes 9437188
  0.6 6.5 %copy-start.1 = (bf16[1,2,4096]{2,1,0:T(2,128)(2,1)S(1)}, bf16[1,2,4096]{2,1,0:T(2,128)(2,1)}, u32[]{:S(2)}) copy-start(bf16[1,2,4096]{2,1,0:T(2,128)(2,1)} %param.11) | copy-start | bytes 49156
  0.7 6.8 %copy-start.2 = (bf16[1,2,4096]{2,1,0:T(2,128)(2,1)S(1)}, bf16[1,2,4096]{2,1,0:T(2,128)(2,1)}, u32[]{:S(2)}) copy-start(bf16[1,2,4096]{2,1,0:T(2,128)(2,1)} %param.8) | copy-start | bytes 49156
  0.7 14.7 %copy-start.3 = (bf16[1,2,4096]{2,1,0:T(2,128)(2,1)S(1)}, bf16[1,2,4096]{2,1,0:T(2,128)(2,1)}, u32[]{:S(2)}) copy-start(bf16[1,2,4096]{2,1,0:T(2,128)(2,1)} %param.10) | copy-start | bytes 49156
  3.3 12.1 %copy-start.4 = (f32[2,4096]{1,0:T(2,128)S(1)}, f32[2,4096]{1,0:T(2,128)}, u32[]{:S(2)}) copy-start(f32[2,4096]{1,0:T(2,128)} %param.15) | copy-start | bytes 98308
  3.3 12.1 %copy-start.5 = (f32[2,4096]{1,0:T(2,128)S(1)}, f32[2,4096]{1,0:T(2,128)}, u32[]{:S(2)}) copy-start(f32[2,4096]{1,0:T(2,128)} %param.14) | copy-start | bytes 98308
  5.2 10.3 %collective-permute-start = (bf16[64,4096]{1,0:T(8,128)(2,1)}, bf16[64,4096]{1,0:T(8,128)(2,1)}, u32[]{:S(2)}, u32[]{:S(2)}) collective-permute-start(bf16[64,4096]{1,0:T(8,128)(2,1)} %convolution_convert_fusion), channel_id=1, source_target_pairs={{0,3},{3,0},{1,4},{4,1},{2,5},{5,2},{6,9},{9,6},{7,10},{10,7},{8,1... | collective-permute-start | bytes 1572872 | tf_op jit(solution)/shard_map/ppermute | solution.py:76
  24.3 40.4 %all-to-all-start = ((bf16[32,4,4096]{2,1,0:T(4,128)(2,1)}), bf16[32,4,4096]{2,1,0:T(4,128)(2,1)}, u32[]{:S(2)}, u32[]{:S(2)}) async-start(bf16[32,4,4096]{2,1,0:T(4,128)(2,1)} %pad_maximum_fusion), calls=%async_computation | async-start | bytes 2097152 | tf_op jit(solution)/shard_map/all_to_all | solution.py:86
  69.4 5.5 %collective-permute-start.2 = (bf16[64,4096]{1,0:T(8,128)(2,1)}, bf16[64,4096]{1,0:T(8,128)(2,1)}, u32[]{:S(2)}, u32[]{:S(2)}) collective-permute-start(bf16[64,4096]{1,0:T(8,128)(2,1)} %reshape.120), channel_id=1, source_target_pairs={{0,3},{3,0},{1,4},{4,1},{2,5},{5,2},{6,9},{9,6},{7,10},{10,7},{8,1... | collective-permute-start | bytes 1572872 | tf_op jit(solution)/shard_map/ppermute | solution.py:89
  88.7 28.8 %all-to-all-start.2 = ((bf16[6,128,128]{2,1,0:T(8,128)(2,1)}), bf16[6,128,128]{2,1,0:T(8,128)(2,1)S(1)}, u32[]{:S(2)}, u32[]{:S(2)}) async-start(bf16[6,128,128]{2,1,0:T(8,128)(2,1)} %broadcast_in_dim.16), calls=%async_computation.2 | async-start | bytes 393216 | tf_op jit(solution)/shard_map/all_to_all | solution.py:113
  99.2 11.3 %collective-permute-start.3 = (bf16[2,4096]{1,0:T(2,128)(2,1)S(1)}, bf16[2,4096]{1,0:T(2,128)(2,1)S(1)}, u32[]{:S(2)}, u32[]{:S(2)}) collective-permute-start(bf16[2,4096]{1,0:T(2,128)(2,1)S(1)} %get-tuple-element.13), channel_id=1, source_target_pairs={{0,576},{192,0},{384,192},{576,384},{1,577},{193,1},{385,193},{577... | collective-permute-start | bytes 49160 | tf_op jit(solution)/shard_map/ppermute | solution.py:17
  108.6 8.9 %collective-permute-start.1 = (bf16[2,4096]{1,0:T(2,128)(2,1)S(1)}, bf16[2,4096]{1,0:T(2,128)(2,1)S(1)}, u32[]{:S(2)}, u32[]{:S(2)}) collective-permute-start(bf16[2,4096]{1,0:T(2,128)(2,1)S(1)} %get-tuple-element.14), channel_id=1, source_target_pairs={{0,192},{192,384},{384,576},{576,0},{1,193},{193,385},{385,577},{5... | collective-permute-start | bytes 49160 | tf_op jit(solution)/shard_map/ppermute | solution.py:17

commit v2 on v1

v2 whole, which is shorter than its diff:
```python
import jax
import jax.numpy as jnp
from jax import lax
from jax.experimental import pallas as pl
from jax.experimental.pallas import tpu as pltpu
from jax.sharding import Mesh, PartitionSpec as P

D = 12288
epsilon = 1e-05

LAYER_AXIS, HALF, COLS = "layer", "half", "cols"
PX, PY = "px", "py"
CORE = "core"
ROWS = (PX, PY, CORE)
SECTION = (LAYER_AXIS, HALF)


def statistics(total, squares):
    average = total / D
    inverse_scale = lax.rsqrt(squares / D - average * average + epsilon)
    return (average[:, None], inverse_scale[:, None])


def gelu_slope(preact, upstream):
    return jax.vjp(lambda value: jax.nn.gelu(value, approximate=True), preact)[1](upstream)[0]


def exchange(blocks, axis):
    return lax.all_to_all(blocks, axis, 0, 0, tiled=True)


def spread(block, axis):
    return exchange(jnp.broadcast_to(block[None], (lax.axis_size(axis), *block.shape)), axis)


def picked(rows, index):
    one_hot = (index[:, None] == jnp.arange(rows.shape[0])[None, :]).astype(rows.dtype)
    return jnp.dot(one_hot, rows, preferred_element_type=jnp.float32).astype(rows.dtype)


def high_low(values):
    high = values.astype(jnp.bfloat16)
    return high, (values - high.astype(jnp.float32)).astype(jnp.bfloat16)


def lane_groups(values):
    return sum(values[:, i : i + 128] for i in range(0, values.shape[1], 128))


def rows_step(rows_ref, vectors_ref, weight_ref, product, first, second):
    count = rows_ref.shape[0]
    floats = rows_ref[...].astype(jnp.float32)
    vectors = vectors_ref[...]
    pieces = high_low(floats * vectors[:1]) + high_low(vectors)
    left = jnp.concatenate(pieces, axis=0)
    result = jnp.dot(left, weight_ref[...], preferred_element_type=jnp.float32)
    more = result[2 * count :]
    product[:count] += result[:count] + result[count : 2 * count]
    product[count:] += more[:8] + more[8:]
    first[...] += lane_groups(floats)
    second[...] += lane_groups(floats * floats)


def near_kernel(rows_ref, vectors_ref, weight_ref, product, first, second):
    @pl.when(pl.program_id(0) == 0)
    def _():
        product[...] = jnp.zeros_like(product)
        first[...] = jnp.zeros_like(first)
        second[...] = jnp.zeros_like(second)

    rows_step(rows_ref, vectors_ref, weight_ref, product, first, second)


def far_kernel(
    rows_ref, vectors_ref, weight_ref, near_ref, near_first, near_second, payload, product, first, second
):
    near_kernel(rows_ref, vectors_ref, weight_ref, product, first, second)

    @pl.when(pl.program_id(0) == pl.num_programs(0) - 1)
    def _():
        count = rows_ref.shape[0]
        totals = [
            jnp.sum(jnp.concatenate((near[...], far[...]), axis=0).T, axis=0, keepdims=True)
            for near, far in ((near_first, first), (near_second, second))
        ]
        totals.append(jnp.zeros((4, 128), jnp.float32))
        for i in range(payload.shape[0]):
            part = slice(i * 128, (i + 1) * 128)
            payload[i, :count] = near_ref[:count, part]
            payload[i, count : 2 * count] = product[:count, part]
            payload[i, 2 * count :] = jnp.concatenate(
                [near_ref[count : count + 2, part]] + totals, axis=0
            )


STEPS = 4


def rows_call(kernel, rows, vectors, weight, near=None):
    count, features = rows.shape
    hidden = weight.shape[1]
    step = features // STEPS
    f32 = jnp.float32
    shapes = [(count + 8, hidden), (count, 128), (count, 128)]
    whole = [pl.BlockSpec(shape, lambda k: (0, 0)) for shape in shapes]
    specs = [
        pl.BlockSpec((count, step), lambda k: (0, k)),
        pl.BlockSpec((8, step), lambda k: (0, k)),
        pl.BlockSpec((step, hidden), lambda k: (k, 0)),
    ]
    if near is None:
        out_shape = [jax.ShapeDtypeStruct(shape, f32) for shape in shapes]
        out_specs, scratch, near = whole, [], ()
    else:
        out = (hidden // 128, 2 * count + 8, 128)
        out_shape = jax.ShapeDtypeStruct(out, f32)
        out_specs = pl.BlockSpec(out, lambda k: (0, 0, 0))
        specs = specs + whole
        scratch = [pltpu.VMEM(shape, f32) for shape in shapes]
    return pl.pallas_call(
        kernel,
        grid=(STEPS,),
        in_specs=specs,
        out_specs=out_specs,
        out_shape=out_shape,
        scratch_shapes=scratch,
        compiler_params=pltpu.CompilerParams(vmem_limit_bytes=24 * 2**20),
        cost_estimate=pl.CostEstimate(
            flops=4 * count * features * hidden, bytes_accessed=4 * 2**20, transcendentals=0
        ),
    )(rows, vectors, weight, *near)


def per_device(act_in, hid_in, grad_in, saved_in, saved_pre, weights, norm_gain, norm_bias):
    f32, bf16 = jnp.float32, jnp.bfloat16
    half = lax.axis_index(HALF)
    core = lax.axis_index(CORE)
    layer = lax.axis_index(LAYER_AXIS)
    is_even = half == 0
    gain = lax.dynamic_index_in_dim(norm_gain, layer, 0, keepdims=False)
    offset_bias = lax.dynamic_index_in_dim(norm_bias, layer, 0, keepdims=False)
    weight = weights[0]
    stream, gradient = act_in[0], grad_in[0]
    features, hidden = weight.shape
    tokens = hid_in.shape[1]
    own = stream.shape[0]
    nx, ny, cols = lax.axis_size(PX), lax.axis_size(PY), lax.axis_size(COLS)
    half_tokens = tokens // 2
    part = hidden // cols

    early = lax.ppermute(
        jnp.where(is_even, stream, gradient), SECTION, [(0, 1), (1, 0), (2, 3), (3, 2)]
    )

    token = jnp.arange(tokens)
    y_of, t_of = (token // own) % ny, token % own
    c_of, x_of = (token // (own * ny)) % 2, token // (own * ny * 2)
    slope = gelu_slope(saved_pre[0].astype(f32), hid_in[0].astype(f32)).astype(bf16)
    right_side = jnp.where(is_even, slope, hid_in[0])
    right_side = picked(right_side, ((x_of * ny + y_of) * 2 + c_of) * own + t_of)
    row_terms = lax.dot_general(
        right_side, weight, (((1,), (1,)), ((), ())), preferred_element_type=f32
    ).astype(bf16)
    chip_blocks = exchange(row_terms.reshape(nx * 2, ny * own, features), (PX, CORE))
    chip_sum = jnp.sum(chip_blocks.astype(f32), axis=0).astype(bf16)
    y_blocks = exchange(chip_sum.reshape(ny, own, features), PY)
    term = jnp.sum(y_blocks.astype(f32), axis=0)

    leading = jnp.where(is_even, stream, gradient)
    near = spread(leading, PY).reshape(ny * own, features)
    near = jnp.concatenate(
        [near]
        + [lax.ppermute(near, PX, [(i, (i + k) % nx) for i in range(nx)]) for k in range(1, nx)]
    )
    far = lax.ppermute(near, CORE, [(0, 1), (1, 0)])
    factor = jnp.where(is_even, gain, 1.0)
    vectors = jnp.concatenate(
        (factor[None], offset_bias[None], jnp.zeros((6, features), f32))
    )
    near_parts = rows_call(near_kernel, near, vectors, weight)
    payload = rows_call(far_kernel, far, vectors, weight, near_parts)

    stream_float = stream.astype(f32)
    saved_float = saved_in[0].astype(f32)
    scaled = term * gain
    moments = jnp.stack(
        (
            jnp.sum(saved_float, axis=-1),
            jnp.sum(saved_float * saved_float, axis=-1),
            jnp.sum(scaled, axis=-1),
            jnp.sum(scaled * saved_float, axis=-1),
        )
    ).reshape(1, -1)

    moments = jnp.pad(moments, ((0, 0), (0, 128 - moments.size)))
    payload = payload.at[:, tokens + 4].set(moments)
    summed = jnp.sum(exchange(payload, COLS), axis=0)
    totals = summed[tokens + 2 : tokens + 4]
    mean, scale = statistics(totals[0], totals[1])
    preact = scale * (summed[:tokens] - mean * summed[tokens]) + summed[tokens + 1]
    hidden_value = jnp.where(
        is_even, jax.nn.gelu(preact, approximate=True), summed[:tokens]
    ).astype(bf16)
    other = ((token // own) % 2 != core).astype(jnp.int32)
    behind = (lax.axis_index(PX) - token // (2 * own * ny)) % nx
    place = ((other * nx + behind) * ny + (token // (2 * own)) % ny) * own + t_of
    hidden_value = picked(hidden_value, place)

    incoming = spread(hidden_value, (HALF, COLS)).reshape(2, cols, tokens, part)
    incoming = lax.dynamic_index_in_dim(incoming, 1 - half, 0, keepdims=False)
    hidden_next = jnp.concatenate([incoming[i] for i in range(cols)], axis=1)

    forward_odd = stream_float + term
    moments = summed[tokens + 4, : 4 * own].reshape(4, own)
    saved_mean, saved_scale = statistics(moments[0], moments[1])
    saved_hat = (saved_float - saved_mean) * saved_scale
    first_mean = moments[2][:, None] / D
    second_mean = saved_scale * (moments[3][:, None] / D - saved_mean * first_mean)
    backward_even = gradient.astype(f32) + saved_scale * (
        scaled - first_mean - saved_hat * second_mean
    )
    late = jnp.where(is_even, backward_even, forward_odd).astype(bf16)
    late = lax.ppermute(late, SECTION, [(0, 3), (3, 0), (1, 2), (2, 1)])

    act_next = jnp.where(is_even, late, early)
    grad_next = jnp.where(is_even, early, late)
    return (act_next[None], hidden_next[None], grad_next[None])


def solution(mesh):
    names = SECTION + ROWS + (COLS,)
    parts = Mesh(mesh.devices.reshape(2, 2, 4, 8, 2, 3), names)
    in_specs = (
        P(SECTION, ROWS, COLS),
        P(SECTION, None, ROWS),
        P(SECTION, ROWS, COLS),
        P(SECTION, ROWS, COLS),
        P(SECTION, None, ROWS),
        P(SECTION, COLS, ROWS),
        P(None, COLS),
        P(None, COLS),
    )
    out_specs = (P(SECTION, ROWS, COLS), P(SECTION, None, ROWS), P(SECTION, ROWS, COLS))
    return jax.shard_map(
        per_device, mesh=parts, in_specs=in_specs, out_specs=out_specs, check_vma=False
    )
```

time: 121 us -> 105 us (0.87)
  starting transfers between devices: 36.7 us -> 59 us
  blocking collectives: 17.2 us -> 0 us
  waiting for transfers between devices: 35.4 us -> 22 us
  local copies, waits for them, and re-layouts: 13.7 us -> 6.43 us
  Pallas kernels: 0 us -> 6.5 us
  matrix products: 8.11 us -> 4.51 us
  other arithmetic: 7.54 us -> 5.13 us
    all_to_all x2 -> x5, waiting for transfers between devices: 28.5 us -> 13.7 us  [exchange(): return lax.all_to_all(blocks, axis, 0, 0, tiled=True)]
    ppermute x4 -> x6, starting transfers between devices: 15.1 us -> 28.8 us  [the longest x3 11.8 us: per_device(): lax.ppermute(near, PX, [(i, (i + k) % nx) for i in range(nx)])]
    all_to_all x1 -> x0, blocking collectives: 9.5 us -> none  [per_device(): summed = jnp.sum(lax.all_to_all(partial, COLS, 0, 0, tiled=True), axis=0)]
    all_to_all x2 -> x5, starting transfers between devices: 21.6 us -> 30.2 us  [exchange(): return lax.all_to_all(blocks, axis, 0, 0, tiled=True)]
    psum x1 -> x0, blocking collectives: 7.66 us -> none  [per_device(): lax.psum(jnp.stack((jnp.sum(stream_float, axis=-1), jnp.sum(stream_float...]
    pallas_call x0 -> x2, Pallas kernels: none -> 6.5 us  [rows_call(): pl.pallas_call(kernel, grid=(STEPS,), in_specs=specs, out_specs=out_specs...]
    reshape x4 -> x3, local copies, waits for them, and re-layouts: 5.31 us -> 0.88 us  [the longest x1 0.75 us: per_device(): y_blocks = exchange(chip_sum.reshape(ny, own, features), PY)]
    dot_general x4 -> x2, matrix products: 8.11 us -> 4.51 us  [the longest x1 4.27 us: per_device(): lax.dot_general(right_side, weight, (((1,), (1,)), ((), ())), preferred_e...]
  transfers between devices with their start and end apart: 6 -> 11, of which waited for: 2 -> 5; matrix products, arithmetic and copies ran while one was open for 4% -> 12% of each run, Pallas kernels for 0% -> 6%
where the time goes in v2:
time: 105 us; the launch traced here: 104 us
  starting transfers between devices  59 us (56%)
  waiting for transfers between devices  22 us (21%)
  Pallas kernels  6.5 us (6%)
  local copies, waits for them, and re-layouts  6.43 us (6%)
  other arithmetic  5.13 us (5%)
  matrix products  4.51 us (4%)
    all_to_all x5, starting transfers between devices, exchange(): return lax.all_to_all(blocks, axis, 0, 0, tiled=True)  30.2 us
    all_to_all x5, waiting for transfers between devices, exchange(): return lax.all_to_all(blocks, axis, 0, 0, tiled=True)  13.7 us
    ppermute x3, starting transfers between devices, per_device(): lax.ppermute(near, PX, [(i, (i + k) % nx) for i in range(nx)])  11.8 us
    ppermute x1, starting transfers between devices, per_device(): late = lax.ppermute(late, SECTION, [(0, 3), (3, 0), (1, 2), (2, 1)])  9.09 us
    ppermute x3, waiting for transfers between devices, per_device(): lax.ppermute(near, PX, [(i, (i + k) % nx) for i in range(nx)])  8.37 us
    pallas_call x2, Pallas kernels, rows_call(): pl.pallas_call(kernel, grid=(STEPS,), in_specs=specs, out_specs=out_specs...  6.5 us
    ppermute x1, starting transfers between devices, per_device(): lax.ppermute(jnp.where(is_even, stream, gradient), SECTION, [(0, 1), (1,...  6.05 us
    dot_general x1, matrix products, per_device(): lax.dot_general(right_side, weight, (((1,), (1,)), ((), ())), preferred_e...  4.27 us
  transfers between devices with their start and end apart: 11, of which 5 were waited for; matrix products, arithmetic and copies ran while one was open for 12% of the time, Pallas kernels for 6%

profile of v2, /device:TPU:8, one launch (start us, length us, event | category | flops | bytes accessed | tf_op | source)
XLA Modules:
  0.0 104.5 jit_solution(15181915986693661632)
XLA Ops:
  0.6 0.0 copy-start
  0.7 0.7 fusion.59
  1.4 0.7 broadcast_in_dim.21
  2.1 12.7 %all-to-all-start = ((bf16[8,2,4096]{2,1,0:T(2,128)(2,1)}), bf16[8,2,4096]{2,1,0:T(2,128)(2,1)S(1)}, u32[]{:S(2)}, u32[]{:S(2)}) async-start(bf16[8,2,4096]{2,1,0:T(2,128)(2,1)} %broadcast_in_dim.21), calls=%async_computation | async-start | bytes 262144 | tf_op jit(solution)/shard_map/all_to_all | solution.py:29
  14.9 0.8 broadcast_select_fusion
  15.7 0.1 pad.16.clone
  15.8 4.3 %convolution_convert_fusion = bf16[128,4096]{1,0:T(8,128)(2,1)} fusion(bf16[1,128,384]{2,1,0:T(8,128)(2,1)} %param.14, bf16[1,128,384]{2,1,0:T(8,128)(2,1)} %param.11, pred[]{:T(512)S(6)} %eq.36, s32[128]{0:T(128)S(1)} %multiply_add_fusion.1, bf16[1,4096,384]{2,1,0:T(8,128)(2,1)} %param.15), kind=kOutput, calls=%fused_computation | convolution fusion | flops 416956416 | bytes 4391425 | tf_op jit(solution)/shard_map/dot_general | solution.py:161
  20.1 2.4 %all-to-all-done = bf16[8,2,4096]{2,1,0:T(2,128)(2,1)S(1)} async-done(((bf16[8,2,4096]{2,1,0:T(2,128)(2,1)}), bf16[8,2,4096]{2,1,0:T(2,128)(2,1)S(1)}, u32[]{:S(2)}, u32[]{:S(2)}) %all-to-all-start) | async-done | bytes 131104 | tf_op jit(solution)/shard_map/all_to_all | solution.py:29
  22.5 4.3 %all-to-all-start.1 = ((bf16[8,16,4096]{2,1,0:T(8,128)(2,1)}), bf16[8,16,4096]{2,1,0:T(8,128)(2,1)}, u32[]{:S(2)}, u32[]{:S(2)}) async-start(bf16[8,16,4096]{2,1,0:T(8,128)(2,1)} %bitcast.111), calls=%async_computation.1 | async-start | bytes 2097152 | tf_op jit(solution)/shard_map/all_to_all | solution.py:29
  26.8 0.1 reshape.263
  26.8 3.8 %collective-permute-start = (bf16[16,4096]{1,0:T(8,128)(2,1)S(1)}, bf16[16,4096]{1,0:T(8,128)(2,1)S(1)}, u32[]{:S(2)}, u32[]{:S(2)}) collective-permute-start(bf16[16,4096]{1,0:T(8,128)(2,1)S(1)} %reshape.263), channel_id=1, source_target_pairs={{0,48},{48,96},{96,144},{144,0},{1,49},{49,97},{97,145},{145,1},{2... | collective-permute-start | bytes 393224 | tf_op jit(solution)/shard_map/ppermute | solution.py:173
  30.6 0.7 constant_dynamic-update-slice_fusion.3
  31.3 4.6 %collective-permute-start.1 = (bf16[16,4096]{1,0:T(8,128)(2,1)S(1)}, bf16[16,4096]{1,0:T(8,128)(2,1)S(1)}, u32[]{:S(2)}, u32[]{:S(2)}) collective-permute-start(bf16[16,4096]{1,0:T(8,128)(2,1)S(1)} %reshape.263), channel_id=1, source_target_pairs={{0,96},{48,144},{96,0},{144,48},{1,97},{49,145},{97,1},{145,49},{2... | collective-permute-start | bytes 393224 | tf_op jit(solution)/shard_map/ppermute | solution.py:173
  35.9 3.4 %collective-permute-start.2 = (bf16[16,4096]{1,0:T(8,128)(2,1)S(1)}, bf16[16,4096]{1,0:T(8,128)(2,1)S(1)}, u32[]{:S(2)}, u32[]{:S(2)}) collective-permute-start(bf16[16,4096]{1,0:T(8,128)(2,1)S(1)} %reshape.263), channel_id=1, source_target_pairs={{0,144},{48,0},{96,48},{144,96},{1,145},{49,1},{97,49},{145,97},{2... | collective-permute-start | bytes 393224 | tf_op jit(solution)/shard_map/ppermute | solution.py:173
  39.3 6.0 %collective-permute-done = bf16[16,4096]{1,0:T(8,128)(2,1)S(1)} collective-permute-done((bf16[16,4096]{1,0:T(8,128)(2,1)S(1)}, bf16[16,4096]{1,0:T(8,128)(2,1)S(1)}, u32[]{:S(2)}, u32[]{:S(2)}) %collective-permute-start) | collective-permute-done | bytes 131104 | tf_op jit(solution)/shard_map/ppermute | solution.py:173
  45.3 0.7 constant_dynamic-update-slice_fusion.2
  46.0 2.3 %collective-permute-done.1 = bf16[16,4096]{1,0:T(8,128)(2,1)S(1)} collective-permute-done((bf16[16,4096]{1,0:T(8,128)(2,1)S(1)}, bf16[16,4096]{1,0:T(8,128)(2,1)S(1)}, u32[]{:S(2)}, u32[]{:S(2)}) %collective-permute-start.1) | collective-permute-done | bytes 131104 | tf_op jit(solution)/shard_map/ppermute | solution.py:173
  48.3 0.7 constant_dynamic-update-slice_fusion.1
  49.0 0.7 constant_dynamic-update-slice_fusion.rows_ref
  49.6 1.9 %collective-permute-start.3 = (bf16[64,4096]{1,0:T(8,128)(2,1)}, bf16[64,4096]{1,0:T(8,128)(2,1)}, u32[]{:S(2)}, u32[]{:S(2)}) collective-permute-start(bf16[64,4096]{1,0:T(8,128)(2,1)} %constant_dynamic-update-slice_fusion.rows_ref), channel_id=1, source_target_pairs={{0,3},{3,0},{1,4},{4,1},{2,5},{5,2},{6,9},{9,6},{7,10},{10,7},{8,1... | collective-permute-start | bytes 1572872 | tf_op jit(solution)/shard_map/ppermute | solution.py:175
  51.6 0.0 all-to-all-done.1
  51.6 1.4 %reduce_sum.68 = bf16[16,4096]{1,0:T(8,128)(2,1)S(1)} reduce(bf16[8,16,4096]{2,1,0:T(8,128)(2,1)} %all-to-all-done.1, bf16[]{:T(256)} %constant.198.clone.1), dimensions={0}, to_apply=%region_2.3 | reduce | flops 458752 | bytes 1179650 | tf_op jit(solution)/shard_map/reduce_sum | solution.py:165
  52.9 0.7 reshape.265
  53.7 5.1 %all-to-all-start.2 = ((bf16[8,2,4096]{2,1,0:T(2,128)(2,1)}), bf16[8,2,4096]{2,1,0:T(2,128)(2,1)S(1)}, u32[]{:S(2)}, u32[]{:S(2)}) async-start(bf16[8,2,4096]{2,1,0:T(2,128)(2,1)} %reshape.265), calls=%async_computation.2 | async-start | bytes 262144 | tf_op jit(solution)/shard_map/all_to_all | solution.py:29
  58.7 0.1 maximum_maximum_fusion.vectors_ref
  58.8 0.1 convert_reduce_fusion.1
  59.0 2.9 %shard_map.103 = (f32[72,384]{1,0:T(8,128)S(1)}, f32[64,128]{1,0:T(8,128)S(1)}, f32[64,128]{1,0:T(8,128)S(1)}) custom-call(bf16[64,4096]{1,0:T(8,128)(2,1)} %constant_dynamic-update-slice_fusion.rows_ref, f32[8,4096]{1,0:T(8,128)S(1)} %maximum_maximum_fusion.vectors_ref, bf16[4096,384]{1,0:T(8,128)(2,1)S(1)} %bitcast.109), custom_call_target="tpu_custom_call" | custom-call | flops 402653184 | bytes 4194304 | tf_op jit(solution)/shard_map/pallas_call | solution.py:120
  61.9 0.0 copy-start.3
  61.9 0.0 copy-start.4
  61.9 3.6 %shard_map.104 = f32[3,136,128]{2,1,0:T(8,128)} custom-call(bf16[64,4096]{1,0:T(8,128)(2,1)} %collective-permute-done.3.rows_ref, f32[8,4096]{1,0:T(8,128)S(1)} %maximum_maximum_fusion.vectors_ref, bf16[4096,384]{1,0:T(8,128)(2,1)S(1)} %bitcast.110, f32[72,384]{1,0:T(8,128)S(1)} %get-tuple-element.18.near_ref, f32[64,128]{1,0:T(8,128)S(1)} %get-tuple-element.19.near_first, ...), custom_call_target="tpu_custom_call" | custom-call | flops 402653184 | bytes 4194304 | tf_op jit(solution)/shard_map/pallas_call | solution.py:120
  65.5 1.4 %all-to-all-done.2 = bf16[8,2,4096]{2,1,0:T(2,128)(2,1)S(1)} async-done(((bf16[8,2,4096]{2,1,0:T(2,128)(2,1)}), bf16[8,2,4096]{2,1,0:T(2,128)(2,1)S(1)}, u32[]{:S(2)}, u32[]{:S(2)}) %all-to-all-start.2) | async-done | bytes 131104 | tf_op jit(solution)/shard_map/all_to_all | solution.py:29
  66.9 0.2 convert_reduce_fusion
  67.1 0.2 multiply_reduce_fusion
  67.3 0.1 reshape.266
  67.4 1.3 %scatter.4 = f32[3,136,128]{2,1,0:T(8,128)} dynamic-update-slice(f32[3,136,128]{2,1,0:T(8,128)} %shard_map.104, f32[3,1,128]{2,1,0:T(1,128)S(1)} %broadcast.452, s32[]{:T(128)} %constant.180.clone.1, s32[]{:T(128)} %constant.199.clone.1, s32[]{:T(128)} %constant.180.clone.1) | dynamic-update-slice | bytes 3076 | tf_op jit(solution)/shard_map/scatter | solution.py:196
  68.7 3.4 %all-to-all-start.3 = ((f32[3,136,128]{2,1,0:T(8,128)}), f32[3,136,128]{2,1,0:T(8,128)S(1)}, u32[]{:S(2)}, u32[]{:S(2)}) async-start(f32[3,136,128]{2,1,0:T(8,128)} %scatter.4), calls=%async_computation.3 | async-start | bytes 417792 | tf_op jit(solution)/shard_map/all_to_all | solution.py:29
  72.2 6.1 %collective-permute-start.5 = (bf16[2,4096]{1,0:T(2,128)(2,1)S(1)}, bf16[2,4096]{1,0:T(2,128)(2,1)S(1)}, u32[]{:S(2)}, u32[]{:S(2)}) collective-permute-start(bf16[2,4096]{1,0:T(2,128)(2,1)S(1)} %fusion.59), channel_id=1, source_target_pairs={{0,192},{192,0},{384,576},{576,384},{1,193},{193,1},{385,577},{577... | collective-permute-start | bytes 49160 | tf_op jit(solution)/shard_map/ppermute | solution.py:151
  78.2 0.0 all-to-all-done.3
  78.3 0.1 fusion.73
  78.4 0.1 fusion.74
  78.5 0.1 fusion.56
  78.6 9.1 %collective-permute-start.4 = (bf16[2,4096]{1,0:T(2,128)(2,1)S(1)}, bf16[2,4096]{1,0:T(2,128)(2,1)S(1)}, u32[]{:S(2)}, u32[]{:S(2)}) collective-permute-start(bf16[2,4096]{1,0:T(2,128)(2,1)S(1)} %fusion.56), channel_id=1, source_target_pairs={{0,576},{576,0},{192,384},{384,192},{1,577},{577,1},{193,385},{385... | collective-permute-start | bytes 49160 | tf_op jit(solution)/shard_map/ppermute | solution.py:223
  87.7 0.2 convolution_convert_fusion.2
  87.9 0.7 broadcast_in_dim.26
  88.6 4.7 %all-to-all-start.4 = ((bf16[6,128,128]{2,1,0:T(8,128)(2,1)}), bf16[6,128,128]{2,1,0:T(8,128)(2,1)S(1)}, u32[]{:S(2)}, u32[]{:S(2)}) async-start(bf16[6,128,128]{2,1,0:T(8,128)(2,1)} %broadcast_in_dim.26), calls=%async_computation.4 | async-start | bytes 393216 | tf_op jit(solution)/shard_map/all_to_all | solution.py:29
  93.3 0.6 fusion.58
  94.0 9.8 %all-to-all-done.4 = bf16[6,128,128]{2,1,0:T(8,128)(2,1)S(1)} async-done(((bf16[6,128,128]{2,1,0:T(8,128)(2,1)}), bf16[6,128,128]{2,1,0:T(8,128)(2,1)S(1)}, u32[]{:S(2)}, u32[]{:S(2)}) %all-to-all-start.4) | async-done | bytes 196640 | tf_op jit(solution)/shard_map/all_to_all | solution.py:29
  103.8 0.7 maximum_bitcast_fusion
  (22 shorter events, 0.1 us)
Async XLA Ops:
  0.6 14.3 %copy-start = (f32[2,4096]{1,0:T(2,128)S(1)}, f32[2,4096]{1,0:T(2,128)}, u32[]{:S(2)}) copy-start(f32[2,4096]{1,0:T(2,128)} %param.17) | copy-start | bytes 98308
  2.1 20.4 %all-to-all-start = ((bf16[8,2,4096]{2,1,0:T(2,128)(2,1)}), bf16[8,2,4096]{2,1,0:T(2,128)(2,1)S(1)}, u32[]{:S(2)}, u32[]{:S(2)}) async-start(bf16[8,2,4096]{2,1,0:T(2,128)(2,1)} %broadcast_in_dim.21), calls=%async_computation | async-start | bytes 262144 | tf_op jit(solution)/shard_map/all_to_all | solution.py:29
  20.1 38.8 %copy-start.2 = (bf16[1,2,4096]{2,1,0:T(2,128)(2,1)S(1)}, bf16[1,2,4096]{2,1,0:T(2,128)(2,1)}, u32[]{:S(2)}) copy-start(bf16[1,2,4096]{2,1,0:T(2,128)(2,1)} %param.13) | copy-start | bytes 49156
  20.1 38.9 %copy-start.1 = (bf16[1,4096,384]{2,1,0:T(8,128)(2,1)S(1)}, bf16[1,4096,384]{2,1,0:T(8,128)(2,1)}, u32[]{:S(2)}) copy-start(bf16[1,4096,384]{2,1,0:T(8,128)(2,1)} %param.15) | copy-start | bytes 9437188
  22.5 29.0 %all-to-all-start.1 = ((bf16[8,16,4096]{2,1,0:T(8,128)(2,1)}), bf16[8,16,4096]{2,1,0:T(8,128)(2,1)}, u32[]{:S(2)}, u32[]{:S(2)}) async-start(bf16[8,16,4096]{2,1,0:T(8,128)(2,1)} %bitcast.111), calls=%async_computation.1 | async-start | bytes 2097152 | tf_op jit(solution)/shard_map/all_to_all | solution.py:29
  26.8 18.5 %collective-permute-start = (bf16[16,4096]{1,0:T(8,128)(2,1)S(1)}, bf16[16,4096]{1,0:T(8,128)(2,1)S(1)}, u32[]{:S(2)}, u32[]{:S(2)}) collective-permute-start(bf16[16,4096]{1,0:T(8,128)(2,1)S(1)} %reshape.263), channel_id=1, source_target_pairs={{0,48},{48,96},{96,144},{144,0},{1,49},{49,97},{97,145},{145,1},{2... | collective-permute-start | bytes 393224 | tf_op jit(solution)/shard_map/ppermute | solution.py:173
  31.3 17.0 %collective-permute-start.1 = (bf16[16,4096]{1,0:T(8,128)(2,1)S(1)}, bf16[16,4096]{1,0:T(8,128)(2,1)S(1)}, u32[]{:S(2)}, u32[]{:S(2)}) collective-permute-start(bf16[16,4096]{1,0:T(8,128)(2,1)S(1)} %reshape.263), channel_id=1, source_target_pairs={{0,96},{48,144},{96,0},{144,48},{1,97},{49,145},{97,1},{145,49},{2... | collective-permute-start | bytes 393224 | tf_op jit(solution)/shard_map/ppermute | solution.py:173
  35.9 13.1 %collective-permute-start.2 = (bf16[16,4096]{1,0:T(8,128)(2,1)S(1)}, bf16[16,4096]{1,0:T(8,128)(2,1)S(1)}, u32[]{:S(2)}, u32[]{:S(2)}) collective-permute-start(bf16[16,4096]{1,0:T(8,128)(2,1)S(1)} %reshape.263), channel_id=1, source_target_pairs={{0,144},{48,0},{96,48},{144,96},{1,145},{49,1},{97,49},{145,97},{2... | collective-permute-start | bytes 393224 | tf_op jit(solution)/shard_map/ppermute | solution.py:173
  49.6 12.3 %collective-permute-start.3 = (bf16[64,4096]{1,0:T(8,128)(2,1)}, bf16[64,4096]{1,0:T(8,128)(2,1)}, u32[]{:S(2)}, u32[]{:S(2)}) collective-permute-start(bf16[64,4096]{1,0:T(8,128)(2,1)} %constant_dynamic-update-slice_fusion.rows_ref), channel_id=1, source_target_pairs={{0,3},{3,0},{1,4},{4,1},{2,5},{5,2},{6,9},{9,6},{7,10},{10,7},{8,1... | collective-permute-start | bytes 1572872 | tf_op jit(solution)/shard_map/ppermute | solution.py:175
  53.7 13.2 %all-to-all-start.2 = ((bf16[8,2,4096]{2,1,0:T(2,128)(2,1)}), bf16[8,2,4096]{2,1,0:T(2,128)(2,1)S(1)}, u32[]{:S(2)}, u32[]{:S(2)}) async-start(bf16[8,2,4096]{2,1,0:T(2,128)(2,1)} %reshape.265), calls=%async_computation.2 | async-start | bytes 262144 | tf_op jit(solution)/shard_map/all_to_all | solution.py:29
  61.9 16.6 %copy-start.3 = (bf16[1,2,4096]{2,1,0:T(2,128)(2,1)S(1)}, bf16[1,2,4096]{2,1,0:T(2,128)(2,1)}, u32[]{:S(2)}) copy-start(bf16[1,2,4096]{2,1,0:T(2,128)(2,1)} %param.10) | copy-start | bytes 49156
  61.9 16.6 %copy-start.4 = (bf16[1,2,4096]{2,1,0:T(2,128)(2,1)S(1)}, bf16[1,2,4096]{2,1,0:T(2,128)(2,1)}, u32[]{:S(2)}) copy-start(bf16[1,2,4096]{2,1,0:T(2,128)(2,1)} %param.12) | copy-start | bytes 49156
  68.7 9.6 %all-to-all-start.3 = ((f32[3,136,128]{2,1,0:T(8,128)}), f32[3,136,128]{2,1,0:T(8,128)S(1)}, u32[]{:S(2)}, u32[]{:S(2)}) async-start(f32[3,136,128]{2,1,0:T(8,128)} %scatter.4), calls=%async_computation.3 | async-start | bytes 417792 | tf_op jit(solution)/shard_map/all_to_all | solution.py:29
  72.2 21.2 %collective-permute-start.5 = (bf16[2,4096]{1,0:T(2,128)(2,1)S(1)}, bf16[2,4096]{1,0:T(2,128)(2,1)S(1)}, u32[]{:S(2)}, u32[]{:S(2)}) collective-permute-start(bf16[2,4096]{1,0:T(2,128)(2,1)S(1)} %fusion.59), channel_id=1, source_target_pairs={{0,192},{192,0},{384,576},{576,384},{1,193},{193,1},{385,577},{577... | collective-permute-start | bytes 49160 | tf_op jit(solution)/shard_map/ppermute | solution.py:151
  78.6 14.7 %collective-permute-start.4 = (bf16[2,4096]{1,0:T(2,128)(2,1)S(1)}, bf16[2,4096]{1,0:T(2,128)(2,1)S(1)}, u32[]{:S(2)}, u32[]{:S(2)}) collective-permute-start(bf16[2,4096]{1,0:T(2,128)(2,1)S(1)} %fusion.56), channel_id=1, source_target_pairs={{0,576},{576,0},{192,384},{384,192},{1,577},{577,1},{193,385},{385... | collective-permute-start | bytes 49160 | tf_op jit(solution)/shard_map/ppermute | solution.py:223
  88.6 15.2 %all-to-all-start.4 = ((bf16[6,128,128]{2,1,0:T(8,128)(2,1)}), bf16[6,128,128]{2,1,0:T(8,128)(2,1)S(1)}, u32[]{:S(2)}, u32[]{:S(2)}) async-start(bf16[6,128,128]{2,1,0:T(8,128)(2,1)} %broadcast_in_dim.26), calls=%async_computation.4 | async-start | bytes 393216 | tf_op jit(solution)/shard_map/all_to_all | solution.py:29

commit v3 on v2

v3 whole, which is shorter than its diff:
```python
import jax
import jax.numpy as jnp
from jax import lax
from jax.experimental import pallas as pl
from jax.experimental.pallas import tpu as pltpu
from jax.sharding import Mesh, PartitionSpec as P

D = 12288
epsilon = 1e-05

LAYER_AXIS, HALF, COLS = "layer", "half", "cols"
PX, PY = "px", "py"
CORE = "core"
ROWS = (PX, PY, CORE)
SECTION = (LAYER_AXIS, HALF)


def gelu_slope(preact, upstream):
    return jax.vjp(lambda value: jax.nn.gelu(value, approximate=True), preact)[1](upstream)[0]


def exchange(blocks, axis):
    return lax.all_to_all(blocks, axis, 0, 0, tiled=True)


def copies(block, axis):
    return jnp.broadcast_to(block[None], (lax.axis_size(axis), *block.shape))


def picked(rows, index):
    one_hot = (index[:, None] == jnp.arange(rows.shape[0])[None, :]).astype(rows.dtype)
    return jnp.dot(one_hot, rows, preferred_element_type=jnp.float32).astype(rows.dtype)


def high_low(values):
    high = values.astype(jnp.bfloat16)
    return high, (values - high.astype(jnp.float32)).astype(jnp.bfloat16)


def lane_groups(values):
    return sum(values[:, i : i + 128] for i in range(0, values.shape[1], 128))


def rows_step(rows, vectors_ref, weight_ref, result_ref):
    count = rows.shape[0]

    @pl.when(pl.program_id(0) == 0)
    def _():
        result_ref[...] = jnp.zeros_like(result_ref)

    floats = rows.astype(jnp.float32)
    vectors = vectors_ref[...]
    pieces = high_low(floats * vectors[:1]) + high_low(vectors)
    left = jnp.concatenate(pieces, axis=0)
    result = jnp.dot(left, weight_ref[...], preferred_element_type=jnp.float32)
    more = result[2 * count :]
    result_ref[:count] += result[:count] + result[count : 2 * count]
    result_ref[count : count + 8] += more[:8] + more[8:]
    result_ref[count + 8 :, :128] += lane_groups(floats)
    result_ref[count + 8 :, 128:256] += lane_groups(floats * floats)


def near_kernel(rows_ref, vectors_ref, weight_ref, result_ref):
    rows_step(rows_ref[...], vectors_ref, weight_ref, result_ref)


def far_kernel(rows_ref, vectors_ref, weight_ref, near_ref, payload, result_ref):
    rows_step(rows_ref[...], vectors_ref, weight_ref, result_ref)

    @pl.when(pl.program_id(0) == pl.num_programs(0) - 1)
    def _():
        count = rows_ref.shape[0]
        both = jnp.concatenate((near_ref[count + 8 :, :256], result_ref[count + 8 :, :256]), axis=0)
        totals = [
            jnp.sum(both[:, i : i + 128].T, axis=0, keepdims=True) for i in (0, 128)
        ] + [jnp.zeros((4, 128), jnp.float32)]
        for i in range(payload.shape[0]):
            part = slice(i * 128, (i + 1) * 128)
            payload[i, :count] = near_ref[:count, part]
            payload[i, count : 2 * count] = result_ref[:count, part]
            payload[i, 2 * count :] = jnp.concatenate(
                [near_ref[count : count + 2, part]] + totals, axis=0
            )


STEPS = 4
VMEM_LIMIT = 16 * 2**20


def rows_call(kernel, blocks, vectors, weight, near=None):
    count = sum(block.shape[0] for block in blocks)
    features, hidden = weight.shape
    step = features // STEPS
    f32 = jnp.float32
    shape = (2 * count + 8, hidden)
    whole = pl.BlockSpec(shape, lambda k: (0, 0))
    specs = [pl.BlockSpec((block.shape[0], step), lambda k: (0, k)) for block in blocks] + [
        pl.BlockSpec((8, step), lambda k: (0, k)),
        pl.BlockSpec((step, hidden), lambda k: (k, 0)),
    ]
    if near is None:
        out_shape, out_specs = jax.ShapeDtypeStruct(shape, f32), whole
        scratch, near = [], ()
    else:
        out = (hidden // 128, 2 * count + 8, 128)
        out_shape = jax.ShapeDtypeStruct(out, f32)
        out_specs = pl.BlockSpec(out, lambda k: (0, 0, 0))
        specs = specs + [whole]
        scratch, near = [pltpu.VMEM(shape, f32)], (near,)
    return pl.pallas_call(
        kernel,
        grid=(STEPS,),
        in_specs=specs,
        out_specs=out_specs,
        out_shape=out_shape,
        scratch_shapes=scratch,
        compiler_params=pltpu.CompilerParams(vmem_limit_bytes=VMEM_LIMIT),
        cost_estimate=pl.CostEstimate(flops=0, bytes_accessed=0, transcendentals=0),
    )(*blocks, vectors, weight, *near)


def blocks_of(values):
    row = lax.broadcasted_iota(jnp.int32, (8, 128), 0) // 2
    blocks = []
    for low in range(0, values.shape[0], 8):
        tiles = [values[low : low + 8, m * 128 : m * 128 + 128] for m in range(8)]
        for i in range(4):
            halves = []
            for first in (0, 4):
                half = jnp.zeros((8, 128), jnp.float32)
                for m in range(4):
                    moved = pltpu.roll(tiles[first + m], (2 * (m - i)) % 8, 0)
                    half = jnp.where(row == m, moved, half)
                halves.append(half)
            blocks.append(jnp.concatenate(halves, axis=0))
    return blocks


def terms_kernel(rows_ref, weight_ref, *refs):
    values = lax.dot_general(
        rows_ref[...],
        weight_ref[...],
        (((1,), (1,)), ((), ())),
        preferred_element_type=jnp.float32,
    )
    for p, block in enumerate(blocks_of(values)):
        if len(refs) == 2:
            block = block + refs[0][p].astype(jnp.float32)
        refs[-1][p] = block.astype(jnp.bfloat16)


def terms_call(rows, weight, *arriving):
    count, hidden = rows.shape
    features = weight.shape[0]
    block = pl.BlockSpec((count // 2, 16, 128), lambda k: (0, 0, k))
    return pl.pallas_call(
        terms_kernel,
        grid=(features // 1024,),
        in_specs=[
            pl.BlockSpec((count, hidden), lambda k: (0, 0)),
            pl.BlockSpec((1024, hidden), lambda k: (k, 0)),
        ]
        + [block] * len(arriving),
        out_specs=block,
        out_shape=jax.ShapeDtypeStruct((count // 2, 16, features // 8), jnp.bfloat16),
        compiler_params=pltpu.CompilerParams(vmem_limit_bytes=VMEM_LIMIT),
        cost_estimate=pl.CostEstimate(
            flops=2 * count * features * hidden, bytes_accessed=4 * 2**20, transcendentals=0
        ),
    )(rows, weight, *arriving)


def lines_of(values):
    values = values.reshape(-1, 2, 4, 8, 128).transpose(0, 3, 1, 2, 4)
    return values.reshape(-1, 16, 512)


def total(values):
    return jnp.sum(jnp.sum(values, axis=0, keepdims=True), axis=1, keepdims=True)


def finish_kernel(blocks, lines_ref, gain_ref, payload_in, term_ref, payload_out):
    term = jnp.sum(blocks[...].astype(jnp.float32), axis=0)
    term_ref[...] = term
    saved = lines_ref[0].astype(jnp.float32)
    scaled = term * gain_ref[...]
    lane = lax.broadcasted_iota(jnp.int32, (1, 128), 1)
    token_of = lax.broadcasted_iota(jnp.int32, saved.shape, 0) % 2
    moments = jnp.zeros((1, 128), jnp.float32)
    for i, values in enumerate((saved, saved * saved, scaled, scaled * saved)):
        for token in range(2):
            part = total(jnp.where(token_of == token, values, 0.0))
            moments = jnp.where(lane == 2 * i + token, part, moments)
    row = lax.broadcasted_iota(jnp.int32, (8, 128), 0)
    for i in range(payload_out.shape[0]):
        payload_out[i] = jnp.where(row == 4, moments, payload_in[i])


def finish_call(blocks, lines, gain, payload):
    vmem = pl.BlockSpec(memory_space=pltpu.VMEM)
    tail = pl.BlockSpec((payload.shape[0], 8, 128), lambda i: (0, payload.shape[1] // 8 - 1, 0))
    return pl.pallas_call(
        finish_kernel,
        grid=(1,),
        in_specs=[vmem, vmem, vmem, tail],
        out_specs=[vmem, tail],
        out_shape=[
            jax.ShapeDtypeStruct(gain.shape, jnp.float32),
            jax.ShapeDtypeStruct(payload.shape, payload.dtype),
        ],
        input_output_aliases={3: 1},
        compiler_params=pltpu.CompilerParams(vmem_limit_bytes=VMEM_LIMIT),
        cost_estimate=pl.CostEstimate(flops=2**20, bytes_accessed=2**20, transcendentals=0),
    )(blocks, lines, gain, payload)


def hidden_kernel(even_ref, received, order_ref, hidden_ref, moments_ref):
    f32, bf16 = jnp.float32, jnp.bfloat16
    tokens = order_ref.shape[0]
    summed = jnp.sum(received[...], axis=0)
    extra = summed[tokens:]
    moments_ref[...] = extra
    mean = extra[2:3] / D
    scale = lax.rsqrt(extra[3:4] / D - mean * mean + epsilon)
    columns = jnp.concatenate((scale, mean, jnp.zeros((tokens - 2, tokens), f32)), axis=0).T
    product = summed[:tokens]
    preact = columns[:, :1] * (product - columns[:, 1:2] * extra[:1]) + extra[1:2]
    gelu = jax.nn.gelu(preact, approximate=True)
    hidden = jnp.where(even_ref[0] == 1, gelu, product).astype(bf16)
    hidden = jnp.dot(order_ref[...], hidden, preferred_element_type=f32).astype(bf16)
    for i in range(hidden_ref.shape[0]):
        hidden_ref[i] = hidden


def late_kernel(even_ref, moments_ref, term_ref, lines_ref, gain_ref, late_ref):
    f32 = jnp.float32
    term = term_ref[...]
    saved, stream, gradient = (lines_ref[i].astype(f32) for i in range(3))
    token_of = lax.broadcasted_iota(jnp.int32, saved.shape, 0) % 2
    saved_total, saved_squares, scaled_total, scaled_saved = (
        jnp.where(token_of == 0, moments_ref[4:5, i : i + 1], moments_ref[4:5, i + 1 : i + 2])
        for i in range(0, 8, 2)
    )
    saved_mean = saved_total / D
    saved_scale = lax.rsqrt(saved_squares / D - saved_mean * saved_mean + epsilon)
    first_mean = scaled_total / D
    second_mean = saved_scale * (scaled_saved / D - saved_mean * first_mean)
    saved_hat = (saved - saved_mean) * saved_scale
    change = saved_scale * (term * gain_ref[...] - first_mean - saved_hat * second_mean)
    late = jnp.where(even_ref[0] == 1, gradient + change, stream + term)
    late_ref[...] = late.astype(jnp.bfloat16)


def vmem_call(kernel, flag, out_shape, cost, *operands):
    vmem = pl.BlockSpec(memory_space=pltpu.VMEM)
    return pl.pallas_call(
        kernel,
        in_specs=[pl.BlockSpec(memory_space=pltpu.SMEM)] + [vmem] * len(operands),
        out_specs=[vmem] * len(out_shape),
        out_shape=out_shape,
        compiler_params=pltpu.CompilerParams(vmem_limit_bytes=VMEM_LIMIT),
        cost_estimate=pl.CostEstimate(flops=cost, bytes_accessed=cost, transcendentals=0),
    )(flag, *operands)


def per_device(act_in, hid_in, grad_in, saved_in, saved_pre, weights, norm_gain, norm_bias):
    f32, bf16 = jnp.float32, jnp.bfloat16
    half = lax.axis_index(HALF)
    core = lax.axis_index(CORE)
    layer = lax.axis_index(LAYER_AXIS)
    is_even = half == 0
    gain = lax.dynamic_index_in_dim(norm_gain, layer, 0, keepdims=False)
    offset_bias = lax.dynamic_index_in_dim(norm_bias, layer, 0, keepdims=False)
    weight = weights[0]
    stream, gradient = act_in[0], grad_in[0]
    features, hidden = weight.shape
    tokens = hid_in.shape[1]
    own = stream.shape[0]
    nx, ny, cols = lax.axis_size(PX), lax.axis_size(PY), lax.axis_size(COLS)
    half_tokens = tokens // 2
    part = hidden // cols

    early = lax.ppermute(
        jnp.where(is_even, stream, gradient), SECTION, [(0, 1), (1, 0), (2, 3), (3, 2)]
    )

    leading = copies(jnp.where(is_even, stream, gradient), PY)

    token = jnp.arange(tokens)
    t_of = token % own
    slope = gelu_slope(saved_pre[0].astype(f32), hid_in[0].astype(f32)).astype(bf16)
    right_side = jnp.where(is_even, slope, hid_in[0])
    row, group = token % half_tokens, token // half_tokens
    right_side = picked(right_side, (row // own * 2 + (group != core)) * own + row % own)
    own_x = exchange(leading, PY).reshape(ny * own, features)
    cores = [(0, 1), (1, 0)]
    arriving = lax.ppermute(terms_call(right_side[half_tokens:], weight), CORE, cores)
    own_x, own_rows = lax.optimization_barrier((own_x, right_side[:half_tokens]))
    chip_terms = terms_call(own_rows, weight, arriving)
    own_x, chip_terms = lax.optimization_barrier((own_x, chip_terms))
    term_blocks = exchange(chip_terms, (PX, PY))

    near = lax.all_gather(own_x, PX, axis=0, tiled=True)
    far = lax.ppermute(near, CORE, cores)
    factor = jnp.where(is_even, gain, 1.0)
    vectors = jnp.concatenate(
        (factor[None], offset_bias[None], jnp.zeros((6, features), f32))
    )
    near_parts = rows_call(near_kernel, [near], vectors, weight)
    payload = rows_call(far_kernel, [far], vectors, weight, near_parts)

    line_gain = lines_of(jnp.broadcast_to(gain[None], (own, features)))[0]
    lines = lines_of(jnp.stack((saved_in[0], stream, gradient)))
    term, payload = finish_call(term_blocks, lines, line_gain, payload)
    other = ((token // own) % 2 != core).astype(jnp.int32)
    x_of = token // (2 * own * ny)
    place = ((other * nx + x_of) * ny + (token // (2 * own)) % ny) * own + t_of
    order = (place[:, None] == token[None, :]).astype(bf16)
    received, early = lax.optimization_barrier((exchange(payload, COLS), early))
    flag = is_even.astype(jnp.int32).reshape(1)
    hidden_value, moments = vmem_call(
        hidden_kernel,
        flag,
        [
            jax.ShapeDtypeStruct((2 * cols, tokens, part), bf16),
            jax.ShapeDtypeStruct((8, part), f32),
        ],
        0,
        received,
        order,
    )
    (late,) = vmem_call(
        late_kernel,
        flag,
        [jax.ShapeDtypeStruct(term.shape, bf16)],
        2**24,
        moments,
        term,
        lines,
        line_gain,
    )

    incoming = exchange(hidden_value, (HALF, COLS)).reshape(2, cols, tokens, part)
    incoming = lax.dynamic_index_in_dim(incoming, 1 - half, 0, keepdims=False)
    hidden_next = jnp.concatenate([incoming[i] for i in range(cols)], axis=1)

    late = lax.ppermute(late, SECTION, [(0, 3), (3, 0), (1, 2), (2, 1)])
    late = late.reshape(8, own, 4, 128).transpose(1, 2, 0, 3).reshape(own, features)

    act_next = jnp.where(is_even, late, early)
    grad_next = jnp.where(is_even, early, late)
    return (act_next[None], hidden_next[None], grad_next[None])


def solution(mesh):
    names = SECTION + ROWS + (COLS,)
    parts = Mesh(mesh.devices.reshape(2, 2, 4, 8, 2, 3), names)
    in_specs = (
        P(SECTION, ROWS, COLS),
        P(SECTION, None, ROWS),
        P(SECTION, ROWS, COLS),
        P(SECTION, ROWS, COLS),
        P(SECTION, None, ROWS),
        P(SECTION, COLS, ROWS),
        P(None, COLS),
        P(None, COLS),
    )
    out_specs = (P(SECTION, ROWS, COLS), P(SECTION, None, ROWS), P(SECTION, ROWS, COLS))
    return jax.shard_map(
        per_device, mesh=parts, in_specs=in_specs, out_specs=out_specs, check_vma=False
    )
```

time: 105 us -> 102 us (0.971)
  the two profiles are of different devices: /device:TPU:8 before, /device:TPU:40 now
where the time goes in v3:
time: 102 us; the launch traced here: 101 us
  starting transfers between devices  50.7 us (50%)
  blocking collectives  16.5 us (16%)
  waiting for transfers between devices  12.6 us (12%)
  Pallas kernels  12.2 us (12%)
  local copies, waits for them, and re-layouts  4.63 us (5%)
  other arithmetic  2.37 us (2%)
  matrix products  1.25 us (1%)
    all_to_all x4, starting transfers between devices, exchange(): return lax.all_to_all(blocks, axis, 0, 0, tiled=True)  28.6 us
    all_gather x1, blocking collectives, per_device(): near = lax.all_gather(own_x, PX, axis=0, tiled=True)  16.5 us
    ppermute x1, starting transfers between devices, per_device(): late = lax.ppermute(late, SECTION, [(0, 3), (3, 0), (1, 2), (2, 1)])  10.6 us
    all_to_all x4, waiting for transfers between devices, exchange(): return lax.all_to_all(blocks, axis, 0, 0, tiled=True)  9.82 us
    ppermute x1, starting transfers between devices, per_device(): lax.ppermute(jnp.where(is_even, stream, gradient), SECTION, [(0, 1), (1,...  7.74 us
    pallas_call x2, Pallas kernels, terms_call(): pl.pallas_call(terms_kernel, grid=(features // 1024,), in_specs=[pl.Block...  5.6 us
    pallas_call x2, Pallas kernels, rows_call(): pl.pallas_call(kernel, grid=(STEPS,), in_specs=specs, out_specs=out_specs...  3.56 us
    unnamed x17, local copies, waits for them, and re-layouts  2.71 us
  transfers between devices with their start and end apart: 8, of which 4 were waited for; matrix products, arithmetic and copies ran while one was open for 3% of the time, Pallas kernels for 6%

profile of v3, /device:TPU:40, one launch (start us, length us, event | category | flops | bytes accessed | tf_op | source)
XLA Modules:
  0.0 101.2 jit_solution(8422630671291416391)
XLA Ops:
  0.6 0.0 copy-start
  0.6 0.0 copy-start.5
  0.7 0.0 copy-start.4
  0.7 0.0 copy-start.6
  0.7 0.0 copy-start.7
  0.7 0.8 fusion.17
  1.5 0.7 broadcast_in_dim.39
  2.2 12.9 %all-to-all-start = ((bf16[8,2,4096]{2,1,0:T(2,128)(2,1)}), bf16[8,2,4096]{2,1,0:T(2,128)(2,1)}, u32[]{:S(2)}, u32[]{:S(2)}) async-start(bf16[8,2,4096]{2,1,0:T(2,128)(2,1)} %broadcast_in_dim.39), calls=%async_computation | async-start | bytes 262144 | tf_op jit(solution)/shard_map/all_to_all | solution.py:23
  15.1 1.2 %convolution_convert_fusion = bf16[128,384]{1,0:T(8,128)(2,1)S(1)} fusion(bf16[1,128,384]{2,1,0:T(8,128)(2,1)} %param.12, bf16[1,128,384]{2,1,0:T(8,128)(2,1)} %param.9, pred[]{:T(512)S(6)} %eq.35, s32[128]{0:T(128)S(1)} %fusion.19), kind=kOutput, calls=%fused_computation | convolution fusion | flops 13778944 | bytes 295425 | tf_op jit(solution)/shard_map/dot_general | solution.py:32
  16.4 0.0 copy-start.1
  16.4 1.9 %copy-done.1 = bf16[1,4096,384]{2,1,0:T(8,128)(2,1)S(1)} copy-done((bf16[1,4096,384]{2,1,0:T(8,128)(2,1)S(1)}, bf16[1,4096,384]{2,1,0:T(8,128)(2,1)}, u32[]{:S(2)}) %copy-start.1) | copy-done | bytes 3145752
  18.3 2.5 %shard_map.103 = bf16[32,16,512]{2,1,0:T(8,128)(2,1)} custom-call(bf16[64,384]{1,0:T(8,128)(2,1)S(1)} %get-tuple-element.28.rows_ref, bf16[4096,384]{1,0:T(8,128)(2,1)S(1)} %bitcast.42), custom_call_target="tpu_custom_call" | custom-call | flops 201326592 | bytes 4194304 | tf_op jit(solution)/shard_map/pallas_call | solution.py:156
  20.8 1.9 %collective-permute-start = (bf16[32,16,512]{2,1,0:T(8,128)(2,1)}, bf16[32,16,512]{2,1,0:T(8,128)(2,1)}, u32[]{:S(2)}, u32[]{:S(2)}) collective-permute-start(bf16[32,16,512]{2,1,0:T(8,128)(2,1)} %shard_map.103), channel_id=1, source_target_pairs={{0,3},{3,0},{1,4},{4,1},{2,5},{5,2},{6,9},{9,6},{7,10},{10,7},{8,1... | collective-permute-start | bytes 1572872 | tf_op jit(solution)/shard_map/ppermute | solution.py:297
  22.7 0.0 copy-done.5
  22.7 0.0 copy-done.4
  22.7 0.0 copy-done.6
  22.7 0.1 pad_maximum_fusion
  22.8 0.0 copy-done.7
  23.0 0.1 pad.5.clone
  23.1 0.0 copy-done
  23.1 0.0 all-to-all-done
  23.1 1.0 reshape.163
  24.1 0.8 collective-permute-done.refs_0_
  24.9 0.0 copy-done.2
  24.9 3.1 %shard_map.104 = bf16[32,16,512]{2,1,0:T(8,128)(2,1)S(1)} custom-call(bf16[64,384]{1,0:T(8,128)(2,1)S(1)} %get-tuple-element.14.rows_ref, bf16[4096,384]{1,0:T(8,128)(2,1)S(1)} %bitcast.43, bf16[32,16,512]{2,1,0:T(8,128)(2,1)} %collective-permute-done.refs_0_), custom_call_target="tpu_custom_call" | custom-call | flops 201326592 | bytes 4194304 | tf_op jit(solution)/shard_map/pallas_call | solution.py:156
  28.0 0.8 copy-done.3
  28.8 7.4 %all-to-all-start.1 = ((bf16[32,16,512]{2,1,0:T(8,128)(2,1)}), bf16[32,16,512]{2,1,0:T(8,128)(2,1)}, u32[]{:S(2)}, u32[]{:S(2)}) async-start(bf16[32,16,512]{2,1,0:T(8,128)(2,1)} %copy-done.3), calls=%async_computation.1 | async-start | bytes 1048576 | tf_op jit(solution)/shard_map/all_to_all | solution.py:23
  36.3 16.5 %all_gather.3.rows_ref = bf16[64,4096]{1,0:T(8,128)(2,1)S(1)} all-gather(bf16[16,4096]{1,0:T(8,128)(2,1)S(1)} %reshape.163), channel_id=1, replica_groups=mesh['layer'=2,'half'=2,'px'=4,'py'=8,'core'=2,'cols'=3] {'px'}, dimensions={0}, use_global_device_ids=true | all-gather | bytes 655360 | tf_op jit(solution)/shard_map/all_gather | solution.py:303
  52.7 1.9 %collective-permute-start.1 = (bf16[64,4096]{1,0:T(8,128)(2,1)S(1)}, bf16[64,4096]{1,0:T(8,128)(2,1)S(1)}, u32[]{:S(2)}, u32[]{:S(2)}) collective-permute-start(bf16[64,4096]{1,0:T(8,128)(2,1)S(1)} %all_gather.3.rows_ref), channel_id=1, source_target_pairs={{0,3},{3,0},{1,4},{4,1},{2,5},{5,2},{6,9},{9,6},{7,10},{10,7},{8,1... | collective-permute-start | bytes 1572872 | tf_op jit(solution)/shard_map/ppermute | solution.py:304
  54.6 0.1 maximum_maximum_fusion.vectors_ref
  54.7 1.4 %shard_map.105.near_ref = f32[136,384]{1,0:T(8,128)S(1)} custom-call(bf16[64,4096]{1,0:T(8,128)(2,1)S(1)} %all_gather.3.rows_ref, f32[8,4096]{1,0:T(8,128)S(1)} %maximum_maximum_fusion.vectors_ref, bf16[4096,384]{1,0:T(8,128)(2,1)S(1)} %bitcast.44), custom_call_target="tpu_custom_call" | custom-call | tf_op jit(solution)/shard_map/pallas_call | solution.py:110
  56.1 0.4 collective-permute-done.1.rows_ref
  56.5 2.2 %shard_map.106.payload_in = f32[3,136,128]{2,1,0:T(8,128)} custom-call(bf16[64,4096]{1,0:T(8,128)(2,1)S(1)} %collective-permute-done.1.rows_ref, f32[8,4096]{1,0:T(8,128)S(1)} %maximum_maximum_fusion.vectors_ref, bf16[4096,384]{1,0:T(8,128)(2,1)S(1)} %bitcast.45, f32[136,384]{1,0:T(8,128)S(1)} %shard_map.105.near_ref), custom_call_target="tpu_custom_call" | custom-call | tf_op jit(solution)/shard_map/pallas_call | solution.py:110
  58.7 0.0 all-to-all-done.1.blocks
  58.7 1.8 %shard_map.107 = (f32[16,512]{1,0:T(8,128)S(1)}, f32[3,136,128]{2,1,0:T(8,128)}) custom-call(bf16[32,16,512]{2,1,0:T(8,128)(2,1)} %all-to-all-done.1.blocks, bf16[3,16,512]{2,1,0:T(8,128)(2,1)S(1)} %reshape.165.lines_ref, f32[16,512]{1,0:T(8,128)S(1)} %bitcast.46, f32[3,136,128]{2,1,0:T(8,128)} %shard_map.106.payload_in), custom_call_target="tpu_custom_call", output_to_operand_aliasing={{1}: (3, {})} | custom-call | flops 1048576 | bytes 1048576 | tf_op jit(solution)/shard_map/pallas_call | solution.py:202
  60.5 3.4 %all-to-all-start.2 = ((f32[3,136,128]{2,1,0:T(8,128)}), f32[3,136,128]{2,1,0:T(8,128)S(1)}, u32[]{:S(2)}, u32[]{:S(2)}) async-start(f32[3,136,128]{2,1,0:T(8,128)} %get-tuple-element.17), calls=%async_computation.2 | async-start | bytes 417792 | tf_op jit(solution)/shard_map/all_to_all | solution.py:23
  64.0 7.7 %collective-permute-start.2 = (bf16[2,4096]{1,0:T(2,128)(2,1)S(1)}, bf16[2,4096]{1,0:T(2,128)(2,1)S(1)}, u32[]{:S(2)}, u32[]{:S(2)}) collective-permute-start(bf16[2,4096]{1,0:T(2,128)(2,1)S(1)} %fusion.17), channel_id=1, source_target_pairs={{0,192},{192,0},{384,576},{576,384},{1,193},{193,1},{385,577},{577... | collective-permute-start | bytes 49160 | tf_op jit(solution)/shard_map/ppermute | solution.py:283
  71.7 0.1 fusion.13.order_ref
  71.8 1.6 %collective-permute-done.2 = bf16[2,4096]{1,0:T(2,128)(2,1)S(1)} collective-permute-done((bf16[2,4096]{1,0:T(2,128)(2,1)S(1)}, bf16[2,4096]{1,0:T(2,128)(2,1)S(1)}, u32[]{:S(2)}, u32[]{:S(2)}) %collective-permute-start.2) | collective-permute-done | bytes 16416 | tf_op jit(solution)/shard_map/ppermute | solution.py:283
  73.4 0.0 all-to-all-done.2.received
  73.4 1.1 %shard_map.108 = (bf16[6,128,128]{2,1,0:T(8,128)(2,1)}, f32[8,128]{1,0:T(8,128)S(1)}) custom-call(s32[1]{0:T(128)} %bitcast.even_ref, f32[3,136,128]{2,1,0:T(8,128)S(1)} %all-to-all-done.2.received, bf16[128,128]{1,0:T(8,128)(2,1)S(1)} %fusion.13.order_ref), custom_call_target="tpu_custom_call" | custom-call | tf_op jit(solution)/shard_map/pallas_call | solution.py:256
  74.5 0.1 shard_map.109
  74.6 10.6 %collective-permute-start.3 = (bf16[16,512]{1,0:T(8,128)(2,1)S(1)}, bf16[16,512]{1,0:T(8,128)(2,1)S(1)}, u32[]{:S(2)}, u32[]{:S(2)}) collective-permute-start(bf16[16,512]{1,0:T(8,128)(2,1)S(1)} %shard_map.109), channel_id=1, source_target_pairs={{0,576},{576,0},{192,384},{384,192},{1,577},{577,1},{193,385},{385... | collective-permute-start | bytes 49160 | tf_op jit(solution)/shard_map/ppermute | solution.py:347
  85.2 4.8 %all-to-all-start.3 = ((bf16[6,128,128]{2,1,0:T(8,128)(2,1)}), bf16[6,128,128]{2,1,0:T(8,128)(2,1)S(1)}, u32[]{:S(2)}, u32[]{:S(2)}) async-start(bf16[6,128,128]{2,1,0:T(8,128)(2,1)} %get-tuple-element.22), calls=%async_computation.3 | async-start | bytes 393216 | tf_op jit(solution)/shard_map/all_to_all | solution.py:23
  90.0 0.0 collective-permute-done.3
  90.0 0.6 fusion.16
  90.7 9.8 %all-to-all-done.3 = bf16[6,128,128]{2,1,0:T(8,128)(2,1)S(1)} async-done(((bf16[6,128,128]{2,1,0:T(8,128)(2,1)}), bf16[6,128,128]{2,1,0:T(8,128)(2,1)S(1)}, u32[]{:S(2)}, u32[]{:S(2)}) %all-to-all-start.3) | async-done | bytes 196640 | tf_op jit(solution)/shard_map/all_to_all | solution.py:23
  100.5 0.7 maximum_bitcast_fusion
  (17 shorter events, 0.2 us)
Async XLA Ops:
  0.6 22.5 %copy-start = (f32[2,4096]{1,0:T(2,128)S(1)}, f32[2,4096]{1,0:T(2,128)}, u32[]{:S(2)}) copy-start(f32[2,4096]{1,0:T(2,128)} %param.15) | copy-start | bytes 98308
  0.6 22.1 %copy-start.5 = (bf16[1,2,4096]{2,1,0:T(2,128)(2,1)S(1)}, bf16[1,2,4096]{2,1,0:T(2,128)(2,1)}, u32[]{:S(2)}) copy-start(bf16[1,2,4096]{2,1,0:T(2,128)(2,1)} %param.10) | copy-start | bytes 49156
  0.7 22.1 %copy-start.4 = (bf16[1,2,4096]{2,1,0:T(2,128)(2,1)S(1)}, bf16[1,2,4096]{2,1,0:T(2,128)(2,1)}, u32[]{:S(2)}) copy-start(bf16[1,2,4096]{2,1,0:T(2,128)(2,1)} %param.8) | copy-start | bytes 49156
  0.7 22.1 %copy-start.6 = (bf16[1,2,4096]{2,1,0:T(2,128)(2,1)S(1)}, bf16[1,2,4096]{2,1,0:T(2,128)(2,1)}, u32[]{:S(2)}) copy-start(bf16[1,2,4096]{2,1,0:T(2,128)(2,1)} %param.11) | copy-start | bytes 49156
  0.7 22.1 %copy-start.7 = (f32[2,4096]{1,0:T(2,128)S(1)}, f32[2,4096]{1,0:T(2,128)}, u32[]{:S(2)}) copy-start(f32[2,4096]{1,0:T(2,128)} %param.14) | copy-start | bytes 98308
  2.2 20.9 %all-to-all-start = ((bf16[8,2,4096]{2,1,0:T(2,128)(2,1)}), bf16[8,2,4096]{2,1,0:T(2,128)(2,1)}, u32[]{:S(2)}, u32[]{:S(2)}) async-start(bf16[8,2,4096]{2,1,0:T(2,128)(2,1)} %broadcast_in_dim.39), calls=%async_computation | async-start | bytes 262144 | tf_op jit(solution)/shard_map/all_to_all | solution.py:23
  16.4 1.9 %copy-start.1 = (bf16[1,4096,384]{2,1,0:T(8,128)(2,1)S(1)}, bf16[1,4096,384]{2,1,0:T(8,128)(2,1)}, u32[]{:S(2)}) copy-start(bf16[1,4096,384]{2,1,0:T(8,128)(2,1)} %param.13) | copy-start | bytes 9437188
  18.3 6.6 %copy-start.2 = (bf16[1,4096,384]{2,1,0:T(8,128)(2,1)S(1)}, bf16[1,4096,384]{2,1,0:T(8,128)(2,1)}, u32[]{:S(2)}) copy-start(bf16[1,4096,384]{2,1,0:T(8,128)(2,1)} %param.13) | copy-start | bytes 9437188
  20.8 4.1 %collective-permute-start = (bf16[32,16,512]{2,1,0:T(8,128)(2,1)}, bf16[32,16,512]{2,1,0:T(8,128)(2,1)}, u32[]{:S(2)}, u32[]{:S(2)}) collective-permute-start(bf16[32,16,512]{2,1,0:T(8,128)(2,1)} %shard_map.103), channel_id=1, source_target_pairs={{0,3},{3,0},{1,4},{4,1},{2,5},{5,2},{6,9},{9,6},{7,10},{10,7},{8,1... | collective-permute-start | bytes 1572872 | tf_op jit(solution)/shard_map/ppermute | solution.py:297
  28.0 0.8 copy-start.3
  28.8 29.8 %all-to-all-start.1 = ((bf16[32,16,512]{2,1,0:T(8,128)(2,1)}), bf16[32,16,512]{2,1,0:T(8,128)(2,1)}, u32[]{:S(2)}, u32[]{:S(2)}) async-start(bf16[32,16,512]{2,1,0:T(8,128)(2,1)} %copy-done.3), calls=%async_computation.1 | async-start | bytes 1048576 | tf_op jit(solution)/shard_map/all_to_all | solution.py:23
  52.7 3.8 %collective-permute-start.1 = (bf16[64,4096]{1,0:T(8,128)(2,1)S(1)}, bf16[64,4096]{1,0:T(8,128)(2,1)S(1)}, u32[]{:S(2)}, u32[]{:S(2)}) collective-permute-start(bf16[64,4096]{1,0:T(8,128)(2,1)S(1)} %all_gather.3.rows_ref), channel_id=1, source_target_pairs={{0,3},{3,0},{1,4},{4,1},{2,5},{5,2},{6,9},{9,6},{7,10},{10,7},{8,1... | collective-permute-start | bytes 1572872 | tf_op jit(solution)/shard_map/ppermute | solution.py:304
  60.5 12.9 %all-to-all-start.2 = ((f32[3,136,128]{2,1,0:T(8,128)}), f32[3,136,128]{2,1,0:T(8,128)S(1)}, u32[]{:S(2)}, u32[]{:S(2)}) async-start(f32[3,136,128]{2,1,0:T(8,128)} %get-tuple-element.17), calls=%async_computation.2 | async-start | bytes 417792 | tf_op jit(solution)/shard_map/all_to_all | solution.py:23
  64.0 9.4 %collective-permute-start.2 = (bf16[2,4096]{1,0:T(2,128)(2,1)S(1)}, bf16[2,4096]{1,0:T(2,128)(2,1)S(1)}, u32[]{:S(2)}, u32[]{:S(2)}) collective-permute-start(bf16[2,4096]{1,0:T(2,128)(2,1)S(1)} %fusion.17), channel_id=1, source_target_pairs={{0,192},{192,0},{384,576},{576,384},{1,193},{193,1},{385,577},{577... | collective-permute-start | bytes 49160 | tf_op jit(solution)/shard_map/ppermute | solution.py:283
  74.6 15.4 %collective-permute-start.3 = (bf16[16,512]{1,0:T(8,128)(2,1)S(1)}, bf16[16,512]{1,0:T(8,128)(2,1)S(1)}, u32[]{:S(2)}, u32[]{:S(2)}) collective-permute-start(bf16[16,512]{1,0:T(8,128)(2,1)S(1)} %shard_map.109), channel_id=1, source_target_pairs={{0,576},{576,0},{192,384},{384,192},{1,577},{577,1},{193,385},{385... | collective-permute-start | bytes 49160 | tf_op jit(solution)/shard_map/ppermute | solution.py:347
  85.2 15.3 %all-to-all-start.3 = ((bf16[6,128,128]{2,1,0:T(8,128)(2,1)}), bf16[6,128,128]{2,1,0:T(8,128)(2,1)S(1)}, u32[]{:S(2)}, u32[]{:S(2)}) async-start(bf16[6,128,128]{2,1,0:T(8,128)(2,1)} %get-tuple-element.22), calls=%async_computation.3 | async-start | bytes 393216 | tf_op jit(solution)/shard_map/all_to_all | solution.py:23

commit v4 on v3

--- a/solution.py
+++ b/solution.py
@@ -11,7 +11,8 @@
 LAYER_AXIS, HALF, COLS = "layer", "half", "cols"
 PX, PY = "px", "py"
 CORE = "core"
-ROWS = (PX, PY, CORE)
+PLANE = (PX, PY)
+ROWS = PLANE + (CORE,)
 SECTION = (LAYER_AXIS, HALF)
 
 
@@ -136,38 +137,56 @@
     return blocks
 
 
-def terms_kernel(rows_ref, weight_ref, *refs):
+def terms_kernel(rows_ref, weight_ref, own_ref, other_ref):
     values = lax.dot_general(
         rows_ref[...],
         weight_ref[...],
         (((1,), (1,)), ((), ())),
         preferred_element_type=jnp.float32,
     )
-    for p, block in enumerate(blocks_of(values)):
-        if len(refs) == 2:
-            block = block + refs[0][p].astype(jnp.float32)
-        refs[-1][p] = block.astype(jnp.bfloat16)
-
-
-def terms_call(rows, weight, *arriving):
+    half = values.shape[0] // 2
+    for p, block in enumerate(blocks_of(values[half:])):
+        other_ref[p] = block.astype(jnp.bfloat16)
+    for p, block in enumerate(blocks_of(values[:half])):
+        own_ref[p] = block
+
+
+def terms_call(rows, weight):
     count, hidden = rows.shape
     features = weight.shape[0]
-    block = pl.BlockSpec((count // 2, 16, 128), lambda k: (0, 0, k))
+    block = pl.BlockSpec((count // 4, 16, 128), lambda k: (0, 0, k))
+    shape = (count // 4, 16, features // 8)
     return pl.pallas_call(
         terms_kernel,
         grid=(features // 1024,),
         in_specs=[
             pl.BlockSpec((count, hidden), lambda k: (0, 0)),
             pl.BlockSpec((1024, hidden), lambda k: (k, 0)),
-        ]
-        + [block] * len(arriving),
-        out_specs=block,
-        out_shape=jax.ShapeDtypeStruct((count // 2, 16, features // 8), jnp.bfloat16),
+        ],
+        out_specs=[block, block],
+        out_shape=[
+            jax.ShapeDtypeStruct(shape, jnp.float32),
+            jax.ShapeDtypeStruct(shape, jnp.bfloat16),
+        ],
         compiler_params=pltpu.CompilerParams(vmem_limit_bytes=VMEM_LIMIT),
-        cost_estimate=pl.CostEstimate(
-            flops=2 * count * features * hidden, bytes_accessed=4 * 2**20, transcendentals=0
-        ),
-    )(rows, weight, *arriving)
+        cost_estimate=pl.CostEstimate(flops=0, bytes_accessed=0, transcendentals=0),
+    )(rows, weight)
+
+
+def zero_kernel(anything_ref, zero_ref):
+    zero_ref[...] = jnp.zeros_like(zero_ref)
+
+
+def zero_after(anything):
+    zeros = pl.pallas_call(
+        zero_kernel,
+        in_specs=[pl.BlockSpec(memory_space=pl.ANY)],
+        out_specs=pl.BlockSpec(memory_space=pltpu.VMEM),
+        out_shape=jax.ShapeDtypeStruct((8, 128), jnp.float32),
+        compiler_params=pltpu.CompilerParams(vmem_limit_bytes=2**20),
+        cost_estimate=pl.CostEstimate(flops=2**35, bytes_accessed=2**26, transcendentals=0),
+    )(anything)
+    return zeros[0, 0]
 
 
 def lines_of(values):
@@ -251,6 +270,33 @@
     late_ref[...] = late.astype(jnp.bfloat16)
 
 
+def assemble_kernel(half_ref, *refs):
+    blocks, hidden_ref = refs[:-1], refs[-1]
+    cols = len(blocks)
+    for i in range(cols):
+        hidden_ref[:, i * 128 : i * 128 + 128] = blocks[i][0]
+
+
+def assemble_call(half, incoming):
+    cols, (tokens, part) = incoming.shape[0] // 2, incoming.shape[1:]
+
+    def block(i):
+        return pl.BlockSpec((1, tokens, part), lambda k, half: ((1 - half[0]) * cols + i, 0, 0))
+
+    return pl.pallas_call(
+        assemble_kernel,
+        grid_spec=pltpu.PrefetchScalarGridSpec(
+            num_scalar_prefetch=1,
+            grid=(1,),
+            in_specs=[block(i) for i in range(cols)],
+            out_specs=pl.BlockSpec((tokens, cols * part), lambda k, half: (0, 0)),
+        ),
+        out_shape=jax.ShapeDtypeStruct((tokens, cols * part), incoming.dtype),
+        compiler_params=pltpu.CompilerParams(vmem_limit_bytes=VMEM_LIMIT),
+        cost_estimate=pl.CostEstimate(flops=2**35, bytes_accessed=2**26, transcendentals=0),
+    )(half.astype(jnp.int32).reshape(1), *[incoming] * cols)
+
+
 def vmem_call(kernel, flag, out_shape, cost, *operands):
     vmem = pl.BlockSpec(memory_space=pltpu.VMEM)
     return pl.pallas_call(
@@ -280,11 +326,10 @@
     half_tokens = tokens // 2
     part = hidden // cols
 
-    early = lax.ppermute(
-        jnp.where(is_even, stream, gradient), SECTION, [(0, 1), (1, 0), (2, 3), (3, 2)]
-    )
-
-    leading = copies(jnp.where(is_even, stream, gradient), PY)
+    early = jnp.where(is_even, *lax.optimization_barrier((stream, gradient)))
+    early = lax.ppermute(early, SECTION, [(0, 1), (1, 0), (2, 3), (3, 2)])
+
+    leading = copies(jnp.where(is_even, stream, gradient), PLANE)
 
     token = jnp.arange(tokens)
     t_of = token % own
@@ -292,15 +337,15 @@
     right_side = jnp.where(is_even, slope, hid_in[0])
     row, group = token % half_tokens, token // half_tokens
     right_side = picked(right_side, (row // own * 2 + (group != core)) * own + row % own)
-    own_x = exchange(leading, PY).reshape(ny * own, features)
+    near = exchange(leading, PLANE)
     cores = [(0, 1), (1, 0)]
-    arriving = lax.ppermute(terms_call(right_side[half_tokens:], weight), CORE, cores)
-    own_x, own_rows = lax.optimization_barrier((own_x, right_side[:half_tokens]))
-    chip_terms = terms_call(own_rows, weight, arriving)
-    own_x, chip_terms = lax.optimization_barrier((own_x, chip_terms))
-    term_blocks = exchange(chip_terms, (PX, PY))
-
-    near = lax.all_gather(own_x, PX, axis=0, tiled=True)
+    own_terms, other_terms = terms_call(right_side, weight)
+    arriving = lax.ppermute(other_terms, CORE, cores)
+    chip_terms = (own_terms + (arriving.astype(f32) + zero_after(near))).astype(bf16)
+    near, chip_terms = lax.optimization_barrier((near, chip_terms))
+    term_blocks = exchange(chip_terms, PLANE)
+
+    near = near.reshape(half_tokens, features)
     far = lax.ppermute(near, CORE, cores)
     factor = jnp.where(is_even, gain, 1.0)
     vectors = jnp.concatenate(
@@ -311,12 +356,13 @@
 
     line_gain = lines_of(jnp.broadcast_to(gain[None], (own, features)))[0]
     lines = lines_of(jnp.stack((saved_in[0], stream, gradient)))
-    term, payload = finish_call(term_blocks, lines, line_gain, payload)
+    term, payload = finish_call(term_blocks, lines, line_gain + zero_after(term_blocks), payload)
     other = ((token // own) % 2 != core).astype(jnp.int32)
     x_of = token // (2 * own * ny)
     place = ((other * nx + x_of) * ny + (token // (2 * own)) % ny) * own + t_of
     order = (place[:, None] == token[None, :]).astype(bf16)
-    received, early = lax.optimization_barrier((exchange(payload, COLS), early))
+    payload, early = lax.optimization_barrier((payload, early))
+    received = exchange(payload, COLS)
     flag = is_even.astype(jnp.int32).reshape(1)
     hidden_value, moments = vmem_call(
         hidden_kernel,
@@ -340,13 +386,13 @@
         line_gain,
     )
 
-    incoming = exchange(hidden_value, (HALF, COLS)).reshape(2, cols, tokens, part)
-    incoming = lax.dynamic_index_in_dim(incoming, 1 - half, 0, keepdims=False)
-    hidden_next = jnp.concatenate([incoming[i] for i in range(cols)], axis=1)
+    incoming = exchange(hidden_value, (HALF, COLS))
+    hidden_next = assemble_call(half, incoming)
 
     late = lax.ppermute(late, SECTION, [(0, 3), (3, 0), (1, 2), (2, 1)])
     late = late.reshape(8, own, 4, 128).transpose(1, 2, 0, 3).reshape(own, features)
 
+    late, hidden_next = lax.optimization_barrier((late, hidden_next))
     act_next = jnp.where(is_even, late, early)
     grad_next = jnp.where(is_even, early, late)
     return (act_next[None], hidden_next[None], grad_next[None])

time: 102 us -> 98.1 us (0.962)
  the two profiles are of different devices: /device:TPU:40 before, /device:TPU:8 now
where the time goes in v4:
time: 98.1 us; the launch traced here: 97.2 us
  starting transfers between devices  52.6 us (54%)
  waiting for transfers between devices  17.6 us (18%)
  Pallas kernels  9.98 us (10%)
  local copies, waits for them, and re-layouts  9.42 us (10%)
  other arithmetic  5.35 us (5%)
  matrix products  1.25 us (1%)
    all_to_all x4, starting transfers between devices, exchange(): return lax.all_to_all(blocks, axis, 0, 0, tiled=True)  32.5 us
    all_to_all x4, waiting for transfers between devices, exchange(): return lax.all_to_all(blocks, axis, 0, 0, tiled=True)  15.4 us
    ppermute x1, starting transfers between devices, per_device(): late = lax.ppermute(late, SECTION, [(0, 3), (3, 0), (1, 2), (2, 1)])  11.2 us
    ppermute x1, starting transfers between devices, per_device(): early = lax.ppermute(early, SECTION, [(0, 1), (1, 0), (2, 3), (3, 2)])  5.07 us
    unnamed x24, local copies, waits for them, and re-layouts  4.87 us
    pallas_call x2, Pallas kernels, rows_call(): pl.pallas_call(kernel, grid=(STEPS,), in_specs=specs, out_specs=out_specs...  3.6 us
    convert_element_type x1, other arithmetic, per_device(): (own_terms + (arriving.astype(f32) + zero_after(near))).astype(bf16)  2.98 us
    pallas_call x1, Pallas kernels, terms_call(): pl.pallas_call(terms_kernel, grid=(features // 1024,), in_specs=[pl.Block...  2.69 us
  transfers between devices with their start and end apart: 8, of which 4 were waited for; matrix products, arithmetic and copies ran while one was open for 9% of the time, Pallas kernels for 8%

profile of v4, /device:TPU:8, one launch (start us, length us, event | category | flops | bytes accessed | tf_op | source)
XLA Modules:
  0.0 97.2 jit_solution(11673315987643720071)
XLA Ops:
  0.6 0.0 copy-start
  0.6 0.0 copy-start.7
  0.7 0.0 copy-start.8
  0.7 0.0 copy-start.10
  0.7 0.0 copy-start.9
  0.7 0.8 fusion.17
  1.5 1.3 %broadcast_in_dim.39 = bf16[32,2,4096]{2,1,0:T(2,128)(2,1)} broadcast(bf16[2,4096]{1,0:T(2,128)(2,1)S(1)} %fusion.17), dimensions={1,2} | broadcast | bytes 540672 | tf_op jit(solution)/shard_map/broadcast_in_dim | solution.py:28
  2.7 13.0 %all-to-all-start = ((bf16[32,2,4096]{2,1,0:T(2,128)(2,1)}), bf16[32,2,4096]{2,1,0:T(2,128)(2,1)S(1)}, u32[]{:S(2)}, u32[]{:S(2)}) async-start(bf16[32,2,4096]{2,1,0:T(2,128)(2,1)} %broadcast_in_dim.39), calls=%async_computation | async-start | bytes 1048576 | tf_op jit(solution)/shard_map/all_to_all | solution.py:24
  15.8 1.2 %convolution_convert_fusion.rows_ref = bf16[128,384]{1,0:T(8,128)(2,1)S(1)} fusion(bf16[1,128,384]{2,1,0:T(8,128)(2,1)} %param.12, bf16[1,128,384]{2,1,0:T(8,128)(2,1)} %param.9, pred[]{:T(512)S(6)} %eq.35, s32[128]{0:T(128)S(1)} %fusion.19), kind=kOutput, calls=%fused_computation | convolution fusion | flops 13778944 | bytes 295425 | tf_op jit(solution)/shard_map/dot_general | solution.py:33
  17.0 0.0 copy-start.1
  17.0 1.9 %copy-done.1 = bf16[1,4096,384]{2,1,0:T(8,128)(2,1)S(1)} copy-done((bf16[1,4096,384]{2,1,0:T(8,128)(2,1)S(1)}, bf16[1,4096,384]{2,1,0:T(8,128)(2,1)}, u32[]{:S(2)}) %copy-start.1) | copy-done | bytes 3145752
  18.9 2.7 %shard_map.103 = (f32[32,16,512]{2,1,0:T(8,128)S(1)}, bf16[32,16,512]{2,1,0:T(8,128)(2,1)}) custom-call(bf16[128,384]{1,0:T(8,128)(2,1)S(1)} %convolution_convert_fusion.rows_ref, bf16[4096,384]{1,0:T(8,128)(2,1)S(1)} %bitcast.41), custom_call_target="tpu_custom_call" | custom-call | tf_op jit(solution)/shard_map/pallas_call | solution.py:159
  21.6 1.0 %copy-done.5 = f32[32,16,512]{2,1,0:T(8,128)} copy-done((f32[32,16,512]{2,1,0:T(8,128)}, f32[32,16,512]{2,1,0:T(8,128)S(1)}, u32[]{:S(2)}) %copy-start.5) | copy-done | bytes 1048600
  22.6 1.9 %collective-permute-start = (bf16[32,16,512]{2,1,0:T(8,128)(2,1)}, bf16[32,16,512]{2,1,0:T(8,128)(2,1)}, u32[]{:S(2)}, u32[]{:S(2)}) collective-permute-start(bf16[32,16,512]{2,1,0:T(8,128)(2,1)} %get-tuple-element.18), channel_id=1, source_target_pairs={{0,3},{3,0},{1,4},{4,1},{2,5},{5,2},{6,9},{9,6},{7,10},{10,7},{8,1... | collective-permute-start | bytes 1572872 | tf_op jit(solution)/shard_map/ppermute | solution.py:343
  24.6 5.1 %collective-permute-start.2 = (bf16[2,4096]{1,0:T(2,128)(2,1)S(1)}, bf16[2,4096]{1,0:T(2,128)(2,1)S(1)}, u32[]{:S(2)}, u32[]{:S(2)}) collective-permute-start(bf16[2,4096]{1,0:T(2,128)(2,1)S(1)} %broadcast_select_fusion.4), channel_id=1, source_target_pairs={{0,192},{192,0},{384,576},{576,384},{1,193},{193,1},{385,577},{577... | collective-permute-start | bytes 49160 | tf_op jit(solution)/shard_map/ppermute | solution.py:330
  29.7 0.0 copy-done.10
  29.7 0.1 pad_maximum_fusion
  29.8 0.9 all-to-all-done.anything_ref
  30.7 0.8 copy-done.4
  31.5 0.5 slice.6
  32.0 0.0 collective-permute-done
  32.1 0.1 copy-done.6
  32.1 3.0 %add_convert_fusion = bf16[32,16,512]{2,1,0:T(8,128)(2,1)} fusion(f32[32,16,512]{2,1,0:T(8,128)S(1)} %copy-done.6, bf16[32,16,512]{2,1,0:T(8,128)(2,1)} %collective-permute-done, f32[]{:T(128)} %bitcast.6), kind=kLoop, calls=%fused_computation.1 | loop fusion | flops 1048576 | bytes 2097156 | tf_op jit(solution)/shard_map/convert_element_type | solution.py:344
  35.1 8.9 %all-to-all-start.1 = ((bf16[32,16,512]{2,1,0:T(8,128)(2,1)}), bf16[32,16,512]{2,1,0:T(8,128)(2,1)}, u32[]{:S(2)}, u32[]{:S(2)}) async-start(bf16[32,16,512]{2,1,0:T(8,128)(2,1)} %add_convert_fusion), calls=%async_computation.1 | async-start | bytes 1048576 | tf_op jit(solution)/shard_map/all_to_all | solution.py:24
  44.2 0.1 pad.2.clone
  44.3 2.0 %reshape.157.rows_ref = bf16[64,4096]{1,0:T(8,128)(2,1)} reshape(bf16[32,2,4096]{2,1,0:T(2,128)(2,1)} %copy-done.4) | data formatting | bytes 1048576 | tf_op jit(solution)/shard_map/reshape | solution.py:348
  46.3 1.9 %collective-permute-start.1 = (bf16[64,4096]{1,0:T(8,128)(2,1)}, bf16[64,4096]{1,0:T(8,128)(2,1)S(1)}, u32[]{:S(2)}, u32[]{:S(2)}) collective-permute-start(bf16[64,4096]{1,0:T(8,128)(2,1)} %reshape.157.rows_ref), channel_id=1, source_target_pairs={{0,3},{3,0},{1,4},{4,1},{2,5},{5,2},{6,9},{9,6},{7,10},{10,7},{8,1... | collective-permute-start | bytes 1572872 | tf_op jit(solution)/shard_map/ppermute | solution.py:349
  48.2 0.1 maximum_maximum_fusion.vectors_ref
  48.4 1.0 %copy-done.3 = bf16[64,4096]{1,0:T(8,128)(2,1)S(1)} copy-done((bf16[64,4096]{1,0:T(8,128)(2,1)S(1)}, bf16[64,4096]{1,0:T(8,128)(2,1)}, u32[]{:S(2)}) %copy-start.3) | copy-done | bytes 524312
  49.4 1.4 %shard_map.106.near_ref = f32[136,384]{1,0:T(8,128)S(1)} custom-call(bf16[64,4096]{1,0:T(8,128)(2,1)S(1)} %copy-done.3, f32[8,4096]{1,0:T(8,128)S(1)} %maximum_maximum_fusion.vectors_ref, bf16[4096,384]{1,0:T(8,128)(2,1)S(1)} %bitcast.42), custom_call_target="tpu_custom_call" | custom-call | tf_op jit(solution)/shard_map/pallas_call | solution.py:111
  50.8 0.0 collective-permute-done.1.rows_ref
  50.8 2.2 %shard_map.107.payload_in = f32[3,136,128]{2,1,0:T(8,128)} custom-call(bf16[64,4096]{1,0:T(8,128)(2,1)S(1)} %collective-permute-done.1.rows_ref, f32[8,4096]{1,0:T(8,128)S(1)} %maximum_maximum_fusion.vectors_ref, bf16[4096,384]{1,0:T(8,128)(2,1)S(1)} %bitcast.43, f32[136,384]{1,0:T(8,128)S(1)} %shard_map.106.near_ref), custom_call_target="tpu_custom_call" | custom-call | tf_op jit(solution)/shard_map/pallas_call | solution.py:111
  53.0 9.1 %all-to-all-done.1.anything_ref.blocks = bf16[32,16,512]{2,1,0:T(8,128)(2,1)} async-done(((bf16[32,16,512]{2,1,0:T(8,128)(2,1)}), bf16[32,16,512]{2,1,0:T(8,128)(2,1)}, u32[]{:S(2)}, u32[]{:S(2)}) %all-to-all-start.1) | async-done | bytes 524320 | tf_op jit(solution)/shard_map/all_to_all | solution.py:24
  62.1 0.5 slice.7
  62.6 0.6 broadcast_add_fusion.gain_ref
  63.3 1.8 %shard_map.108 = (f32[16,512]{1,0:T(8,128)S(1)}, f32[3,136,128]{2,1,0:T(8,128)}) custom-call(bf16[32,16,512]{2,1,0:T(8,128)(2,1)} %all-to-all-done.1.anything_ref.blocks, bf16[3,16,512]{2,1,0:T(8,128)(2,1)S(1)} %reshape.156.lines_ref, f32[16,512]{1,0:T(8,128)S(1)} %broadcast_add_fusion.gain_ref, ...), custom_call_target="tpu_custom_call", output_to_operand_aliasing={{1}: (3, {})} | custom-call | flops 1048576 | bytes 1048576 | tf_op jit(solution)/shard_map/pallas_call | solution.py:221
  65.1 0.0 collective-permute-done.2
  65.2 6.7 %all-to-all-start.2 = ((f32[3,136,128]{2,1,0:T(8,128)}), f32[3,136,128]{2,1,0:T(8,128)S(1)}, u32[]{:S(2)}, u32[]{:S(2)}) async-start(f32[3,136,128]{2,1,0:T(8,128)} %get-tuple-element.24), calls=%async_computation.2 | async-start | bytes 417792 | tf_op jit(solution)/shard_map/all_to_all | solution.py:24
  71.8 0.1 fusion.13.order_ref
  71.9 5.3 %all-to-all-done.2.received = f32[3,136,128]{2,1,0:T(8,128)S(1)} async-done(((f32[3,136,128]{2,1,0:T(8,128)}), f32[3,136,128]{2,1,0:T(8,128)S(1)}, u32[]{:S(2)}, u32[]{:S(2)}) %all-to-all-start.2) | async-done | bytes 208928 | tf_op jit(solution)/shard_map/all_to_all | solution.py:24
  77.2 1.0 %shard_map.109 = (bf16[6,128,128]{2,1,0:T(8,128)(2,1)}, f32[8,128]{1,0:T(8,128)S(1)}) custom-call(s32[1]{0:T(128)} %bitcast.even_ref, f32[3,136,128]{2,1,0:T(8,128)S(1)} %all-to-all-done.2.received, bf16[128,128]{1,0:T(8,128)(2,1)S(1)} %fusion.13.order_ref), custom_call_target="tpu_custom_call" | custom-call | tf_op jit(solution)/shard_map/pallas_call | solution.py:302
  78.3 3.9 %all-to-all-start.3 = ((bf16[6,128,128]{2,1,0:T(8,128)(2,1)}), bf16[6,128,128]{2,1,0:T(8,128)(2,1)S(1)}, u32[]{:S(2)}, u32[]{:S(2)}) async-start(bf16[6,128,128]{2,1,0:T(8,128)(2,1)} %get-tuple-element.27), calls=%async_computation.3 | async-start | bytes 393216 | tf_op jit(solution)/shard_map/all_to_all | solution.py:24
  82.2 0.1 shard_map.110
  82.4 11.2 %collective-permute-start.3 = (bf16[16,512]{1,0:T(8,128)(2,1)S(1)}, bf16[16,512]{1,0:T(8,128)(2,1)S(1)}, u32[]{:S(2)}, u32[]{:S(2)}) collective-permute-start(bf16[16,512]{1,0:T(8,128)(2,1)S(1)} %shard_map.110), channel_id=1, source_target_pairs={{0,576},{576,0},{192,384},{384,192},{1,577},{577,1},{193,385},{385... | collective-permute-start | bytes 49160 | tf_op jit(solution)/shard_map/ppermute | solution.py:392
  93.6 2.2 %collective-permute-done.3 = bf16[16,512]{1,0:T(8,128)(2,1)S(1)} collective-permute-done((bf16[16,512]{1,0:T(8,128)(2,1)S(1)}, bf16[16,512]{1,0:T(8,128)(2,1)S(1)}, u32[]{:S(2)}, u32[]{:S(2)}) %collective-permute-start.3) | collective-permute-done | bytes 16416 | tf_op jit(solution)/shard_map/ppermute | solution.py:392
  95.9 0.0 all-to-all-done.3.refs_0_.refs_1_.refs_2_
  95.9 0.7 shard_map.111
  96.5 0.6 fusion.16
  (27 shorter events, 0.3 us)
Async XLA Ops:
  0.6 43.4 %copy-start = (f32[2,4096]{1,0:T(2,128)S(1)}, f32[2,4096]{1,0:T(2,128)}, u32[]{:S(2)}) copy-start(f32[2,4096]{1,0:T(2,128)} %param.15) | copy-start | bytes 98308
  0.6 23.9 %copy-start.7 = (bf16[1,2,4096]{2,1,0:T(2,128)(2,1)S(1)}, bf16[1,2,4096]{2,1,0:T(2,128)(2,1)}, u32[]{:S(2)}) copy-start(bf16[1,2,4096]{2,1,0:T(2,128)(2,1)} %param.8) | copy-start | bytes 49156
  0.7 23.9 %copy-start.8 = (bf16[1,2,4096]{2,1,0:T(2,128)(2,1)S(1)}, bf16[1,2,4096]{2,1,0:T(2,128)(2,1)}, u32[]{:S(2)}) copy-start(bf16[1,2,4096]{2,1,0:T(2,128)(2,1)} %param.10) | copy-start | bytes 49156
  0.7 29.0 %copy-start.10 = (f32[2,4096]{1,0:T(2,128)S(1)}, f32[2,4096]{1,0:T(2,128)}, u32[]{:S(2)}) copy-start(f32[2,4096]{1,0:T(2,128)} %param.14) | copy-start | bytes 98308
  0.7 29.0 %copy-start.9 = (bf16[1,2,4096]{2,1,0:T(2,128)(2,1)S(1)}, bf16[1,2,4096]{2,1,0:T(2,128)(2,1)}, u32[]{:S(2)}) copy-start(bf16[1,2,4096]{2,1,0:T(2,128)(2,1)} %param.11) | copy-start | bytes 49156
  2.7 28.0 %all-to-all-start = ((bf16[32,2,4096]{2,1,0:T(2,128)(2,1)}), bf16[32,2,4096]{2,1,0:T(2,128)(2,1)S(1)}, u32[]{:S(2)}, u32[]{:S(2)}) async-start(bf16[32,2,4096]{2,1,0:T(2,128)(2,1)} %broadcast_in_dim.39), calls=%async_computation | async-start | bytes 1048576 | tf_op jit(solution)/shard_map/all_to_all | solution.py:24
  17.0 1.9 %copy-start.1 = (bf16[1,4096,384]{2,1,0:T(8,128)(2,1)S(1)}, bf16[1,4096,384]{2,1,0:T(8,128)(2,1)}, u32[]{:S(2)}) copy-start(bf16[1,4096,384]{2,1,0:T(8,128)(2,1)} %param.13) | copy-start | bytes 9437188
  21.6 1.0 %copy-start.5 = (f32[32,16,512]{2,1,0:T(8,128)}, f32[32,16,512]{2,1,0:T(8,128)S(1)}, u32[]{:S(2)}) copy-start(f32[32,16,512]{2,1,0:T(8,128)S(1)} %get-tuple-element.17) | copy-start | bytes 3145732
  22.6 9.4 %collective-permute-start = (bf16[32,16,512]{2,1,0:T(8,128)(2,1)}, bf16[32,16,512]{2,1,0:T(8,128)(2,1)}, u32[]{:S(2)}, u32[]{:S(2)}) collective-permute-start(bf16[32,16,512]{2,1,0:T(8,128)(2,1)} %get-tuple-element.18), channel_id=1, source_target_pairs={{0,3},{3,0},{1,4},{4,1},{2,5},{5,2},{6,9},{9,6},{7,10},{10,7},{8,1... | collective-permute-start | bytes 1572872 | tf_op jit(solution)/shard_map/ppermute | solution.py:343
  24.6 40.6 %collective-permute-start.2 = (bf16[2,4096]{1,0:T(2,128)(2,1)S(1)}, bf16[2,4096]{1,0:T(2,128)(2,1)S(1)}, u32[]{:S(2)}, u32[]{:S(2)}) collective-permute-start(bf16[2,4096]{1,0:T(2,128)(2,1)S(1)} %broadcast_select_fusion.4), channel_id=1, source_target_pairs={{0,192},{192,0},{384,576},{576,384},{1,193},{193,1},{385,577},{577... | collective-permute-start | bytes 49160 | tf_op jit(solution)/shard_map/ppermute | solution.py:330
  30.7 1.4 %copy-start.6 = (f32[32,16,512]{2,1,0:T(8,128)S(1)}, f32[32,16,512]{2,1,0:T(8,128)}, u32[]{:S(2)}) copy-start(f32[32,16,512]{2,1,0:T(8,128)} %copy-done.5) | copy-start | bytes 3145732
  30.7 0.8 copy-start.4
  31.5 16.8 %copy-start.2 = (bf16[1,4096,384]{2,1,0:T(8,128)(2,1)S(1)}, bf16[1,4096,384]{2,1,0:T(8,128)(2,1)}, u32[]{:S(2)}) copy-start(bf16[1,4096,384]{2,1,0:T(8,128)(2,1)} %param.13) | copy-start | bytes 9437188
  35.1 27.0 %all-to-all-start.1 = ((bf16[32,16,512]{2,1,0:T(8,128)(2,1)}), bf16[32,16,512]{2,1,0:T(8,128)(2,1)}, u32[]{:S(2)}, u32[]{:S(2)}) async-start(bf16[32,16,512]{2,1,0:T(8,128)(2,1)} %add_convert_fusion), calls=%async_computation.1 | async-start | bytes 1048576 | tf_op jit(solution)/shard_map/all_to_all | solution.py:24
  46.3 4.5 %collective-permute-start.1 = (bf16[64,4096]{1,0:T(8,128)(2,1)}, bf16[64,4096]{1,0:T(8,128)(2,1)S(1)}, u32[]{:S(2)}, u32[]{:S(2)}) collective-permute-start(bf16[64,4096]{1,0:T(8,128)(2,1)} %reshape.157.rows_ref), channel_id=1, source_target_pairs={{0,3},{3,0},{1,4},{4,1},{2,5},{5,2},{6,9},{9,6},{7,10},{10,7},{8,1... | collective-permute-start | bytes 1572872 | tf_op jit(solution)/shard_map/ppermute | solution.py:349
  48.3 1.0 %copy-start.3 = (bf16[64,4096]{1,0:T(8,128)(2,1)S(1)}, bf16[64,4096]{1,0:T(8,128)(2,1)}, u32[]{:S(2)}) copy-start(bf16[64,4096]{1,0:T(8,128)(2,1)} %reshape.157.rows_ref) | copy-start | bytes 1572868
  65.2 12.1 %all-to-all-start.2 = ((f32[3,136,128]{2,1,0:T(8,128)}), f32[3,136,128]{2,1,0:T(8,128)S(1)}, u32[]{:S(2)}, u32[]{:S(2)}) async-start(f32[3,136,128]{2,1,0:T(8,128)} %get-tuple-element.24), calls=%async_computation.2 | async-start | bytes 417792 | tf_op jit(solution)/shard_map/all_to_all | solution.py:24
  78.3 17.6 %all-to-all-start.3 = ((bf16[6,128,128]{2,1,0:T(8,128)(2,1)}), bf16[6,128,128]{2,1,0:T(8,128)(2,1)S(1)}, u32[]{:S(2)}, u32[]{:S(2)}) async-start(bf16[6,128,128]{2,1,0:T(8,128)(2,1)} %get-tuple-element.27), calls=%async_computation.3 | async-start | bytes 393216 | tf_op jit(solution)/shard_map/all_to_all | solution.py:24
  82.4 13.5 %collective-permute-start.3 = (bf16[16,512]{1,0:T(8,128)(2,1)S(1)}, bf16[16,512]{1,0:T(8,128)(2,1)S(1)}, u32[]{:S(2)}, u32[]{:S(2)}) collective-permute-start(bf16[16,512]{1,0:T(8,128)(2,1)S(1)} %shard_map.110), channel_id=1, source_target_pairs={{0,576},{576,0},{192,384},{384,192},{1,577},{577,1},{193,385},{385... | collective-permute-start | bytes 49160 | tf_op jit(solution)/shard_map/ppermute | solution.py:392

commit v5 on v4

--- a/solution.py
+++ b/solution.py
@@ -85,7 +85,7 @@
 
 
 STEPS = 4
-VMEM_LIMIT = 16 * 2**20
+VMEM_LIMIT = 12 * 2**20
 
 
 def rows_call(kernel, blocks, vectors, weight, near=None):
@@ -165,8 +165,8 @@
         ],
         out_specs=[block, block],
         out_shape=[
-            jax.ShapeDtypeStruct(shape, jnp.float32),
-            jax.ShapeDtypeStruct(shape, jnp.bfloat16),
+            pltpu.HBM(shape, jnp.float32),
+            pltpu.HBM(shape, jnp.bfloat16),
         ],
         compiler_params=pltpu.CompilerParams(vmem_limit_bytes=VMEM_LIMIT),
         cost_estimate=pl.CostEstimate(flops=0, bytes_accessed=0, transcendentals=0),
@@ -178,15 +178,32 @@
 
 
 def zero_after(anything):
-    zeros = pl.pallas_call(
+    return pl.pallas_call(
         zero_kernel,
         in_specs=[pl.BlockSpec(memory_space=pl.ANY)],
         out_specs=pl.BlockSpec(memory_space=pltpu.VMEM),
         out_shape=jax.ShapeDtypeStruct((8, 128), jnp.float32),
         compiler_params=pltpu.CompilerParams(vmem_limit_bytes=2**20),
         cost_estimate=pl.CostEstimate(flops=2**35, bytes_accessed=2**26, transcendentals=0),
-    )(anything)
-    return zeros[0, 0]
+    )(pltpu.with_memory_space_constraint(anything, pltpu.HBM))
+
+
+def add_kernel(own_ref, arriving_ref, zero_ref, sum_ref):
+    values = own_ref[...] + arriving_ref[...].astype(jnp.float32)
+    sum_ref[...] = (values + zero_ref[0, 0]).astype(jnp.bfloat16)
+
+
+def add_call(own, arriving, zeros):
+    block = pl.BlockSpec((own.shape[0] // 2, *own.shape[1:]), lambda k: (k, 0, 0))
+    return pl.pallas_call(
+        add_kernel,
+        grid=(2,),
+        in_specs=[block, block, pl.BlockSpec(zeros.shape, lambda k: (0, 0))],
+        out_specs=block,
+        out_shape=pltpu.HBM(own.shape, jnp.bfloat16),
+        compiler_params=pltpu.CompilerParams(vmem_limit_bytes=VMEM_LIMIT),
+        cost_estimate=pl.CostEstimate(flops=0, bytes_accessed=0, transcendentals=0),
+    )(pltpu.with_memory_space_constraint(own, pltpu.HBM), arriving, zeros)
 
 
 def lines_of(values):
@@ -198,8 +215,8 @@
     return jnp.sum(jnp.sum(values, axis=0, keepdims=True), axis=1, keepdims=True)
 
 
-def finish_kernel(blocks, lines_ref, gain_ref, payload_in, term_ref, payload_out):
-    term = jnp.sum(blocks[...].astype(jnp.float32), axis=0)
+def finish_kernel(blocks, lines_ref, gain_ref, zero_ref, payload_in, term_ref, payload_out):
+    term = jnp.sum(blocks[...].astype(jnp.float32), axis=0) + zero_ref[0, 0]
     term_ref[...] = term
     saved = lines_ref[0].astype(jnp.float32)
     scaled = term * gain_ref[...]
@@ -215,22 +232,22 @@
         payload_out[i] = jnp.where(row == 4, moments, payload_in[i])
 
 
-def finish_call(blocks, lines, gain, payload):
+def finish_call(blocks, lines, gain, zeros, payload):
     vmem = pl.BlockSpec(memory_space=pltpu.VMEM)
     tail = pl.BlockSpec((payload.shape[0], 8, 128), lambda i: (0, payload.shape[1] // 8 - 1, 0))
     return pl.pallas_call(
         finish_kernel,
         grid=(1,),
-        in_specs=[vmem, vmem, vmem, tail],
+        in_specs=[vmem, vmem, vmem, vmem, tail],
         out_specs=[vmem, tail],
         out_shape=[
             jax.ShapeDtypeStruct(gain.shape, jnp.float32),
             jax.ShapeDtypeStruct(payload.shape, payload.dtype),
         ],
-        input_output_aliases={3: 1},
+        input_output_aliases={4: 1},
         compiler_params=pltpu.CompilerParams(vmem_limit_bytes=VMEM_LIMIT),
         cost_estimate=pl.CostEstimate(flops=2**20, bytes_accessed=2**20, transcendentals=0),
-    )(blocks, lines, gain, payload)
+    )(blocks, lines, gain, zeros, payload)
 
 
 def hidden_kernel(even_ref, received, order_ref, hidden_ref, moments_ref):
@@ -341,7 +358,7 @@
     cores = [(0, 1), (1, 0)]
     own_terms, other_terms = terms_call(right_side, weight)
     arriving = lax.ppermute(other_terms, CORE, cores)
-    chip_terms = (own_terms + (arriving.astype(f32) + zero_after(near))).astype(bf16)
+    chip_terms = add_call(own_terms, arriving, zero_after(near))
     near, chip_terms = lax.optimization_barrier((near, chip_terms))
     term_blocks = exchange(chip_terms, PLANE)
 
@@ -356,7 +373,9 @@
 
     line_gain = lines_of(jnp.broadcast_to(gain[None], (own, features)))[0]
     lines = lines_of(jnp.stack((saved_in[0], stream, gradient)))
-    term, payload = finish_call(term_blocks, lines, line_gain + zero_after(term_blocks), payload)
+    term, payload = finish_call(
+        term_blocks, lines, line_gain, zero_after(term_blocks), payload
+    )
     other = ((token // own) % 2 != core).astype(jnp.int32)
     x_of = token // (2 * own * ny)
     place = ((other * nx + x_of) * ny + (token // (2 * own)) % ny) * own + t_of

time: 98.1 us -> 94.6 us (0.964)
  other arithmetic: 5.35 us -> 1.72 us
  Pallas kernels: 9.98 us -> 12.4 us
  local copies, waits for them, and re-layouts: 9.42 us -> 7.3 us
    convert_element_type x1 -> x0, other arithmetic: 2.98 us -> none  [per_device(): (own_terms + (arriving.astype(f32) + zero_after(near))).astype(bf16)]
    pallas_call x1 -> x2, Pallas kernels: 1.84 us -> 4.17 us  [the longest x1 2.3 us: add_call(): pl.pallas_call(add_kernel, grid=(2,), in_specs=[block, block, pl.BlockSpe...]
    unnamed x24 -> x20, local copies, waits for them, and re-layouts: 4.87 us -> 3.77 us
    slice x2 -> x0, local copies, waits for them, and re-layouts: 1.03 us -> none  [zero_after(): return zeros[0, 0]]
  transfers between devices with their start and end apart: 8 -> 8, of which waited for: 4 -> 4; matrix products, arithmetic and copies ran while one was open for 9% -> 4% of each run, Pallas kernels for 8% -> 11%
where the time goes in v5:
time: 94.6 us; the launch traced here: 93.8 us
  starting transfers between devices  51.7 us (55%)
  waiting for transfers between devices  18.5 us (20%)
  Pallas kernels  12.4 us (13%)
  local copies, waits for them, and re-layouts  7.3 us (8%)
  other arithmetic  1.72 us (2%)
  matrix products  1.25 us (1%)
  between operations  0.96 us (1%)
    all_to_all x4, starting transfers between devices, exchange(): return lax.all_to_all(blocks, axis, 0, 0, tiled=True)  32.5 us
    all_to_all x4, waiting for transfers between devices, exchange(): return lax.all_to_all(blocks, axis, 0, 0, tiled=True)  16.3 us
    ppermute x1, starting transfers between devices, per_device(): late = lax.ppermute(late, SECTION, [(0, 3), (3, 0), (1, 2), (2, 1)])  10.3 us
    ppermute x1, starting transfers between devices, per_device(): early = lax.ppermute(early, SECTION, [(0, 1), (1, 0), (2, 3), (3, 2)])  5.06 us
    unnamed x20, local copies, waits for them, and re-layouts  3.77 us
    pallas_call x2, Pallas kernels, rows_call(): pl.pallas_call(kernel, grid=(STEPS,), in_specs=specs, out_specs=out_specs...  3.61 us
    pallas_call x1, Pallas kernels, terms_call(): pl.pallas_call(terms_kernel, grid=(features // 1024,), in_specs=[pl.Block...  2.75 us
    pallas_call x1, Pallas kernels, add_call(): pl.pallas_call(add_kernel, grid=(2,), in_specs=[block, block, pl.BlockSpe...  2.3 us
  transfers between devices with their start and end apart: 8, of which 4 were waited for; matrix products, arithmetic and copies ran while one was open for 4% of the time, Pallas kernels for 11%

profile of v5, /device:TPU:8, one launch (start us, length us, event | category | flops | bytes accessed | tf_op | source)
XLA Modules:
  0.0 93.8 jit_solution(16751097724094916534)
XLA Ops:
  0.6 0.0 copy-start
  0.6 0.0 copy-start.5
  0.7 0.0 copy-start.6
  0.7 0.0 copy-start.8
  0.7 0.0 copy-start.7
  0.7 0.8 fusion.17
  1.5 1.3 %broadcast_in_dim.39 = bf16[32,2,4096]{2,1,0:T(2,128)(2,1)} broadcast(bf16[2,4096]{1,0:T(2,128)(2,1)S(1)} %fusion.17), dimensions={1,2} | broadcast | bytes 540672 | tf_op jit(solution)/shard_map/broadcast_in_dim | solution.py:28
  2.7 13.0 %all-to-all-start = ((bf16[32,2,4096]{2,1,0:T(2,128)(2,1)}), bf16[32,2,4096]{2,1,0:T(2,128)(2,1)S(1)}, u32[]{:S(2)}, u32[]{:S(2)}) async-start(bf16[32,2,4096]{2,1,0:T(2,128)(2,1)} %broadcast_in_dim.39), calls=%async_computation | async-start | bytes 1048576 | tf_op jit(solution)/shard_map/all_to_all | solution.py:24
  15.8 1.2 %convolution_convert_fusion.rows_ref = bf16[128,384]{1,0:T(8,128)(2,1)S(1)} fusion(bf16[1,128,384]{2,1,0:T(8,128)(2,1)} %param.12, bf16[1,128,384]{2,1,0:T(8,128)(2,1)} %param.9, pred[]{:T(512)S(6)} %eq.35, s32[128]{0:T(128)S(1)} %fusion.19), kind=kOutput, calls=%fused_computation | convolution fusion | flops 13778944 | bytes 295425 | tf_op jit(solution)/shard_map/dot_general | solution.py:33
  17.0 0.0 copy-start.1
  17.0 1.9 %copy-done.1 = bf16[1,4096,384]{2,1,0:T(8,128)(2,1)S(1)} copy-done((bf16[1,4096,384]{2,1,0:T(8,128)(2,1)S(1)}, bf16[1,4096,384]{2,1,0:T(8,128)(2,1)}, u32[]{:S(2)}) %copy-start.1) | copy-done | bytes 3145752
  18.9 2.7 %shard_map.103 = (f32[32,16,512]{2,1,0:T(8,128)}, bf16[32,16,512]{2,1,0:T(8,128)(2,1)}) custom-call(bf16[128,384]{1,0:T(8,128)(2,1)S(1)} %convolution_convert_fusion.rows_ref, bf16[4096,384]{1,0:T(8,128)(2,1)S(1)} %bitcast.37), custom_call_target="tpu_custom_call" | custom-call | tf_op jit(solution)/shard_map/pallas_call | solution.py:159
  21.7 1.9 %collective-permute-start = (bf16[32,16,512]{2,1,0:T(8,128)(2,1)}, bf16[32,16,512]{2,1,0:T(8,128)(2,1)}, u32[]{:S(2)}, u32[]{:S(2)}) collective-permute-start(bf16[32,16,512]{2,1,0:T(8,128)(2,1)} %get-tuple-element.18), channel_id=1, source_target_pairs={{0,3},{3,0},{1,4},{4,1},{2,5},{5,2},{6,9},{9,6},{7,10},{10,7},{8,1... | collective-permute-start | bytes 1572872 | tf_op jit(solution)/shard_map/ppermute | solution.py:360
  23.6 0.0 copy-done.5
  23.6 0.0 copy-done.6
  23.6 5.1 %collective-permute-start.2 = (bf16[2,4096]{1,0:T(2,128)(2,1)S(1)}, bf16[2,4096]{1,0:T(2,128)(2,1)S(1)}, u32[]{:S(2)}, u32[]{:S(2)}) collective-permute-start(bf16[2,4096]{1,0:T(2,128)(2,1)S(1)} %broadcast_select_fusion.4), channel_id=1, source_target_pairs={{0,192},{192,0},{384,576},{576,384},{1,193},{193,1},{385,577},{577... | collective-permute-start | bytes 49160 | tf_op jit(solution)/shard_map/ppermute | solution.py:347
  28.7 0.0 copy-done.8
  28.8 0.0 copy-done.7
  28.8 0.1 pad_maximum_fusion
  28.8 1.9 %all-to-all-done.anything_ref = bf16[32,2,4096]{2,1,0:T(2,128)(2,1)S(1)} async-done(((bf16[32,2,4096]{2,1,0:T(2,128)(2,1)}), bf16[32,2,4096]{2,1,0:T(2,128)(2,1)S(1)}, u32[]{:S(2)}, u32[]{:S(2)}) %all-to-all-start) | async-done | bytes 524320 | tf_op jit(solution)/shard_map/all_to_all | solution.py:24
  30.7 0.8 copy-done.4
  31.5 0.0 collective-permute-done.arriving_ref
  31.5 2.3 %shard_map.105 = bf16[32,16,512]{2,1,0:T(8,128)(2,1)} custom-call(f32[32,16,512]{2,1,0:T(8,128)} %get-tuple-element.17.own_ref, bf16[32,16,512]{2,1,0:T(8,128)(2,1)} %collective-permute-done.arriving_ref, f32[8,128]{1,0:T(8,128)S(1)} %shard_map.104.zero_ref), custom_call_target="tpu_custom_call" | custom-call | tf_op jit(solution)/shard_map/pallas_call | solution.py:198
  33.8 8.0 %all-to-all-start.1 = ((bf16[32,16,512]{2,1,0:T(8,128)(2,1)}), bf16[32,16,512]{2,1,0:T(8,128)(2,1)}, u32[]{:S(2)}, u32[]{:S(2)}) async-start(bf16[32,16,512]{2,1,0:T(8,128)(2,1)} %shard_map.105), calls=%async_computation.1 | async-start | bytes 1048576 | tf_op jit(solution)/shard_map/all_to_all | solution.py:24
  41.8 0.0 copy-done
  42.0 0.1 pad.2.clone
  42.1 2.0 %reshape.157.rows_ref = bf16[64,4096]{1,0:T(8,128)(2,1)} reshape(bf16[32,2,4096]{2,1,0:T(2,128)(2,1)} %copy-done.4) | data formatting | bytes 1048576 | tf_op jit(solution)/shard_map/reshape | solution.py:365
  44.1 1.9 %collective-permute-start.1 = (bf16[64,4096]{1,0:T(8,128)(2,1)}, bf16[64,4096]{1,0:T(8,128)(2,1)S(1)}, u32[]{:S(2)}, u32[]{:S(2)}) collective-permute-start(bf16[64,4096]{1,0:T(8,128)(2,1)} %reshape.157.rows_ref), channel_id=1, source_target_pairs={{0,3},{3,0},{1,4},{4,1},{2,5},{5,2},{6,9},{9,6},{7,10},{10,7},{8,1... | collective-permute-start | bytes 1572872 | tf_op jit(solution)/shard_map/ppermute | solution.py:366
  46.1 0.1 maximum_maximum_fusion.vectors_ref
  46.1 0.0 copy-done.2
  46.2 1.0 %copy-done.3 = bf16[64,4096]{1,0:T(8,128)(2,1)S(1)} copy-done((bf16[64,4096]{1,0:T(8,128)(2,1)S(1)}, bf16[64,4096]{1,0:T(8,128)(2,1)}, u32[]{:S(2)}) %copy-start.3) | copy-done | bytes 524312
  47.2 1.4 %shard_map.107.near_ref = f32[136,384]{1,0:T(8,128)S(1)} custom-call(bf16[64,4096]{1,0:T(8,128)(2,1)S(1)} %copy-done.3, f32[8,4096]{1,0:T(8,128)S(1)} %maximum_maximum_fusion.vectors_ref, bf16[4096,384]{1,0:T(8,128)(2,1)S(1)} %bitcast.38), custom_call_target="tpu_custom_call" | custom-call | tf_op jit(solution)/shard_map/pallas_call | solution.py:111
  48.6 0.0 collective-permute-done.1.rows_ref
  48.6 2.2 %shard_map.108.payload_in = f32[3,136,128]{2,1,0:T(8,128)} custom-call(bf16[64,4096]{1,0:T(8,128)(2,1)S(1)} %collective-permute-done.1.rows_ref, f32[8,4096]{1,0:T(8,128)S(1)} %maximum_maximum_fusion.vectors_ref, bf16[4096,384]{1,0:T(8,128)(2,1)S(1)} %bitcast.39, f32[136,384]{1,0:T(8,128)S(1)} %shard_map.107.near_ref), custom_call_target="tpu_custom_call" | custom-call | tf_op jit(solution)/shard_map/pallas_call | solution.py:111
  50.8 9.1 %all-to-all-done.1.anything_ref.blocks = bf16[32,16,512]{2,1,0:T(8,128)(2,1)} async-done(((bf16[32,16,512]{2,1,0:T(8,128)(2,1)}), bf16[32,16,512]{2,1,0:T(8,128)(2,1)}, u32[]{:S(2)}, u32[]{:S(2)}) %all-to-all-start.1) | async-done | bytes 524320 | tf_op jit(solution)/shard_map/all_to_all | solution.py:24
  59.9 1.9 %shard_map.109 = (f32[16,512]{1,0:T(8,128)S(1)}, f32[3,136,128]{2,1,0:T(8,128)}) custom-call(bf16[32,16,512]{2,1,0:T(8,128)(2,1)} %all-to-all-done.1.anything_ref.blocks, bf16[3,16,512]{2,1,0:T(8,128)(2,1)S(1)} %reshape.156.lines_ref, f32[16,512]{1,0:T(8,128)S(1)} %bitcast.40, f32[8,128]{1,0:T(8,128)S(1)} %shard_map.106.zero_ref, ...), custom_call_target="tpu_custom_call", output_to_operand_aliasing={{1}: (4, {})} | custom-call | flops 1048576 | bytes 1048576 | tf_op jit(solution)/shard_map/pallas_call | solution.py:238
  61.8 0.0 collective-permute-done.2
  61.8 6.7 %all-to-all-start.2 = ((f32[3,136,128]{2,1,0:T(8,128)}), f32[3,136,128]{2,1,0:T(8,128)S(1)}, u32[]{:S(2)}, u32[]{:S(2)}) async-start(f32[3,136,128]{2,1,0:T(8,128)} %get-tuple-element.24), calls=%async_computation.2 | async-start | bytes 417792 | tf_op jit(solution)/shard_map/all_to_all | solution.py:24
  68.4 0.1 fusion.13.order_ref
  68.5 5.3 %all-to-all-done.2.received = f32[3,136,128]{2,1,0:T(8,128)S(1)} async-done(((f32[3,136,128]{2,1,0:T(8,128)}), f32[3,136,128]{2,1,0:T(8,128)S(1)}, u32[]{:S(2)}, u32[]{:S(2)}) %all-to-all-start.2) | async-done | bytes 208928 | tf_op jit(solution)/shard_map/all_to_all | solution.py:24
  73.8 1.1 %shard_map.110 = (bf16[6,128,128]{2,1,0:T(8,128)(2,1)}, f32[8,128]{1,0:T(8,128)S(1)}) custom-call(s32[1]{0:T(128)} %bitcast.even_ref, f32[3,136,128]{2,1,0:T(8,128)S(1)} %all-to-all-done.2.received, bf16[128,128]{1,0:T(8,128)(2,1)S(1)} %fusion.13.order_ref), custom_call_target="tpu_custom_call" | custom-call | tf_op jit(solution)/shard_map/pallas_call | solution.py:319
  74.9 4.9 %all-to-all-start.3 = ((bf16[6,128,128]{2,1,0:T(8,128)(2,1)}), bf16[6,128,128]{2,1,0:T(8,128)(2,1)S(1)}, u32[]{:S(2)}, u32[]{:S(2)}) async-start(bf16[6,128,128]{2,1,0:T(8,128)(2,1)} %get-tuple-element.27), calls=%async_computation.3 | async-start | bytes 393216 | tf_op jit(solution)/shard_map/all_to_all | solution.py:24
  79.8 0.1 shard_map.111
  79.9 10.3 %collective-permute-start.3 = (bf16[16,512]{1,0:T(8,128)(2,1)S(1)}, bf16[16,512]{1,0:T(8,128)(2,1)S(1)}, u32[]{:S(2)}, u32[]{:S(2)}) collective-permute-start(bf16[16,512]{1,0:T(8,128)(2,1)S(1)} %shard_map.111), channel_id=1, source_target_pairs={{0,576},{576,0},{192,384},{384,192},{1,577},{577,1},{193,385},{385... | collective-permute-start | bytes 49160 | tf_op jit(solution)/shard_map/ppermute | solution.py:411
  90.2 2.3 %collective-permute-done.3 = bf16[16,512]{1,0:T(8,128)(2,1)S(1)} collective-permute-done((bf16[16,512]{1,0:T(8,128)(2,1)S(1)}, bf16[16,512]{1,0:T(8,128)(2,1)S(1)}, u32[]{:S(2)}, u32[]{:S(2)}) %collective-permute-start.3) | collective-permute-done | bytes 16416 | tf_op jit(solution)/shard_map/ppermute | solution.py:411
  92.5 0.0 all-to-all-done.3.refs_0_.refs_1_.refs_2_
  92.5 0.7 shard_map.112
  93.2 0.6 fusion.16
  (20 shorter events, 0.2 us)
Async XLA Ops:
  0.6 41.2 %copy-start = (f32[2,4096]{1,0:T(2,128)S(1)}, f32[2,4096]{1,0:T(2,128)}, u32[]{:S(2)}) copy-start(f32[2,4096]{1,0:T(2,128)} %param.15) | copy-start | bytes 98308
  0.6 22.9 %copy-start.5 = (bf16[1,2,4096]{2,1,0:T(2,128)(2,1)S(1)}, bf16[1,2,4096]{2,1,0:T(2,128)(2,1)}, u32[]{:S(2)}) copy-start(bf16[1,2,4096]{2,1,0:T(2,128)(2,1)} %param.8) | copy-start | bytes 49156
  0.7 22.9 %copy-start.6 = (bf16[1,2,4096]{2,1,0:T(2,128)(2,1)S(1)}, bf16[1,2,4096]{2,1,0:T(2,128)(2,1)}, u32[]{:S(2)}) copy-start(bf16[1,2,4096]{2,1,0:T(2,128)(2,1)} %param.10) | copy-start | bytes 49156
  0.7 28.0 %copy-start.8 = (f32[2,4096]{1,0:T(2,128)S(1)}, f32[2,4096]{1,0:T(2,128)}, u32[]{:S(2)}) copy-start(f32[2,4096]{1,0:T(2,128)} %param.14) | copy-start | bytes 98308
  0.7 28.1 %copy-start.7 = (bf16[1,2,4096]{2,1,0:T(2,128)(2,1)S(1)}, bf16[1,2,4096]{2,1,0:T(2,128)(2,1)}, u32[]{:S(2)}) copy-start(bf16[1,2,4096]{2,1,0:T(2,128)(2,1)} %param.11) | copy-start | bytes 49156
  2.7 28.0 %all-to-all-start = ((bf16[32,2,4096]{2,1,0:T(2,128)(2,1)}), bf16[32,2,4096]{2,1,0:T(2,128)(2,1)S(1)}, u32[]{:S(2)}, u32[]{:S(2)}) async-start(bf16[32,2,4096]{2,1,0:T(2,128)(2,1)} %broadcast_in_dim.39), calls=%async_computation | async-start | bytes 1048576 | tf_op jit(solution)/shard_map/all_to_all | solution.py:24
  17.0 1.9 %copy-start.1 = (bf16[1,4096,384]{2,1,0:T(8,128)(2,1)S(1)}, bf16[1,4096,384]{2,1,0:T(8,128)(2,1)}, u32[]{:S(2)}) copy-start(bf16[1,4096,384]{2,1,0:T(8,128)(2,1)} %param.13) | copy-start | bytes 9437188
  21.7 9.9 %collective-permute-start = (bf16[32,16,512]{2,1,0:T(8,128)(2,1)}, bf16[32,16,512]{2,1,0:T(8,128)(2,1)}, u32[]{:S(2)}, u32[]{:S(2)}) collective-permute-start(bf16[32,16,512]{2,1,0:T(8,128)(2,1)} %get-tuple-element.18), channel_id=1, source_target_pairs={{0,3},{3,0},{1,4},{4,1},{2,5},{5,2},{6,9},{9,6},{7,10},{10,7},{8,1... | collective-permute-start | bytes 1572872 | tf_op jit(solution)/shard_map/ppermute | solution.py:360
  23.6 38.1 %collective-permute-start.2 = (bf16[2,4096]{1,0:T(2,128)(2,1)S(1)}, bf16[2,4096]{1,0:T(2,128)(2,1)S(1)}, u32[]{:S(2)}, u32[]{:S(2)}) collective-permute-start(bf16[2,4096]{1,0:T(2,128)(2,1)S(1)} %broadcast_select_fusion.4), channel_id=1, source_target_pairs={{0,192},{192,0},{384,576},{576,384},{1,193},{193,1},{385,577},{577... | collective-permute-start | bytes 49160 | tf_op jit(solution)/shard_map/ppermute | solution.py:347
  30.7 0.8 copy-start.4
  31.5 14.6 %copy-start.2 = (bf16[1,4096,384]{2,1,0:T(8,128)(2,1)S(1)}, bf16[1,4096,384]{2,1,0:T(8,128)(2,1)}, u32[]{:S(2)}) copy-start(bf16[1,4096,384]{2,1,0:T(8,128)(2,1)} %param.13) | copy-start | bytes 9437188
  33.8 26.0 %all-to-all-start.1 = ((bf16[32,16,512]{2,1,0:T(8,128)(2,1)}), bf16[32,16,512]{2,1,0:T(8,128)(2,1)}, u32[]{:S(2)}, u32[]{:S(2)}) async-start(bf16[32,16,512]{2,1,0:T(8,128)(2,1)} %shard_map.105), calls=%async_computation.1 | async-start | bytes 1048576 | tf_op jit(solution)/shard_map/all_to_all | solution.py:24
  44.1 4.5 %collective-permute-start.1 = (bf16[64,4096]{1,0:T(8,128)(2,1)}, bf16[64,4096]{1,0:T(8,128)(2,1)S(1)}, u32[]{:S(2)}, u32[]{:S(2)}) collective-permute-start(bf16[64,4096]{1,0:T(8,128)(2,1)} %reshape.157.rows_ref), channel_id=1, source_target_pairs={{0,3},{3,0},{1,4},{4,1},{2,5},{5,2},{6,9},{9,6},{7,10},{10,7},{8,1... | collective-permute-start | bytes 1572872 | tf_op jit(solution)/shard_map/ppermute | solution.py:366
  46.1 1.0 %copy-start.3 = (bf16[64,4096]{1,0:T(8,128)(2,1)S(1)}, bf16[64,4096]{1,0:T(8,128)(2,1)}, u32[]{:S(2)}) copy-start(bf16[64,4096]{1,0:T(8,128)(2,1)} %reshape.157.rows_ref) | copy-start | bytes 1572868
  61.8 12.1 %all-to-all-start.2 = ((f32[3,136,128]{2,1,0:T(8,128)}), f32[3,136,128]{2,1,0:T(8,128)S(1)}, u32[]{:S(2)}, u32[]{:S(2)}) async-start(f32[3,136,128]{2,1,0:T(8,128)} %get-tuple-element.24), calls=%async_computation.2 | async-start | bytes 417792 | tf_op jit(solution)/shard_map/all_to_all | solution.py:24
  74.9 17.6 %all-to-all-start.3 = ((bf16[6,128,128]{2,1,0:T(8,128)(2,1)}), bf16[6,128,128]{2,1,0:T(8,128)(2,1)S(1)}, u32[]{:S(2)}, u32[]{:S(2)}) async-start(bf16[6,128,128]{2,1,0:T(8,128)(2,1)} %get-tuple-element.27), calls=%async_computation.3 | async-start | bytes 393216 | tf_op jit(solution)/shard_map/all_to_all | solution.py:24
  79.9 12.5 %collective-permute-start.3 = (bf16[16,512]{1,0:T(8,128)(2,1)S(1)}, bf16[16,512]{1,0:T(8,128)(2,1)S(1)}, u32[]{:S(2)}, u32[]{:S(2)}) collective-permute-start(bf16[16,512]{1,0:T(8,128)(2,1)S(1)} %shard_map.111), channel_id=1, source_target_pairs={{0,576},{576,0},{192,384},{384,192},{1,577},{577,1},{193,385},{385... | collective-permute-start | bytes 49160 | tf_op jit(solution)/shard_map/ppermute | solution.py:411

commit v6 on v5

--- a/solution.py
+++ b/solution.py
@@ -185,7 +185,7 @@
         out_shape=jax.ShapeDtypeStruct((8, 128), jnp.float32),
         compiler_params=pltpu.CompilerParams(vmem_limit_bytes=2**20),
         cost_estimate=pl.CostEstimate(flops=2**35, bytes_accessed=2**26, transcendentals=0),
-    )(pltpu.with_memory_space_constraint(anything, pltpu.HBM))
+    )(anything)
 
 
 def add_kernel(own_ref, arriving_ref, zero_ref, sum_ref):
@@ -346,7 +346,7 @@
     early = jnp.where(is_even, *lax.optimization_barrier((stream, gradient)))
     early = lax.ppermute(early, SECTION, [(0, 1), (1, 0), (2, 3), (3, 2)])
 
-    leading = copies(jnp.where(is_even, stream, gradient), PLANE)
+    leading = jnp.where(is_even, copies(stream, PLANE), copies(gradient, PLANE))
 
     token = jnp.arange(tokens)
     t_of = token % own
@@ -358,7 +358,7 @@
     cores = [(0, 1), (1, 0)]
     own_terms, other_terms = terms_call(right_side, weight)
     arriving = lax.ppermute(other_terms, CORE, cores)
-    chip_terms = add_call(own_terms, arriving, zero_after(near))
+    chip_terms = add_call(own_terms, arriving, zero_after(near[0, :, :128]))
     near, chip_terms = lax.optimization_barrier((near, chip_terms))
     term_blocks = exchange(chip_terms, PLANE)
 

time: 94.6 us -> 94.6 us (level)
  no operation moved by 1% of the time
where the time goes in v6:
time: 94.6 us; the launch traced here: 93.8 us
  starting transfers between devices  51.7 us (55%)
  waiting for transfers between devices  18.5 us (20%)
  Pallas kernels  12.4 us (13%)
  local copies, waits for them, and re-layouts  7.3 us (8%)
  other arithmetic  1.73 us (2%)
  matrix products  1.25 us (1%)
  between operations  0.96 us (1%)
    all_to_all x4, starting transfers between devices, exchange(): return lax.all_to_all(blocks, axis, 0, 0, tiled=True)  32.5 us
    all_to_all x4, waiting for transfers between devices, exchange(): return lax.all_to_all(blocks, axis, 0, 0, tiled=True)  16.3 us
    ppermute x1, starting transfers between devices, per_device(): late = lax.ppermute(late, SECTION, [(0, 3), (3, 0), (1, 2), (2, 1)])  10.3 us
    ppermute x1, starting transfers between devices, per_device(): early = lax.ppermute(early, SECTION, [(0, 1), (1, 0), (2, 3), (3, 2)])  5.06 us
    unnamed x20, local copies, waits for them, and re-layouts  3.76 us
    pallas_call x2, Pallas kernels, rows_call(): pl.pallas_call(kernel, grid=(STEPS,), in_specs=specs, out_specs=out_specs...  3.61 us
    pallas_call x1, Pallas kernels, terms_call(): pl.pallas_call(terms_kernel, grid=(features // 1024,), in_specs=[pl.Block...  2.75 us
    pallas_call x1, Pallas kernels, add_call(): pl.pallas_call(add_kernel, grid=(2,), in_specs=[block, block, pl.BlockSpe...  2.3 us
  transfers between devices with their start and end apart: 8, of which 4 were waited for; matrix products, arithmetic and copies ran while one was open for 4% of the time, Pallas kernels for 11%

profile of v6, /device:TPU:8, one launch (start us, length us, event | category | flops | bytes accessed | tf_op | source)
XLA Modules:
  0.0 93.8 jit_solution(18076688168910997553)
XLA Ops:
  0.6 0.0 copy-start
  0.6 0.0 copy-start.6
  0.7 0.0 copy-start.5
  0.7 0.0 copy-start.8
  0.7 0.0 copy-start.7
  0.7 0.8 broadcast_select_fusion.4
  1.5 1.3 %broadcast_in_dim.44 = bf16[32,2,4096]{2,1,0:T(2,128)(2,1)} broadcast(bf16[2,4096]{1,0:T(2,128)(2,1)S(1)} %broadcast_select_fusion.4), dimensions={1,2} | broadcast | bytes 540672 | tf_op jit(solution)/shard_map/broadcast_in_dim | solution.py:28
  2.7 13.0 %all-to-all-start = ((bf16[32,2,4096]{2,1,0:T(2,128)(2,1)}), bf16[32,2,4096]{2,1,0:T(2,128)(2,1)S(1)}, u32[]{:S(2)}, u32[]{:S(2)}) async-start(bf16[32,2,4096]{2,1,0:T(2,128)(2,1)} %broadcast_in_dim.44), calls=%async_computation | async-start | bytes 1048576 | tf_op jit(solution)/shard_map/all_to_all | solution.py:24
  15.8 1.2 %convolution_convert_fusion.rows_ref = bf16[128,384]{1,0:T(8,128)(2,1)S(1)} fusion(bf16[1,128,384]{2,1,0:T(8,128)(2,1)} %param.12, bf16[1,128,384]{2,1,0:T(8,128)(2,1)} %param.9, pred[]{:T(512)S(6)} %eq.35, s32[128]{0:T(128)S(1)} %fusion.18), kind=kOutput, calls=%fused_computation | convolution fusion | flops 13778944 | bytes 295425 | tf_op jit(solution)/shard_map/dot_general | solution.py:33
  17.0 0.0 copy-start.1
  17.0 1.9 %copy-done.1 = bf16[1,4096,384]{2,1,0:T(8,128)(2,1)S(1)} copy-done((bf16[1,4096,384]{2,1,0:T(8,128)(2,1)S(1)}, bf16[1,4096,384]{2,1,0:T(8,128)(2,1)}, u32[]{:S(2)}) %copy-start.1) | copy-done | bytes 3145752
  18.9 2.7 %shard_map.103 = (f32[32,16,512]{2,1,0:T(8,128)}, bf16[32,16,512]{2,1,0:T(8,128)(2,1)}) custom-call(bf16[128,384]{1,0:T(8,128)(2,1)S(1)} %convolution_convert_fusion.rows_ref, bf16[4096,384]{1,0:T(8,128)(2,1)S(1)} %bitcast.39), custom_call_target="tpu_custom_call" | custom-call | tf_op jit(solution)/shard_map/pallas_call | solution.py:159
  21.7 1.9 %collective-permute-start = (bf16[32,16,512]{2,1,0:T(8,128)(2,1)}, bf16[32,16,512]{2,1,0:T(8,128)(2,1)}, u32[]{:S(2)}, u32[]{:S(2)}) collective-permute-start(bf16[32,16,512]{2,1,0:T(8,128)(2,1)} %get-tuple-element.18), channel_id=1, source_target_pairs={{0,3},{3,0},{1,4},{4,1},{2,5},{5,2},{6,9},{9,6},{7,10},{10,7},{8,1... | collective-permute-start | bytes 1572872 | tf_op jit(solution)/shard_map/ppermute | solution.py:360
  23.6 0.0 copy-done.6
  23.6 0.0 copy-done.5
  23.6 5.1 %collective-permute-start.2 = (bf16[2,4096]{1,0:T(2,128)(2,1)S(1)}, bf16[2,4096]{1,0:T(2,128)(2,1)S(1)}, u32[]{:S(2)}, u32[]{:S(2)}) collective-permute-start(bf16[2,4096]{1,0:T(2,128)(2,1)S(1)} %broadcast_select_fusion.3), channel_id=1, source_target_pairs={{0,192},{192,0},{384,576},{576,384},{1,193},{193,1},{385,577},{577... | collective-permute-start | bytes 49160 | tf_op jit(solution)/shard_map/ppermute | solution.py:347
  28.7 0.0 copy-done.8
  28.8 0.0 copy-done.7
  28.8 0.1 pad_maximum_fusion
  28.9 1.9 %all-to-all-done = bf16[32,2,4096]{2,1,0:T(2,128)(2,1)S(1)} async-done(((bf16[32,2,4096]{2,1,0:T(2,128)(2,1)}), bf16[32,2,4096]{2,1,0:T(2,128)(2,1)S(1)}, u32[]{:S(2)}, u32[]{:S(2)}) %all-to-all-start) | async-done | bytes 524320 | tf_op jit(solution)/shard_map/all_to_all | solution.py:24
  30.7 0.8 copy-done.4
  31.5 0.0 collective-permute-done.arriving_ref
  31.5 2.3 %shard_map.105 = bf16[32,16,512]{2,1,0:T(8,128)(2,1)} custom-call(f32[32,16,512]{2,1,0:T(8,128)} %get-tuple-element.17.own_ref, bf16[32,16,512]{2,1,0:T(8,128)(2,1)} %collective-permute-done.arriving_ref, f32[8,128]{1,0:T(8,128)S(1)} %shard_map.104.zero_ref), custom_call_target="tpu_custom_call" | custom-call | tf_op jit(solution)/shard_map/pallas_call | solution.py:198
  33.8 8.0 %all-to-all-start.1 = ((bf16[32,16,512]{2,1,0:T(8,128)(2,1)}), bf16[32,16,512]{2,1,0:T(8,128)(2,1)}, u32[]{:S(2)}, u32[]{:S(2)}) async-start(bf16[32,16,512]{2,1,0:T(8,128)(2,1)} %shard_map.105), calls=%async_computation.1 | async-start | bytes 1048576 | tf_op jit(solution)/shard_map/all_to_all | solution.py:24
  41.8 0.0 copy-done
  42.0 0.1 pad.2.clone
  42.1 2.0 %reshape.157.rows_ref = bf16[64,4096]{1,0:T(8,128)(2,1)} reshape(bf16[32,2,4096]{2,1,0:T(2,128)(2,1)} %copy-done.4) | data formatting | bytes 1048576 | tf_op jit(solution)/shard_map/reshape | solution.py:365
  44.1 1.9 %collective-permute-start.1 = (bf16[64,4096]{1,0:T(8,128)(2,1)}, bf16[64,4096]{1,0:T(8,128)(2,1)S(1)}, u32[]{:S(2)}, u32[]{:S(2)}) collective-permute-start(bf16[64,4096]{1,0:T(8,128)(2,1)} %reshape.157.rows_ref), channel_id=1, source_target_pairs={{0,3},{3,0},{1,4},{4,1},{2,5},{5,2},{6,9},{9,6},{7,10},{10,7},{8,1... | collective-permute-start | bytes 1572872 | tf_op jit(solution)/shard_map/ppermute | solution.py:366
  46.0 0.1 maximum_maximum_fusion.vectors_ref
  46.1 0.0 copy-done.2
  46.2 1.0 %copy-done.3 = bf16[64,4096]{1,0:T(8,128)(2,1)S(1)} copy-done((bf16[64,4096]{1,0:T(8,128)(2,1)S(1)}, bf16[64,4096]{1,0:T(8,128)(2,1)}, u32[]{:S(2)}) %copy-start.3) | copy-done | bytes 524312
  47.2 1.4 %shard_map.107.near_ref = f32[136,384]{1,0:T(8,128)S(1)} custom-call(bf16[64,4096]{1,0:T(8,128)(2,1)S(1)} %copy-done.3, f32[8,4096]{1,0:T(8,128)S(1)} %maximum_maximum_fusion.vectors_ref, bf16[4096,384]{1,0:T(8,128)(2,1)S(1)} %bitcast.40), custom_call_target="tpu_custom_call" | custom-call | tf_op jit(solution)/shard_map/pallas_call | solution.py:111
  48.6 0.0 collective-permute-done.1.rows_ref
  48.6 2.2 %shard_map.108.payload_in = f32[3,136,128]{2,1,0:T(8,128)} custom-call(bf16[64,4096]{1,0:T(8,128)(2,1)S(1)} %collective-permute-done.1.rows_ref, f32[8,4096]{1,0:T(8,128)S(1)} %maximum_maximum_fusion.vectors_ref, bf16[4096,384]{1,0:T(8,128)(2,1)S(1)} %bitcast.41, f32[136,384]{1,0:T(8,128)S(1)} %shard_map.107.near_ref), custom_call_target="tpu_custom_call" | custom-call | tf_op jit(solution)/shard_map/pallas_call | solution.py:111
  50.8 9.1 %all-to-all-done.1.anything_ref.blocks = bf16[32,16,512]{2,1,0:T(8,128)(2,1)} async-done(((bf16[32,16,512]{2,1,0:T(8,128)(2,1)}), bf16[32,16,512]{2,1,0:T(8,128)(2,1)}, u32[]{:S(2)}, u32[]{:S(2)}) %all-to-all-start.1) | async-done | bytes 524320 | tf_op jit(solution)/shard_map/all_to_all | solution.py:24
  59.9 1.9 %shard_map.109 = (f32[16,512]{1,0:T(8,128)S(1)}, f32[3,136,128]{2,1,0:T(8,128)}) custom-call(bf16[32,16,512]{2,1,0:T(8,128)(2,1)} %all-to-all-done.1.anything_ref.blocks, bf16[3,16,512]{2,1,0:T(8,128)(2,1)S(1)} %reshape.156.lines_ref, f32[16,512]{1,0:T(8,128)S(1)} %bitcast.42, f32[8,128]{1,0:T(8,128)S(1)} %shard_map.106.zero_ref, ...), custom_call_target="tpu_custom_call", output_to_operand_aliasing={{1}: (4, {})} | custom-call | flops 1048576 | bytes 1048576 | tf_op jit(solution)/shard_map/pallas_call | solution.py:238
  61.8 0.0 collective-permute-done.2
  61.8 6.7 %all-to-all-start.2 = ((f32[3,136,128]{2,1,0:T(8,128)}), f32[3,136,128]{2,1,0:T(8,128)S(1)}, u32[]{:S(2)}, u32[]{:S(2)}) async-start(f32[3,136,128]{2,1,0:T(8,128)} %get-tuple-element.24), calls=%async_computation.2 | async-start | bytes 417792 | tf_op jit(solution)/shard_map/all_to_all | solution.py:24
  68.4 0.1 fusion.13.order_ref
  68.5 5.3 %all-to-all-done.2.received = f32[3,136,128]{2,1,0:T(8,128)S(1)} async-done(((f32[3,136,128]{2,1,0:T(8,128)}), f32[3,136,128]{2,1,0:T(8,128)S(1)}, u32[]{:S(2)}, u32[]{:S(2)}) %all-to-all-start.2) | async-done | bytes 208928 | tf_op jit(solution)/shard_map/all_to_all | solution.py:24
  73.8 1.1 %shard_map.110 = (bf16[6,128,128]{2,1,0:T(8,128)(2,1)}, f32[8,128]{1,0:T(8,128)S(1)}) custom-call(s32[1]{0:T(128)} %bitcast.even_ref, f32[3,136,128]{2,1,0:T(8,128)S(1)} %all-to-all-done.2.received, bf16[128,128]{1,0:T(8,128)(2,1)S(1)} %fusion.13.order_ref), custom_call_target="tpu_custom_call" | custom-call | tf_op jit(solution)/shard_map/pallas_call | solution.py:319
  74.9 4.9 %all-to-all-start.3 = ((bf16[6,128,128]{2,1,0:T(8,128)(2,1)}), bf16[6,128,128]{2,1,0:T(8,128)(2,1)S(1)}, u32[]{:S(2)}, u32[]{:S(2)}) async-start(bf16[6,128,128]{2,1,0:T(8,128)(2,1)} %get-tuple-element.27), calls=%async_computation.3 | async-start | bytes 393216 | tf_op jit(solution)/shard_map/all_to_all | solution.py:24
  79.8 0.1 shard_map.111
  79.9 10.3 %collective-permute-start.3 = (bf16[16,512]{1,0:T(8,128)(2,1)S(1)}, bf16[16,512]{1,0:T(8,128)(2,1)S(1)}, u32[]{:S(2)}, u32[]{:S(2)}) collective-permute-start(bf16[16,512]{1,0:T(8,128)(2,1)S(1)} %shard_map.111), channel_id=1, source_target_pairs={{0,576},{576,0},{192,384},{384,192},{1,577},{577,1},{193,385},{385... | collective-permute-start | bytes 49160 | tf_op jit(solution)/shard_map/ppermute | solution.py:411
  90.2 2.3 %collective-permute-done.3 = bf16[16,512]{1,0:T(8,128)(2,1)S(1)} collective-permute-done((bf16[16,512]{1,0:T(8,128)(2,1)S(1)}, bf16[16,512]{1,0:T(8,128)(2,1)S(1)}, u32[]{:S(2)}, u32[]{:S(2)}) %collective-permute-start.3) | collective-permute-done | bytes 16416 | tf_op jit(solution)/shard_map/ppermute | solution.py:411
  92.5 0.0 all-to-all-done.3.refs_0_.refs_1_.refs_2_
  92.5 0.7 shard_map.112
  93.2 0.6 fusion.16
  (21 shorter events, 0.3 us)
Async XLA Ops:
  0.6 41.2 %copy-start = (f32[2,4096]{1,0:T(2,128)S(1)}, f32[2,4096]{1,0:T(2,128)}, u32[]{:S(2)}) copy-start(f32[2,4096]{1,0:T(2,128)} %param.15) | copy-start | bytes 98308
  0.6 22.9 %copy-start.6 = (bf16[1,2,4096]{2,1,0:T(2,128)(2,1)S(1)}, bf16[1,2,4096]{2,1,0:T(2,128)(2,1)}, u32[]{:S(2)}) copy-start(bf16[1,2,4096]{2,1,0:T(2,128)(2,1)} %param.10) | copy-start | bytes 49156
  0.7 22.9 %copy-start.5 = (bf16[1,2,4096]{2,1,0:T(2,128)(2,1)S(1)}, bf16[1,2,4096]{2,1,0:T(2,128)(2,1)}, u32[]{:S(2)}) copy-start(bf16[1,2,4096]{2,1,0:T(2,128)(2,1)} %param.8) | copy-start | bytes 49156
  0.7 28.1 %copy-start.8 = (f32[2,4096]{1,0:T(2,128)S(1)}, f32[2,4096]{1,0:T(2,128)}, u32[]{:S(2)}) copy-start(f32[2,4096]{1,0:T(2,128)} %param.14) | copy-start | bytes 98308
  0.7 28.1 %copy-start.7 = (bf16[1,2,4096]{2,1,0:T(2,128)(2,1)S(1)}, bf16[1,2,4096]{2,1,0:T(2,128)(2,1)}, u32[]{:S(2)}) copy-start(bf16[1,2,4096]{2,1,0:T(2,128)(2,1)} %param.11) | copy-start | bytes 49156
  2.7 28.0 %all-to-all-start = ((bf16[32,2,4096]{2,1,0:T(2,128)(2,1)}), bf16[32,2,4096]{2,1,0:T(2,128)(2,1)S(1)}, u32[]{:S(2)}, u32[]{:S(2)}) async-start(bf16[32,2,4096]{2,1,0:T(2,128)(2,1)} %broadcast_in_dim.44), calls=%async_computation | async-start | bytes 1048576 | tf_op jit(solution)/shard_map/all_to_all | solution.py:24
  17.0 1.9 %copy-start.1 = (bf16[1,4096,384]{2,1,0:T(8,128)(2,1)S(1)}, bf16[1,4096,384]{2,1,0:T(8,128)(2,1)}, u32[]{:S(2)}) copy-start(bf16[1,4096,384]{2,1,0:T(8,128)(2,1)} %param.13) | copy-start | bytes 9437188
  21.7 9.9 %collective-permute-start = (bf16[32,16,512]{2,1,0:T(8,128)(2,1)}, bf16[32,16,512]{2,1,0:T(8,128)(2,1)}, u32[]{:S(2)}, u32[]{:S(2)}) collective-permute-start(bf16[32,16,512]{2,1,0:T(8,128)(2,1)} %get-tuple-element.18), channel_id=1, source_target_pairs={{0,3},{3,0},{1,4},{4,1},{2,5},{5,2},{6,9},{9,6},{7,10},{10,7},{8,1... | collective-permute-start | bytes 1572872 | tf_op jit(solution)/shard_map/ppermute | solution.py:360
  23.6 38.1 %collective-permute-start.2 = (bf16[2,4096]{1,0:T(2,128)(2,1)S(1)}, bf16[2,4096]{1,0:T(2,128)(2,1)S(1)}, u32[]{:S(2)}, u32[]{:S(2)}) collective-permute-start(bf16[2,4096]{1,0:T(2,128)(2,1)S(1)} %broadcast_select_fusion.3), channel_id=1, source_target_pairs={{0,192},{192,0},{384,576},{576,384},{1,193},{193,1},{385,577},{577... | collective-permute-start | bytes 49160 | tf_op jit(solution)/shard_map/ppermute | solution.py:347
  30.7 0.8 copy-start.4
  31.5 14.6 %copy-start.2 = (bf16[1,4096,384]{2,1,0:T(8,128)(2,1)S(1)}, bf16[1,4096,384]{2,1,0:T(8,128)(2,1)}, u32[]{:S(2)}) copy-start(bf16[1,4096,384]{2,1,0:T(8,128)(2,1)} %param.13) | copy-start | bytes 9437188
  33.8 26.0 %all-to-all-start.1 = ((bf16[32,16,512]{2,1,0:T(8,128)(2,1)}), bf16[32,16,512]{2,1,0:T(8,128)(2,1)}, u32[]{:S(2)}, u32[]{:S(2)}) async-start(bf16[32,16,512]{2,1,0:T(8,128)(2,1)} %shard_map.105), calls=%async_computation.1 | async-start | bytes 1048576 | tf_op jit(solution)/shard_map/all_to_all | solution.py:24
  44.1 4.5 %collective-permute-start.1 = (bf16[64,4096]{1,0:T(8,128)(2,1)}, bf16[64,4096]{1,0:T(8,128)(2,1)S(1)}, u32[]{:S(2)}, u32[]{:S(2)}) collective-permute-start(bf16[64,4096]{1,0:T(8,128)(2,1)} %reshape.157.rows_ref), channel_id=1, source_target_pairs={{0,3},{3,0},{1,4},{4,1},{2,5},{5,2},{6,9},{9,6},{7,10},{10,7},{8,1... | collective-permute-start | bytes 1572872 | tf_op jit(solution)/shard_map/ppermute | solution.py:366
  46.1 1.0 %copy-start.3 = (bf16[64,4096]{1,0:T(8,128)(2,1)S(1)}, bf16[64,4096]{1,0:T(8,128)(2,1)}, u32[]{:S(2)}) copy-start(bf16[64,4096]{1,0:T(8,128)(2,1)} %reshape.157.rows_ref) | copy-start | bytes 1572868
  61.8 12.1 %all-to-all-start.2 = ((f32[3,136,128]{2,1,0:T(8,128)}), f32[3,136,128]{2,1,0:T(8,128)S(1)}, u32[]{:S(2)}, u32[]{:S(2)}) async-start(f32[3,136,128]{2,1,0:T(8,128)} %get-tuple-element.24), calls=%async_computation.2 | async-start | bytes 417792 | tf_op jit(solution)/shard_map/all_to_all | solution.py:24
  74.9 17.6 %all-to-all-start.3 = ((bf16[6,128,128]{2,1,0:T(8,128)(2,1)}), bf16[6,128,128]{2,1,0:T(8,128)(2,1)S(1)}, u32[]{:S(2)}, u32[]{:S(2)}) async-start(bf16[6,128,128]{2,1,0:T(8,128)(2,1)} %get-tuple-element.27), calls=%async_computation.3 | async-start | bytes 393216 | tf_op jit(solution)/shard_map/all_to_all | solution.py:24
  79.9 12.5 %collective-permute-start.3 = (bf16[16,512]{1,0:T(8,128)(2,1)S(1)}, bf16[16,512]{1,0:T(8,128)(2,1)S(1)}, u32[]{:S(2)}, u32[]{:S(2)}) collective-permute-start(bf16[16,512]{1,0:T(8,128)(2,1)S(1)} %shard_map.111), channel_id=1, source_target_pairs={{0,576},{576,0},{192,384},{384,192},{1,577},{577,1},{193,385},{385... | collective-permute-start | bytes 49160 | tf_op jit(solution)/shard_map/ppermute | solution.py:411

commit v7 on v6

--- a/solution.py
+++ b/solution.py
@@ -361,6 +361,7 @@
     chip_terms = add_call(own_terms, arriving, zero_after(near[0, :, :128]))
     near, chip_terms = lax.optimization_barrier((near, chip_terms))
     term_blocks = exchange(chip_terms, PLANE)
+    term_blocks = pltpu.with_memory_space_constraint(term_blocks, pltpu.VMEM)
 
     near = near.reshape(half_tokens, features)
     far = lax.ppermute(near, CORE, cores)

time: 94.6 us -> 94.6 us (level)
  no operation moved by 1% of the time
where the time goes in v7:
time: 94.6 us; the launch traced here: 93.8 us
  starting transfers between devices  51.7 us (55%)
  waiting for transfers between devices  18.5 us (20%)
  Pallas kernels  12.4 us (13%)
  local copies, waits for them, and re-layouts  7.3 us (8%)
  other arithmetic  1.73 us (2%)
  matrix products  1.25 us (1%)
  between operations  0.96 us (1%)
    all_to_all x4, starting transfers between devices, exchange(): return lax.all_to_all(blocks, axis, 0, 0, tiled=True)  32.5 us
    all_to_all x4, waiting for transfers between devices, exchange(): return lax.all_to_all(blocks, axis, 0, 0, tiled=True)  16.3 us
    ppermute x1, starting transfers between devices, per_device(): late = lax.ppermute(late, SECTION, [(0, 3), (3, 0), (1, 2), (2, 1)])  10.3 us
    ppermute x1, starting transfers between devices, per_device(): early = lax.ppermute(early, SECTION, [(0, 1), (1, 0), (2, 3), (3, 2)])  5.06 us
    unnamed x20, local copies, waits for them, and re-layouts  3.76 us
    pallas_call x2, Pallas kernels, rows_call(): pl.pallas_call(kernel, grid=(STEPS,), in_specs=specs, out_specs=out_specs...  3.61 us
    pallas_call x1, Pallas kernels, terms_call(): pl.pallas_call(terms_kernel, grid=(features // 1024,), in_specs=[pl.Block...  2.75 us
    pallas_call x1, Pallas kernels, add_call(): pl.pallas_call(add_kernel, grid=(2,), in_specs=[block, block, pl.BlockSpe...  2.3 us
  transfers between devices with their start and end apart: 8, of which 4 were waited for; matrix products, arithmetic and copies ran while one was open for 4% of the time, Pallas kernels for 11%

profile of v7, /device:TPU:8, one launch (start us, length us, event | category | flops | bytes accessed | tf_op | source)
XLA Modules:
  0.0 93.8 jit_solution(18076688168910997553)
XLA Ops:
  0.6 0.0 copy-start
  0.6 0.0 copy-start.6
  0.7 0.0 copy-start.5
  0.7 0.0 copy-start.8
  0.7 0.0 copy-start.7
  0.7 0.8 broadcast_select_fusion.4
  1.5 1.3 %broadcast_in_dim.44 = bf16[32,2,4096]{2,1,0:T(2,128)(2,1)} broadcast(bf16[2,4096]{1,0:T(2,128)(2,1)S(1)} %broadcast_select_fusion.4), dimensions={1,2} | broadcast | bytes 540672 | tf_op jit(solution)/shard_map/broadcast_in_dim | solution.py:28
  2.7 13.0 %all-to-all-start = ((bf16[32,2,4096]{2,1,0:T(2,128)(2,1)}), bf16[32,2,4096]{2,1,0:T(2,128)(2,1)S(1)}, u32[]{:S(2)}, u32[]{:S(2)}) async-start(bf16[32,2,4096]{2,1,0:T(2,128)(2,1)} %broadcast_in_dim.44), calls=%async_computation | async-start | bytes 1048576 | tf_op jit(solution)/shard_map/all_to_all | solution.py:24
  15.8 1.2 %convolution_convert_fusion.rows_ref = bf16[128,384]{1,0:T(8,128)(2,1)S(1)} fusion(bf16[1,128,384]{2,1,0:T(8,128)(2,1)} %param.12, bf16[1,128,384]{2,1,0:T(8,128)(2,1)} %param.9, pred[]{:T(512)S(6)} %eq.35, s32[128]{0:T(128)S(1)} %fusion.18), kind=kOutput, calls=%fused_computation | convolution fusion | flops 13778944 | bytes 295425 | tf_op jit(solution)/shard_map/dot_general | solution.py:33
  17.0 0.0 copy-start.1
  17.0 1.9 %copy-done.1 = bf16[1,4096,384]{2,1,0:T(8,128)(2,1)S(1)} copy-done((bf16[1,4096,384]{2,1,0:T(8,128)(2,1)S(1)}, bf16[1,4096,384]{2,1,0:T(8,128)(2,1)}, u32[]{:S(2)}) %copy-start.1) | copy-done | bytes 3145752
  18.9 2.7 %shard_map.103 = (f32[32,16,512]{2,1,0:T(8,128)}, bf16[32,16,512]{2,1,0:T(8,128)(2,1)}) custom-call(bf16[128,384]{1,0:T(8,128)(2,1)S(1)} %convolution_convert_fusion.rows_ref, bf16[4096,384]{1,0:T(8,128)(2,1)S(1)} %bitcast.39), custom_call_target="tpu_custom_call" | custom-call | tf_op jit(solution)/shard_map/pallas_call | solution.py:159
  21.7 1.9 %collective-permute-start = (bf16[32,16,512]{2,1,0:T(8,128)(2,1)}, bf16[32,16,512]{2,1,0:T(8,128)(2,1)}, u32[]{:S(2)}, u32[]{:S(2)}) collective-permute-start(bf16[32,16,512]{2,1,0:T(8,128)(2,1)} %get-tuple-element.18), channel_id=1, source_target_pairs={{0,3},{3,0},{1,4},{4,1},{2,5},{5,2},{6,9},{9,6},{7,10},{10,7},{8,1... | collective-permute-start | bytes 1572872 | tf_op jit(solution)/shard_map/ppermute | solution.py:360
  23.6 0.0 copy-done.6
  23.6 0.0 copy-done.5
  23.6 5.1 %collective-permute-start.2 = (bf16[2,4096]{1,0:T(2,128)(2,1)S(1)}, bf16[2,4096]{1,0:T(2,128)(2,1)S(1)}, u32[]{:S(2)}, u32[]{:S(2)}) collective-permute-start(bf16[2,4096]{1,0:T(2,128)(2,1)S(1)} %broadcast_select_fusion.3), channel_id=1, source_target_pairs={{0,192},{192,0},{384,576},{576,384},{1,193},{193,1},{385,577},{577... | collective-permute-start | bytes 49160 | tf_op jit(solution)/shard_map/ppermute | solution.py:347
  28.7 0.0 copy-done.8
  28.8 0.0 copy-done.7
  28.8 0.1 pad_maximum_fusion
  28.9 1.9 %all-to-all-done = bf16[32,2,4096]{2,1,0:T(2,128)(2,1)S(1)} async-done(((bf16[32,2,4096]{2,1,0:T(2,128)(2,1)}), bf16[32,2,4096]{2,1,0:T(2,128)(2,1)S(1)}, u32[]{:S(2)}, u32[]{:S(2)}) %all-to-all-start) | async-done | bytes 524320 | tf_op jit(solution)/shard_map/all_to_all | solution.py:24
  30.7 0.8 copy-done.4
  31.5 0.0 collective-permute-done.arriving_ref
  31.5 2.3 %shard_map.105 = bf16[32,16,512]{2,1,0:T(8,128)(2,1)} custom-call(f32[32,16,512]{2,1,0:T(8,128)} %get-tuple-element.17.own_ref, bf16[32,16,512]{2,1,0:T(8,128)(2,1)} %collective-permute-done.arriving_ref, f32[8,128]{1,0:T(8,128)S(1)} %shard_map.104.zero_ref), custom_call_target="tpu_custom_call" | custom-call | tf_op jit(solution)/shard_map/pallas_call | solution.py:198
  33.8 8.0 %all-to-all-start.1 = ((bf16[32,16,512]{2,1,0:T(8,128)(2,1)}), bf16[32,16,512]{2,1,0:T(8,128)(2,1)}, u32[]{:S(2)}, u32[]{:S(2)}) async-start(bf16[32,16,512]{2,1,0:T(8,128)(2,1)} %shard_map.105), calls=%async_computation.1 | async-start | bytes 1048576 | tf_op jit(solution)/shard_map/all_to_all | solution.py:24
  41.8 0.0 copy-done
  42.0 0.1 pad.2.clone
  42.1 2.0 %reshape.157.rows_ref = bf16[64,4096]{1,0:T(8,128)(2,1)} reshape(bf16[32,2,4096]{2,1,0:T(2,128)(2,1)} %copy-done.4) | data formatting | bytes 1048576 | tf_op jit(solution)/shard_map/reshape | solution.py:366
  44.1 1.9 %collective-permute-start.1 = (bf16[64,4096]{1,0:T(8,128)(2,1)}, bf16[64,4096]{1,0:T(8,128)(2,1)S(1)}, u32[]{:S(2)}, u32[]{:S(2)}) collective-permute-start(bf16[64,4096]{1,0:T(8,128)(2,1)} %reshape.157.rows_ref), channel_id=1, source_target_pairs={{0,3},{3,0},{1,4},{4,1},{2,5},{5,2},{6,9},{9,6},{7,10},{10,7},{8,1... | collective-permute-start | bytes 1572872 | tf_op jit(solution)/shard_map/ppermute | solution.py:367
  46.0 0.1 maximum_maximum_fusion.vectors_ref
  46.1 0.0 copy-done.2
  46.2 1.0 %copy-done.3 = bf16[64,4096]{1,0:T(8,128)(2,1)S(1)} copy-done((bf16[64,4096]{1,0:T(8,128)(2,1)S(1)}, bf16[64,4096]{1,0:T(8,128)(2,1)}, u32[]{:S(2)}) %copy-start.3) | copy-done | bytes 524312
  47.2 1.4 %shard_map.107.near_ref = f32[136,384]{1,0:T(8,128)S(1)} custom-call(bf16[64,4096]{1,0:T(8,128)(2,1)S(1)} %copy-done.3, f32[8,4096]{1,0:T(8,128)S(1)} %maximum_maximum_fusion.vectors_ref, bf16[4096,384]{1,0:T(8,128)(2,1)S(1)} %bitcast.40), custom_call_target="tpu_custom_call" | custom-call | tf_op jit(solution)/shard_map/pallas_call | solution.py:111
  48.6 0.0 collective-permute-done.1.rows_ref
  48.6 2.2 %shard_map.108.payload_in = f32[3,136,128]{2,1,0:T(8,128)} custom-call(bf16[64,4096]{1,0:T(8,128)(2,1)S(1)} %collective-permute-done.1.rows_ref, f32[8,4096]{1,0:T(8,128)S(1)} %maximum_maximum_fusion.vectors_ref, bf16[4096,384]{1,0:T(8,128)(2,1)S(1)} %bitcast.41, f32[136,384]{1,0:T(8,128)S(1)} %shard_map.107.near_ref), custom_call_target="tpu_custom_call" | custom-call | tf_op jit(solution)/shard_map/pallas_call | solution.py:111
  50.8 9.1 %all-to-all-done.1.anything_ref.blocks = bf16[32,16,512]{2,1,0:T(8,128)(2,1)} async-done(((bf16[32,16,512]{2,1,0:T(8,128)(2,1)}), bf16[32,16,512]{2,1,0:T(8,128)(2,1)}, u32[]{:S(2)}, u32[]{:S(2)}) %all-to-all-start.1) | async-done | bytes 524320 | tf_op jit(solution)/shard_map/all_to_all | solution.py:24
  59.9 1.9 %shard_map.109 = (f32[16,512]{1,0:T(8,128)S(1)}, f32[3,136,128]{2,1,0:T(8,128)}) custom-call(bf16[32,16,512]{2,1,0:T(8,128)(2,1)} %all-to-all-done.1.anything_ref.blocks, bf16[3,16,512]{2,1,0:T(8,128)(2,1)S(1)} %reshape.156.lines_ref, f32[16,512]{1,0:T(8,128)S(1)} %bitcast.42, f32[8,128]{1,0:T(8,128)S(1)} %shard_map.106.zero_ref, ...), custom_call_target="tpu_custom_call", output_to_operand_aliasing={{1}: (4, {})} | custom-call | flops 1048576 | bytes 1048576 | tf_op jit(solution)/shard_map/pallas_call | solution.py:238
  61.8 0.0 collective-permute-done.2
  61.8 6.7 %all-to-all-start.2 = ((f32[3,136,128]{2,1,0:T(8,128)}), f32[3,136,128]{2,1,0:T(8,128)S(1)}, u32[]{:S(2)}, u32[]{:S(2)}) async-start(f32[3,136,128]{2,1,0:T(8,128)} %get-tuple-element.24), calls=%async_computation.2 | async-start | bytes 417792 | tf_op jit(solution)/shard_map/all_to_all | solution.py:24
  68.4 0.1 fusion.13.order_ref
  68.5 5.3 %all-to-all-done.2.received = f32[3,136,128]{2,1,0:T(8,128)S(1)} async-done(((f32[3,136,128]{2,1,0:T(8,128)}), f32[3,136,128]{2,1,0:T(8,128)S(1)}, u32[]{:S(2)}, u32[]{:S(2)}) %all-to-all-start.2) | async-done | bytes 208928 | tf_op jit(solution)/shard_map/all_to_all | solution.py:24
  73.8 1.1 %shard_map.110 = (bf16[6,128,128]{2,1,0:T(8,128)(2,1)}, f32[8,128]{1,0:T(8,128)S(1)}) custom-call(s32[1]{0:T(128)} %bitcast.even_ref, f32[3,136,128]{2,1,0:T(8,128)S(1)} %all-to-all-done.2.received, bf16[128,128]{1,0:T(8,128)(2,1)S(1)} %fusion.13.order_ref), custom_call_target="tpu_custom_call" | custom-call | tf_op jit(solution)/shard_map/pallas_call | solution.py:319
  74.9 4.9 %all-to-all-start.3 = ((bf16[6,128,128]{2,1,0:T(8,128)(2,1)}), bf16[6,128,128]{2,1,0:T(8,128)(2,1)S(1)}, u32[]{:S(2)}, u32[]{:S(2)}) async-start(bf16[6,128,128]{2,1,0:T(8,128)(2,1)} %get-tuple-element.27), calls=%async_computation.3 | async-start | bytes 393216 | tf_op jit(solution)/shard_map/all_to_all | solution.py:24
  79.8 0.1 shard_map.111
  79.9 10.3 %collective-permute-start.3 = (bf16[16,512]{1,0:T(8,128)(2,1)S(1)}, bf16[16,512]{1,0:T(8,128)(2,1)S(1)}, u32[]{:S(2)}, u32[]{:S(2)}) collective-permute-start(bf16[16,512]{1,0:T(8,128)(2,1)S(1)} %shard_map.111), channel_id=1, source_target_pairs={{0,576},{576,0},{192,384},{384,192},{1,577},{577,1},{193,385},{385... | collective-permute-start | bytes 49160 | tf_op jit(solution)/shard_map/ppermute | solution.py:412
  90.2 2.3 %collective-permute-done.3 = bf16[16,512]{1,0:T(8,128)(2,1)S(1)} collective-permute-done((bf16[16,512]{1,0:T(8,128)(2,1)S(1)}, bf16[16,512]{1,0:T(8,128)(2,1)S(1)}, u32[]{:S(2)}, u32[]{:S(2)}) %collective-permute-start.3) | collective-permute-done | bytes 16416 | tf_op jit(solution)/shard_map/ppermute | solution.py:412
  92.5 0.0 all-to-all-done.3.refs_0_.refs_1_.refs_2_
  92.5 0.7 shard_map.112
  93.2 0.6 fusion.16
  (21 shorter events, 0.3 us)
Async XLA Ops:
  0.6 41.2 %copy-start = (f32[2,4096]{1,0:T(2,128)S(1)}, f32[2,4096]{1,0:T(2,128)}, u32[]{:S(2)}) copy-start(f32[2,4096]{1,0:T(2,128)} %param.15) | copy-start | bytes 98308
  0.6 22.9 %copy-start.6 = (bf16[1,2,4096]{2,1,0:T(2,128)(2,1)S(1)}, bf16[1,2,4096]{2,1,0:T(2,128)(2,1)}, u32[]{:S(2)}) copy-start(bf16[1,2,4096]{2,1,0:T(2,128)(2,1)} %param.10) | copy-start | bytes 49156
  0.7 22.9 %copy-start.5 = (bf16[1,2,4096]{2,1,0:T(2,128)(2,1)S(1)}, bf16[1,2,4096]{2,1,0:T(2,128)(2,1)}, u32[]{:S(2)}) copy-start(bf16[1,2,4096]{2,1,0:T(2,128)(2,1)} %param.8) | copy-start | bytes 49156
  0.7 28.1 %copy-start.8 = (f32[2,4096]{1,0:T(2,128)S(1)}, f32[2,4096]{1,0:T(2,128)}, u32[]{:S(2)}) copy-start(f32[2,4096]{1,0:T(2,128)} %param.14) | copy-start | bytes 98308
  0.7 28.1 %copy-start.7 = (bf16[1,2,4096]{2,1,0:T(2,128)(2,1)S(1)}, bf16[1,2,4096]{2,1,0:T(2,128)(2,1)}, u32[]{:S(2)}) copy-start(bf16[1,2,4096]{2,1,0:T(2,128)(2,1)} %param.11) | copy-start | bytes 49156
  2.7 28.0 %all-to-all-start = ((bf16[32,2,4096]{2,1,0:T(2,128)(2,1)}), bf16[32,2,4096]{2,1,0:T(2,128)(2,1)S(1)}, u32[]{:S(2)}, u32[]{:S(2)}) async-start(bf16[32,2,4096]{2,1,0:T(2,128)(2,1)} %broadcast_in_dim.44), calls=%async_computation | async-start | bytes 1048576 | tf_op jit(solution)/shard_map/all_to_all | solution.py:24
  17.0 1.9 %copy-start.1 = (bf16[1,4096,384]{2,1,0:T(8,128)(2,1)S(1)}, bf16[1,4096,384]{2,1,0:T(8,128)(2,1)}, u32[]{:S(2)}) copy-start(bf16[1,4096,384]{2,1,0:T(8,128)(2,1)} %param.13) | copy-start | bytes 9437188
  21.7 9.9 %collective-permute-start = (bf16[32,16,512]{2,1,0:T(8,128)(2,1)}, bf16[32,16,512]{2,1,0:T(8,128)(2,1)}, u32[]{:S(2)}, u32[]{:S(2)}) collective-permute-start(bf16[32,16,512]{2,1,0:T(8,128)(2,1)} %get-tuple-element.18), channel_id=1, source_target_pairs={{0,3},{3,0},{1,4},{4,1},{2,5},{5,2},{6,9},{9,6},{7,10},{10,7},{8,1... | collective-permute-start | bytes 1572872 | tf_op jit(solution)/shard_map/ppermute | solution.py:360
  23.6 38.1 %collective-permute-start.2 = (bf16[2,4096]{1,0:T(2,128)(2,1)S(1)}, bf16[2,4096]{1,0:T(2,128)(2,1)S(1)}, u32[]{:S(2)}, u32[]{:S(2)}) collective-permute-start(bf16[2,4096]{1,0:T(2,128)(2,1)S(1)} %broadcast_select_fusion.3), channel_id=1, source_target_pairs={{0,192},{192,0},{384,576},{576,384},{1,193},{193,1},{385,577},{577... | collective-permute-start | bytes 49160 | tf_op jit(solution)/shard_map/ppermute | solution.py:347
  30.7 0.8 copy-start.4
  31.5 14.6 %copy-start.2 = (bf16[1,4096,384]{2,1,0:T(8,128)(2,1)S(1)}, bf16[1,4096,384]{2,1,0:T(8,128)(2,1)}, u32[]{:S(2)}) copy-start(bf16[1,4096,384]{2,1,0:T(8,128)(2,1)} %param.13) | copy-start | bytes 9437188
  33.8 26.0 %all-to-all-start.1 = ((bf16[32,16,512]{2,1,0:T(8,128)(2,1)}), bf16[32,16,512]{2,1,0:T(8,128)(2,1)}, u32[]{:S(2)}, u32[]{:S(2)}) async-start(bf16[32,16,512]{2,1,0:T(8,128)(2,1)} %shard_map.105), calls=%async_computation.1 | async-start | bytes 1048576 | tf_op jit(solution)/shard_map/all_to_all | solution.py:24
  44.1 4.5 %collective-permute-start.1 = (bf16[64,4096]{1,0:T(8,128)(2,1)}, bf16[64,4096]{1,0:T(8,128)(2,1)S(1)}, u32[]{:S(2)}, u32[]{:S(2)}) collective-permute-start(bf16[64,4096]{1,0:T(8,128)(2,1)} %reshape.157.rows_ref), channel_id=1, source_target_pairs={{0,3},{3,0},{1,4},{4,1},{2,5},{5,2},{6,9},{9,6},{7,10},{10,7},{8,1... | collective-permute-start | bytes 1572872 | tf_op jit(solution)/shard_map/ppermute | solution.py:367
  46.1 1.0 %copy-start.3 = (bf16[64,4096]{1,0:T(8,128)(2,1)S(1)}, bf16[64,4096]{1,0:T(8,128)(2,1)}, u32[]{:S(2)}) copy-start(bf16[64,4096]{1,0:T(8,128)(2,1)} %reshape.157.rows_ref) | copy-start | bytes 1572868
  61.8 12.1 %all-to-all-start.2 = ((f32[3,136,128]{2,1,0:T(8,128)}), f32[3,136,128]{2,1,0:T(8,128)S(1)}, u32[]{:S(2)}, u32[]{:S(2)}) async-start(f32[3,136,128]{2,1,0:T(8,128)} %get-tuple-element.24), calls=%async_computation.2 | async-start | bytes 417792 | tf_op jit(solution)/shard_map/all_to_all | solution.py:24
  74.9 17.6 %all-to-all-start.3 = ((bf16[6,128,128]{2,1,0:T(8,128)(2,1)}), bf16[6,128,128]{2,1,0:T(8,128)(2,1)S(1)}, u32[]{:S(2)}, u32[]{:S(2)}) async-start(bf16[6,128,128]{2,1,0:T(8,128)(2,1)} %get-tuple-element.27), calls=%async_computation.3 | async-start | bytes 393216 | tf_op jit(solution)/shard_map/all_to_all | solution.py:24
  79.9 12.5 %collective-permute-start.3 = (bf16[16,512]{1,0:T(8,128)(2,1)S(1)}, bf16[16,512]{1,0:T(8,128)(2,1)S(1)}, u32[]{:S(2)}, u32[]{:S(2)}) collective-permute-start(bf16[16,512]{1,0:T(8,128)(2,1)S(1)} %shard_map.111), channel_id=1, source_target_pairs={{0,576},{576,0},{192,384},{384,192},{1,577},{577,1},{193,385},{385... | collective-permute-start | bytes 49160 | tf_op jit(solution)/shard_map/ppermute | solution.py:412
